TPU v7x, 256 devices: a whole 4x4x8 slice. The times are simulated.
256 devices in a mesh: emb: 64 (over z_hi, x, y), rep: 4 (over z_lo, core).
Axes of the slice: x: 4, y: 4, z: 8 (z_hi: 4, z_lo: 2; z = z_hi * 2 + z_lo), core: 2. Of those that a mesh axis runs over, the one named last changes fastest.
Arguments:
- feature_ids: int32 [8192, 4, 128, 2], P(None, 'rep', 'emb'), may hold values from 0 to 511
- bag_lengths: int32 [8192, 4, 128], P(None, 'rep', 'emb'), may hold values from 1 to 2
- click_labels: int32 [8192, 4], P('emb', 'rep'), may hold values 0 or 1
- tables: bfloat16 [128, 512, 192], P('emb'), may hold values from -4 to 4
- projection: bfloat16 [128, 16], replicated, may hold values from -0.5 to 0.5
- compress: bfloat16 [32, 128], replicated, may hold values from -0.5 to 0.5
- w_in: bfloat16 [2048, 256], replicated, may hold values from -0.125 to 0.125
- w_out: bfloat16 [256, 768], replicated, may hold values from -0.375 to 0.375
- w_head: bfloat16 [6912], replicated, may hold values from -0.078125 to 0.078125
Outputs:
- loss: float32 [], replicated
- grad_projection: float32 [128, 16], replicated
- grad_compress: float32 [32, 128], replicated
- grad_w_in: float32 [2048, 256], replicated
- grad_w_out: float32 [256, 768], replicated
- grad_w_head: float32 [6912], replicated
- grad_tables: float32 [128, 512, 192], P('emb')
All inputs are finite; a program needn't handle non-finite values. No bound on the sum of `click_labels` on one device may be relied on, other than what follows from the above.
Results may differ from a plain program's by a relative error of at most 0.0065.
Values may be sent and summed in bfloat16 or wider, within the bound.
A program may use at most 128 MiB of HBM per device.

v0:
```python
import math

import jax
import jax.numpy as jnp
from jax import lax
from jax.sharding import PartitionSpec as P

EPS = 1e-05


def einmix(form, left, right):
    return jnp.einsum(form, left, right, preferred_element_type=jnp.float32)


def per_device(
    feature_ids, bag_lengths, click_labels, tables, projection, compress, w_in, w_out, w_head
):
    n_emb = lax.axis_size("emb")
    n_rep = lax.axis_size("rep")
    f_dev, rows, width = tables.shape
    b_rep = feature_ids.shape[0]
    b_dev = b_rep // n_emb
    bag_size = feature_ids.shape[3]
    n_rank = projection.shape[1]
    n_feat = projection.shape[0]
    n_lin = compress.shape[0]
    ids_now = feature_ids[:, 0]
    lens_now = bag_lengths[:, 0]
    flat_tables = tables.reshape(f_dev * rows, width)
    offsets = (jnp.arange(f_dev, dtype=jnp.int32) * rows)[None, :]
    pooled_sum = jnp.zeros((b_rep, f_dev, width), jnp.float32)
    for slot in range(bag_size):
        picked = jnp.take(flat_tables, ids_now[:, :, slot] + offsets, axis=0)
        pooled_sum = pooled_sum + jnp.where(
            (lens_now > slot)[..., None], picked.astype(jnp.float32), 0.0
        )
    pooled = pooled_sum.astype(jnp.bfloat16).reshape(n_emb, b_dev, f_dev, width)
    both_weights = jnp.concatenate([projection, compress.T], 1)
    embedded_part = lax.all_to_all(pooled, "emb", split_axis=0, concat_axis=2, tiled=True)[0]
    mixed = einmix("bfd,fc->bdc", embedded_part, both_weights)
    compact_part = mixed[:, :, :n_rank].astype(jnp.bfloat16)
    linear_part = mixed[:, :, n_rank:]
    interact_part = einmix("bfd,bdk->bfk", embedded_part, compact_part)
    flat = interact_part.reshape(b_dev, -1)
    center = jnp.mean(flat, 1, keepdims=True)
    shifted = flat - center
    rstd = lax.rsqrt(jnp.mean(shifted * shifted, 1, keepdims=True) + EPS)
    normed = shifted * rstd
    normed_bf = normed.astype(jnp.bfloat16)
    pre_act = jnp.dot(normed_bf, w_in, preferred_element_type=jnp.float32)
    hidden = jax.nn.silu(pre_act).astype(jnp.bfloat16)
    factor_out = jnp.dot(hidden, w_out, preferred_element_type=jnp.float32)
    linear_out = jnp.transpose(linear_part, (0, 2, 1))
    joined = jnp.concatenate([factor_out, linear_out.reshape(b_dev, -1)], 1)
    head = w_head.astype(jnp.float32)
    logits = jnp.sum(joined * head[None, :], 1)
    target = click_labels[:, 0].astype(jnp.float32)
    loss_terms = jax.nn.softplus(logits) - target * logits
    scale = 1.0 / math.sqrt(b_rep * n_rep)
    slope = scale * (jax.nn.sigmoid(logits) - target)
    grad_head = jnp.sum(slope[:, None] * joined, 0)
    grad_joined = slope[:, None] * head[None, :]
    n_out = w_out.shape[1]
    grad_factor = grad_joined[:, :n_out].astype(jnp.bfloat16)
    grad_linear = grad_joined[:, n_out:].reshape(linear_out.shape).astype(jnp.bfloat16)
    grad_linear_t = jnp.transpose(grad_linear, (0, 2, 1))
    grad_wout = jnp.dot(hidden.T, grad_factor, preferred_element_type=jnp.float32)
    grad_hidden = jnp.dot(grad_factor, w_out.T, preferred_element_type=jnp.float32)
    sigma = jax.nn.sigmoid(pre_act)
    grad_pre = (grad_hidden * sigma * (1.0 + pre_act * (1.0 - sigma))).astype(jnp.bfloat16)
    grad_win = jnp.dot(normed_bf.T, grad_pre, preferred_element_type=jnp.float32)
    grad_normed = jnp.dot(grad_pre, w_in.T, preferred_element_type=jnp.float32)
    grad_flat = rstd * (
        grad_normed
        - jnp.mean(grad_normed, 1, keepdims=True)
        - normed * jnp.mean(grad_normed * normed, 1, keepdims=True)
    )
    grad_interact = grad_flat.astype(jnp.bfloat16).reshape(interact_part.shape)
    grad_compact = einmix("bfd,bfk->bdk", embedded_part, grad_interact).astype(jnp.bfloat16)
    right_side = jnp.concatenate([compact_part, grad_compact, grad_linear_t], 2)
    left_side = jnp.concatenate(
        [
            grad_interact,
            jnp.broadcast_to(projection[None], (b_dev, n_feat, n_rank)),
            jnp.broadcast_to(compress.T[None], (b_dev, n_feat, n_lin)),
        ],
        2,
    )
    grad_embedded = einmix("bfc,bdc->bfd", left_side, right_side)
    weight_grads = einmix(
        "bfd,bdc->fc", embedded_part, jnp.concatenate([grad_compact, grad_linear_t], 2)
    )
    grad_proj = weight_grads[:, :n_rank]
    grad_comp = weight_grads[:, n_rank:].T
    outgoing = grad_embedded.astype(jnp.bfloat16)[None]
    returned = lax.all_to_all(outgoing, "emb", split_axis=2, concat_axis=0, tiled=True)
    columns = returned.shape[3]
    grad_rows = returned.reshape(b_rep * f_dev, columns).astype(jnp.float32)
    summed = jnp.zeros((f_dev * rows, columns), jnp.float32)
    for slot in range(bag_size):
        index = jnp.where(lens_now > slot, ids_now[:, :, slot] + offsets, f_dev * rows).reshape(-1)
        summed = summed + jax.ops.segment_sum(grad_rows, index, num_segments=f_dev * rows)
    table_grad = summed
    table_grad = lax.psum(table_grad.reshape(f_dev, rows, width), "rep")
    partials = (jnp.sum(loss_terms), grad_proj, grad_comp, grad_win, grad_wout, grad_head)
    totals = lax.psum(
        (partials[0], partials[1], partials[2], partials[3], partials[4], partials[5]),
        ("emb", "rep"),
    )
    loss = totals[0] / (b_rep * n_rep)
    return (loss, totals[1], totals[2], totals[3], totals[4], totals[5], table_grad)


def solution(mesh):
    placed = (
        P(None, "rep", "emb", None),
        P(None, "rep", "emb"),
        P("emb", "rep"),
        P("emb", None, None),
        P(),
        P(),
        P(),
        P(),
        P(),
    )
    return jax.shard_map(
        per_device,
        mesh=mesh,
        in_specs=placed,
        out_specs=(P(), P(), P(), P(), P(), P(), P("emb", None, None)),
        check_vma=False,
    )
```

profile of v0, /device:TPU:1, one launch (start us, length us, event | category | flops | bytes accessed | tf_op | source)
XLA Modules:
  0.0 1192.4 jit_solution(3345568487732023736)
XLA Ops:
  10.9 2.6 copy.173
  13.5 4.0 reshape.227
  17.5 2.6 copy.175
  20.2 4.0 reshape.231
  24.2 64.9 %gather_fusion.1 = bf16[16384,192]{1,0:T(8,128)(2,1)} fusion(bf16[1024,192]{1,0:T(8,128)(2,1)S(1)} %bitcast.91, s32[16384]{0:T(1024)S(1)} %broadcast_clamp_fusion), kind=kCustom, calls=%fused_computation.1.clone | custom fusion | bytes 12648448 | tf_op jit(solution)/shard_map/jit(_take)/gather | solution.py:33
  89.1 13.6 %reshape.234 = bf16[8192,2,192]{2,1,0:T(2,128)(2,1)} reshape(bf16[16384,192]{1,0:T(8,128)(2,1)} %gather_fusion.1) | data formatting | bytes 12582912 | tf_op jit(solution)/shard_map/jit(_take)/gather | solution.py:33
  102.8 20.8 %copy.176 = bf16[8192,2,192]{0,2,1:T(8,128)(2,1)} copy(bf16[8192,2,192]{2,1,0:T(2,128)(2,1)} %reshape.234) | data formatting | bytes 12582912 | tf_op jit(solution)/shard_map/jit(_take)/gather | solution.py:33
  123.5 64.9 %gather_fusion = bf16[16384,192]{1,0:T(8,128)(2,1)} fusion(bf16[1024,192]{1,0:T(8,128)(2,1)S(1)} %bitcast.92, s32[16384]{0:T(1024)S(1)} %broadcast_clamp_fusion.1), kind=kCustom, calls=%fused_computation.clone | custom fusion | bytes 12648448 | tf_op jit(solution)/shard_map/jit(_take)/gather | solution.py:33
  188.4 13.6 %reshape.230 = bf16[8192,2,192]{2,1,0:T(2,128)(2,1)} reshape(bf16[16384,192]{1,0:T(8,128)(2,1)} %gather_fusion) | data formatting | bytes 12582912 | tf_op jit(solution)/shard_map/jit(_take)/gather | solution.py:33
  202.1 20.7 %copy.174 = bf16[8192,2,192]{0,2,1:T(8,128)(2,1)} copy(bf16[8192,2,192]{2,1,0:T(2,128)(2,1)} %reshape.230) | data formatting | bytes 12582912 | tf_op jit(solution)/shard_map/jit(_take)/gather | solution.py:33
  222.8 11.9 copy_bitcast_fusion
  234.7 15.7 %all-to-all-start = ((bf16[64,128,2,192]{1,3,2,0:T(8,128)(2,1)}), bf16[64,128,2,192]{1,3,2,0:T(8,128)(2,1)}, u32[]{:S(2)}, u32[]{:S(2)}) async-start(bf16[64,128,2,192]{1,3,2,0:T(8,128)(2,1)} %copy_bitcast_fusion), calls=%async_computation | async-start | bytes 12582912 | tf_op jit(solution)/shard_map/all_to_all | solution.py:39
  250.4 135.9 %all-to-all-done = bf16[64,128,2,192]{1,3,2,0:T(8,128)(2,1)} async-done(((bf16[64,128,2,192]{1,3,2,0:T(8,128)(2,1)}), bf16[64,128,2,192]{1,3,2,0:T(8,128)(2,1)}, u32[]{:S(2)}, u32[]{:S(2)}) %all-to-all-start) | async-done | bytes 6291488 | tf_op jit(solution)/shard_map/all_to_all | solution.py:39
  386.3 9.7 copy.179
  396.0 9.2 copy.178
  405.2 5.1 fusion.24
  410.9 3.6 copy.183
  415.6 4.8 fusion.41
  425.3 3.6 multiply_reduce_fusion.1
  428.9 5.0 multiply_reduce_fusion
  438.7 7.2 fusion.42
  445.9 2.3 copy.188
  448.2 4.1 pad_maximum_fusion.1
  452.3 7.3 copy.195
  459.8 6.7 convert_bitcast_fusion.1
  466.5 9.7 copy.196
  476.2 13.2 %all-to-all-start.1 = ((bf16[1,128,128,192]{1,3,0,2:T(8,128)(2,1)}), bf16[1,128,128,192]{1,3,0,2:T(8,128)(2,1)}, u32[]{:S(2)}, u32[]{:S(2)}) async-start(bf16[1,128,128,192]{1,3,0,2:T(8,128)(2,1)} %copy.196), calls=%async_computation.1 | async-start | bytes 12582912 | tf_op jit(solution)/shard_map/all_to_all | solution.py:96
  493.8 2.7 copy.200
  496.4 2.8 copy.192
  499.2 5.1 gt.46
  504.4 5.2 gt.47
  509.6 5.5 squeeze.25
  515.1 5.7 squeeze.24
  520.8 2.3 add.114.clone
  523.1 5.5 add.124
  528.9 91.5 %all-to-all-done.1 = bf16[1,128,128,192]{1,3,0,2:T(8,128)(2,1)} async-done(((bf16[1,128,128,192]{1,3,0,2:T(8,128)(2,1)}), bf16[1,128,128,192]{1,3,0,2:T(8,128)(2,1)}, u32[]{:S(2)}, u32[]{:S(2)}) %all-to-all-start.1) | async-done | bytes 6291488 | tf_op jit(solution)/shard_map/all_to_all | solution.py:96
  620.4 9.0 convert_bitcast_fusion
  629.4 24.0 %copy.198 = f32[64,1,128,2,192]{4,3,2,0,1:T(2,128)} copy(f32[64,1,128,2,192]{2,4,3,0,1:T(8,128)} %convert_bitcast_fusion) | data formatting | bytes 25165824 | tf_op jit(solution)/shard_map/convert_element_type | solution.py:98
  653.4 20.5 %reshape.219 = f32[16384,192]{1,0:T(8,128)} reshape(f32[64,1,128,2,192]{4,3,2,0,1:T(2,128)} %copy.198) | data formatting | bytes 25165824 | tf_op jit(solution)/shard_map/convert_element_type | solution.py:98
  673.9 89.1 %scatter_custom_fusion.1 = f32[1024,192]{1,0:T(8,128)} fusion(s32[16384]{0:T(1024)S(1)} %bitcast.105, f32[16384,192]{1,0:T(8,128)} %reshape.219, f32[]{:T(128)} %constant.13.clone.1), kind=kCustom, calls=%fused_computation.35 | custom fusion | flops 3145728 | bytes 786944 | tf_op jit(solution)/shard_map/scatter-add | solution.py:102
  763.0 89.4 %scatter_custom_fusion = f32[1024,192]{1,0:T(8,128)} fusion(s32[16384]{0:T(1024)S(1)} %bitcast.104, f32[16384,192]{1,0:T(8,128)} %reshape.219, f32[]{:T(128)} %constant.13.clone.1), kind=kCustom, calls=%fused_computation.37 | custom fusion | flops 3145728 | bytes 786944 | tf_op jit(solution)/shard_map/scatter-add | solution.py:102
  852.4 2.7 add.127
  855.0 2.2 copy.204
  861.3 4.5 fusion.12
  866.5 87.0 %all-reduce = (f32[]{:T(128)}, f32[128,16]{0,1:T(8,128)}, f32[32,128]{1,0:T(8,128)}, f32[6912]{0:T(1024)}) all-reduce(f32[]{:T(128)} %fusion.30, f32[128,16]{0,1:T(8,128)S(1)} %slice.47, f32[32,128]{1,0:T(8,128)S(1)} %slice_bitcast_fusion.1, f32[6912]{0:T(1024)S(1)} %copy-done.16), channel_id=1, replica_groups=mesh['emb'=64,'rep'=4] {'emb','rep'}, use_global_device_ids=true, to_apply=%region_4.6 | all-reduce | flops 13057 | bytes 104456 | tf_op jit(solution)/shard_map/psum | solution.py:106
  954.2 2.2 copy.202
  956.4 223.6 %all-reduce.7.cloned.1.call-done = (f32[2048,256]{1,0:T(8,128)}, f32[256,768]{1,0:T(8,128)}) async-done(((f32[2048,256]{1,0:T(8,128)}, f32[256,768]{1,0:T(8,128)}), (f32[2048,256]{1,0:T(8,128)}, f32[256,768]{1,0:T(8,128)})) %all-reduce.7.cloned.1.call-update) | async-done | bytes 2883600 | tf_op jit(solution)/shard_map/psum | solution.py:106
  1180.0 3.1 copy.223
  (99 shorter events, 25.4 us)
Async XLA Ops:
  7.2 416.1 %copy-start = (bf16[2048,256]{1,0:T(8,128)(2,1)S(1)}, bf16[2048,256]{1,0:T(8,128)(2,1)}, u32[]{:S(2)}) copy-start(bf16[2048,256]{1,0:T(8,128)(2,1)} %param.17) | copy-start | bytes 3145732
  7.2 10.3 copy-start.22
  8.2 214.6 %copy-start.10 = (pred[8192,1,2]{0,2,1:T(4,128)(4,1)}, pred[8192,1,2]{0,2,1:T(4,128)(4,1)S(1)}, u32[]{:S(2)}) copy-start(pred[8192,1,2]{0,2,1:T(4,128)(4,1)S(1)} %get-tuple-element.60) | copy-start | bytes 49156
  8.2 214.6 %copy-start.12 = (pred[8192,1,2]{0,2,1:T(4,128)(4,1)}, pred[8192,1,2]{0,2,1:T(4,128)(4,1)S(1)}, u32[]{:S(2)}) copy-start(pred[8192,1,2]{0,2,1:T(4,128)(4,1)S(1)} %get-tuple-element.59) | copy-start | bytes 49156
  9.3 4.2 copy-start.5
  9.3 8.2 copy-start.7
  234.7 15.7 %copy-start.19 = (bf16[6912]{0:T(1024)(128)(2,1)S(1)}, bf16[6912]{0:T(1024)(128)(2,1)}, u32[]{:S(2)}) copy-start(bf16[6912]{0:T(1024)(128)(2,1)} %param.19) | copy-start | bytes 41476
  234.7 151.6 %all-to-all-start = ((bf16[64,128,2,192]{1,3,2,0:T(8,128)(2,1)}), bf16[64,128,2,192]{1,3,2,0:T(8,128)(2,1)}, u32[]{:S(2)}, u32[]{:S(2)}) async-start(bf16[64,128,2,192]{1,3,2,0:T(8,128)(2,1)} %copy_bitcast_fusion), calls=%async_computation | async-start | bytes 12582912 | tf_op jit(solution)/shard_map/all_to_all | solution.py:39
  396.0 9.2 copy-start.17
  396.0 9.2 copy-start.18
  410.4 4.1 copy-start.2
  421.0 7.9 copy-start.26
  422.9 14.3 %copy-start.20 = (f32[128]{0:T(128)}, f32[128]{0:T(128)S(1)}, u32[]{:S(2)}) copy-start(f32[128]{0:T(128)S(1)} %add_rsqrt_fusion) | copy-start | bytes 1540
  423.3 2.0 copy-start.1
  423.6 10.3 copy-start.9
  428.9 5.5 copy-start.24
  434.0 3.2 copy-start.3
  434.3 2.9 copy-start.14
  476.2 13.3 %copy-start.13 = (pred[8192,1,2]{0,2,1:T(4,128)(4,1)S(1)}, pred[8192,1,2]{0,2,1:T(4,128)(4,1)}, u32[]{:S(2)}) copy-start(pred[8192,1,2]{0,2,1:T(4,128)(4,1)} %copy-done.12) | copy-start | bytes 49156
  476.2 15.4 %copy-start.11 = (pred[8192,1,2]{0,2,1:T(4,128)(4,1)S(1)}, pred[8192,1,2]{0,2,1:T(4,128)(4,1)}, u32[]{:S(2)}) copy-start(pred[8192,1,2]{0,2,1:T(4,128)(4,1)} %copy-done.10) | copy-start | bytes 49156
  476.2 17.6 %copy-start.8 = (s32[8192,2,1]{0,2,1:T(1,128)S(1)}, s32[8192,2,1]{0,2,1:T(1,128)}, u32[]{:S(2)}) copy-start(s32[8192,2,1]{0,2,1:T(1,128)} %copy-done.7) | copy-start | bytes 196612
  476.2 144.2 %all-to-all-start.1 = ((bf16[1,128,128,192]{1,3,0,2:T(8,128)(2,1)}), bf16[1,128,128,192]{1,3,0,2:T(8,128)(2,1)}, u32[]{:S(2)}, u32[]{:S(2)}) async-start(bf16[1,128,128,192]{1,3,0,2:T(8,128)(2,1)} %copy.196), calls=%async_computation.1 | async-start | bytes 12582912 | tf_op jit(solution)/shard_map/all_to_all | solution.py:96
  489.4 7.0 copy-start.6
  489.4 464.8 %all-reduce.5.cloned.1.call-start = ((), (), s32[]{:S(2)}) async-start(), calls=%async_computation.2 | async-start | bytes 1572864 | tf_op jit(solution)/shard_map/psum | solution.py:104
  504.4 16.4 %copy-start.23 = (s32[2]{0:T(128)S(1)}, s32[2]{0:T(128)}, u32[]{:S(2)}) copy-start(s32[2]{0:T(128)} %copy-done.22) | copy-start | bytes 28
  673.9 185.5 %copy-start.15 = (bf16[128,256]{1,0:T(8,128)(2,1)S(1)}, bf16[128,256]{1,0:T(8,128)(2,1)}, u32[]{:S(2)}) copy-start(bf16[128,256]{1,0:T(8,128)(2,1)} %copy-done.14) | copy-start | bytes 196612
  673.9 185.5 %copy-start.21 = (f32[128]{0:T(128)S(1)}, f32[128]{0:T(128)}, u32[]{:S(2)}) copy-start(f32[128]{0:T(128)} %copy-done.20) | copy-start | bytes 1540
  857.2 322.7 %all-reduce.7.cloned.1.call-start = ((), (), s32[]{:S(2)}) async-start(), calls=%async_computation.3 | async-start | bytes 5767168 | tf_op jit(solution)/shard_map/psum | solution.py:106
  861.3 4.6 copy-start.25
  861.3 4.6 copy-start.27
  861.3 5.2 copy-start.16
  1180.0 3.1 copy-start.4
Sparse Core Ops, SparseCore 0:
  857.4 54.1 all-reduce.4
  917.7 262.2 all-reduce.6
where the time goes:
time: 1200 us; the launch traced here: 1190 us
  waiting for transfers between devices  451 us (38%)
  local copies, waits for them, and re-layouts  354 us (30%)
  other arithmetic  219 us (18%)
  blocking collectives  87 us (7%)
  matrix products  35 us (3%)
  starting transfers between devices  29 us (2%)
  between operations  16.8 us (1%)
    psum x1, waiting for transfers between devices, per_device(): lax.psum((partials[0], partials[1], partials[2], partials[3], partials[4]...  224 us
    gather x6, local copies, waits for them, and re-layouts, per_device(): picked = jnp.take(flat_tables, ids_now[:, :, slot] + offsets, axis=0)  199 us
    scatter-add x2, other arithmetic, per_device(): jax.ops.segment_sum(grad_rows, index, num_segments=f_dev * rows)  178 us
    all_to_all x1, waiting for transfers between devices, per_device(): lax.all_to_all(pooled, 'emb', split_axis=0, concat_axis=2, tiled=True)[0]  136 us
    all_to_all x1, waiting for transfers between devices, per_device(): lax.all_to_all(outgoing, 'emb', split_axis=2, concat_axis=0, tiled=True)  91.5 us
    psum x1, blocking collectives, per_device(): lax.psum((partials[0], partials[1], partials[2], partials[3], partials[4]...  87 us
    convert_element_type x2, local copies, waits for them, and re-layouts, per_device(): grad_rows = returned.reshape(b_rep * f_dev, columns).astype(jnp.float32)  44.5 us
    dot_general x5, matrix products, einmix(): return jnp.einsum(form, left, right, preferred_element_type=jnp.float32)  28.2 us
  transfers between devices with their start and end apart: 4, of which 3 were waited for; matrix products, arithmetic and copies ran while one was open for 4% of the time, Pallas kernels for 0%

commit v1 on v0

v1 whole, which is shorter than its diff:
```python
import functools
import math

import jax
import jax.numpy as jnp
from jax import lax
from jax.experimental import pallas as pl
from jax.experimental.pallas import tpu as pltpu
from jax.sharding import Mesh, PartitionSpec as P

EPS = 1e-05
BF = jnp.bfloat16
F32 = jnp.float32
NT = (((1,), (1,)), ((), ()))
TN = (((0,), (0,)), ((), ()))
VMEM_LIMIT = 60 * 1024 * 1024


def mm(a, b, dims=None):
    if dims is None:
        return jnp.dot(a, b, preferred_element_type=F32)
    return lax.dot_general(a, b, dims, preferred_element_type=F32)


def lookup_kernel(ids_ref, w1_ref, w2_ref, y_ref, col_ref):
    n_dest, n_f = y_ref.shape[:2]
    half = n_dest * 64
    rows = w1_ref.shape[1]
    for i in range(2 * half // 128):
        col_ref[pl.ds(i * 128, 128), :] = ids_ref[:, i * 128 : (i + 1) * 128].T
    group = 4

    def chunk(c, carry):
        base = pl.multiple_of(c * group * 64, group * 64)
        for f in range(n_f):
            parts = []
            for h, w_ref in ((0, w1_ref), (1, w2_ref)):
                both = col_ref[pl.ds(h * half + base, group * 64), 2 * f : 2 * f + 2]
                lane = lax.broadcasted_iota(jnp.int32, (group * 64, rows), 1)
                hot = jnp.where(lane == both[:, 0:1], 1.0, 0.0) + jnp.where(
                    lane == both[:, 1:2], 1.0, 0.0
                )
                parts.append(mm(hot.astype(BF), w_ref[f]))
            p1, p2 = parts
            rest = p1[:, 128:] + p2[:, 128:]
            for k, block in enumerate((p1[:, :128], p2[:, :128], rest)):
                y_ref[pl.ds(c * group, group), f, k * 64 : (k + 1) * 64, :] = block.astype(
                    BF
                ).reshape(group, 64, 128)
        return carry

    lax.fori_loop(0, n_dest // group, chunk, 0)


def scatter_kernel(ids_ref, g_ref, out_ref):
    n_src, n_f = g_ref.shape[:2]
    half = n_src * 64
    rows = out_ref.shape[1]
    group = 4
    for f in range(n_f):
        sums = [jnp.zeros((rows, 256), F32), jnp.zeros((rows, 256), F32)]
        for c in range(n_src // group):
            rest = g_ref[c * group : (c + 1) * group, f, 128:192, :].reshape(group * 64, 128)
            for h in range(2):
                base = h * half + c * group * 64
                row = lax.broadcasted_iota(jnp.int32, (rows, group * 64), 0)
                id0 = ids_ref[2 * f : 2 * f + 1, base : base + group * 64]
                id1 = ids_ref[2 * f + 1 : 2 * f + 2, base : base + group * 64]
                hot = jnp.where(row == id0, 1.0, 0.0) + jnp.where(row == id1, 1.0, 0.0)
                main = g_ref[c * group : (c + 1) * group, f, h * 64 : (h + 1) * 64, :].reshape(
                    group * 64, 128
                )
                sums[h] = sums[h] + mm(hot.astype(BF), jnp.concatenate([main, rest], 1))
        s1, s2 = sums
        out_ref[f, :, :128] = s1[:, :128] + s2[:, :128]
        tail = s1[:, 128:] + pltpu.roll(s2[:, 128:], 64, 1)
        out_ref[f, :, 128:192] = tail[:, :64]


def dense_kernel(
    scale,
    x_ref,
    wt_ref,
    win_ref,
    wout_ref,
    head_ref,
    hpair_ref,
    label_ref,
    g_ref,
    loss_ref,
    gw_ref,
    gwin_ref,
    gwout_ref,
    ghead_ref,
    ghl_ref,
    split_ref,
    xp_ref,
    mix_ref,
    inter_ref,
    nb_ref,
    ld_ref,
    slope_ref,
):
    n_f = x_ref.shape[0]
    n_b = 128
    n_k = 16
    tile = 16
    lane1 = lax.broadcasted_iota(jnp.int32, (n_k, 384), 1) < 192
    row_lane1 = lax.broadcasted_iota(jnp.int32, (1, 384), 1) < 192
    wt = wt_ref[...]

    def load_group(q, carry):
        for part in range(3):
            block = x_ref[:, pl.ds(pl.multiple_of(part * 64 + q * tile, tile), tile), :]
            split_ref[part] = block.astype(F32).reshape(n_f * tile, 128)

        def pair(j, inner):
            p = q * tile + j
            pieces = [
                split_ref[part, pl.ds(j, n_f, stride=tile), :].astype(BF) for part in (0, 2, 1)
            ]
            x3 = jnp.concatenate(pieces, 1)
            xp_ref[p] = x3
            mixed = mm(wt, x3)
            mix_ref[p] = mixed
            compact = mixed[:n_k]
            stacked = jnp.concatenate(
                [jnp.where(lane1, compact, 0.0), jnp.where(lane1, 0.0, compact)], 0
            ).astype(BF)
            inter = mm(stacked, x3, NT)
            inter_ref[pl.ds(p, n_k, stride=n_b), :] = inter[:n_k]
            inter_ref[pl.ds(64 + p, n_k, stride=n_b), :] = inter[n_k:]
            ld_ref[pl.ds(p, 1), :] = jnp.sum(mixed[n_k:] * hpair_ref[...], 0, keepdims=True)
            return inner

        lax.fori_loop(0, tile, pair, 0, unroll=2)
        return carry

    lax.fori_loop(0, 64 // tile, load_group, 0)

    total = jnp.zeros((n_b, n_f), F32)
    for k in range(n_k):
        total = total + inter_ref[k * n_b : (k + 1) * n_b, :]
    width = n_k * n_f
    center = jnp.sum(total, 1, keepdims=True) / width
    total = jnp.zeros((n_b, n_f), F32)
    for k in range(n_k):
        shifted = inter_ref[k * n_b : (k + 1) * n_b, :] - center
        total = total + shifted * shifted
    rstd = lax.rsqrt(jnp.sum(total, 1, keepdims=True) / width + EPS)
    for k in range(n_k):
        normed = (inter_ref[k * n_b : (k + 1) * n_b, :] - center) * rstd
        inter_ref[k * n_b : (k + 1) * n_b, :] = normed
        nb_ref[:, k * n_f : (k + 1) * n_f] = normed.astype(BF)
    pre_act = mm(nb_ref[...], win_ref[...])
    sigma = 1.0 / (1.0 + jnp.exp(-pre_act))
    hidden = (pre_act * sigma).astype(BF)
    factor = mm(hidden, wout_ref[...])
    head = head_ref[...]
    lin = ld_ref[...]
    lin1 = jnp.sum(jnp.where(row_lane1, lin, 0.0), 1, keepdims=True)
    lin2 = jnp.sum(jnp.where(row_lane1, 0.0, lin), 1, keepdims=True)
    logit = jnp.sum(factor * head, 1, keepdims=True) + jnp.concatenate([lin1, lin2], 0)
    target = label_ref[...]
    terms = jnp.maximum(logit, 0.0) + jnp.log1p(jnp.exp(-jnp.abs(logit))) - target * logit
    loss_ref[...] = jnp.sum(jnp.broadcast_to(terms, (n_b, 128)), 0, keepdims=True)
    slope = scale * (1.0 / (1.0 + jnp.exp(-logit)) - target)
    slope_ref[...] = jnp.broadcast_to(slope, (n_b, 128))
    ghead_ref[...] = jnp.sum(slope * factor, 0, keepdims=True)
    gfactor = (slope * head).astype(BF)
    gwout_ref[...] = mm(hidden, gfactor, TN)
    ghidden = mm(gfactor, wout_ref[...], NT)
    gpre = (ghidden * sigma * (1.0 + pre_act * (1.0 - sigma))).astype(BF)
    first = jnp.zeros((n_b, n_f), F32)
    second = jnp.zeros((n_b, n_f), F32)
    for k in range(n_k):
        rows = slice(k * n_f, (k + 1) * n_f)
        gwin_ref[rows, :] = mm(nb_ref[:, rows], gpre, TN)
        gnormed = mm(gpre, win_ref[rows, :], NT)
        first = first + gnormed
        second = second + gnormed * inter_ref[k * n_b : (k + 1) * n_b, :]
    mean1 = jnp.sum(first, 1, keepdims=True) / width
    mean2 = jnp.sum(second, 1, keepdims=True) / width
    for k in range(n_k):
        rows = slice(k * n_f, (k + 1) * n_f)
        span = slice(k * n_b, (k + 1) * n_b)
        gnormed = mm(gpre, win_ref[rows, :], NT)
        inter_ref[span, :] = rstd * (gnormed - mean1 - inter_ref[span, :] * mean2)

    gw_ref[...] = jnp.zeros_like(gw_ref)
    ghl_ref[...] = jnp.zeros_like(ghl_ref)

    def back_group(q, carry):
        def pair(j, inner):
            p = q * tile + j
            x3 = xp_ref[p]
            gi = jnp.concatenate(
                [
                    inter_ref[pl.ds(p, n_k, stride=n_b), :],
                    inter_ref[pl.ds(64 + p, n_k, stride=n_b), :],
                ],
                0,
            ).astype(BF)
            gc = mm(gi, x3)
            gc = jnp.where(lane1, gc[:n_k], gc[n_k:]).astype(BF)
            s1 = slope_ref[pl.ds(p, 1), :]
            s2 = slope_ref[pl.ds(64 + p, 1), :]
            srow = jnp.where(
                row_lane1,
                jnp.concatenate([s1, s1, s1], 1),
                jnp.concatenate([s2, s2, s2], 1),
            )
            gl = (srow * hpair_ref[...]).astype(BF)
            mixed = mix_ref[p]
            ghl_ref[...] += srow * mixed[n_k:]
            compact = mixed[:n_k]
            tail = jnp.concatenate([gc, gl], 0)
            right = jnp.concatenate(
                [
                    jnp.where(lane1, compact, 0.0).astype(BF),
                    jnp.where(lane1, 0.0, compact).astype(BF),
                    tail,
                ],
                0,
            )
            left = jnp.concatenate([gi, wt], 0)
            gp = mm(left, right, TN)
            gw_ref[...] += mm(tail, x3, NT)
            for part, at in ((0, 0), (2, 128), (1, 256)):
                split_ref[part, pl.ds(j, n_f, stride=tile), :] = gp[:, at : at + 128]
            return inner

        lax.fori_loop(0, tile, pair, 0, unroll=2)
        for part in range(3):
            g_ref[:, pl.ds(pl.multiple_of(part * 64 + q * tile, tile), tile), :] = (
                split_ref[part].reshape(n_f, tile, 128).astype(BF)
            )
        return carry

    lax.fori_loop(0, 64 // tile, back_group, 0)


def whole(n):
    return [pl.BlockSpec(memory_space=pltpu.VMEM)] * n


def lookup(ids, w1, w2, n_dest):
    n_f = w1.shape[0]
    return pl.pallas_call(
        lookup_kernel,
        out_shape=jax.ShapeDtypeStruct((n_dest, n_f, 192, 128), BF),
        in_specs=whole(3),
        out_specs=whole(1)[0],
        scratch_shapes=[pltpu.VMEM((ids.shape[1], ids.shape[0]), jnp.int32)],
        compiler_params=pltpu.CompilerParams(vmem_limit_bytes=VMEM_LIMIT),
        name="lookup",
    )(ids, w1, w2)


def scatter(ids, g, rows):
    n_f = g.shape[1]
    return pl.pallas_call(
        scatter_kernel,
        out_shape=jax.ShapeDtypeStruct((n_f, rows, 192), F32),
        in_specs=whole(2),
        out_specs=whole(1)[0],
        compiler_params=pltpu.CompilerParams(vmem_limit_bytes=VMEM_LIMIT),
        name="table_grad",
    )(ids, g)


def dense(scale, x, wt, win, wout, head, hpair, label):
    n_f = x.shape[0]
    shapes = [
        (x.shape, BF),
        ((1, 128), F32),
        ((48, n_f), F32),
        (win.shape, F32),
        (wout.shape, F32),
        (head.shape, F32),
        ((32, 384), F32),
    ]
    return pl.pallas_call(
        functools.partial(dense_kernel, scale),
        out_shape=[jax.ShapeDtypeStruct(*s) for s in shapes],
        in_specs=whole(7),
        out_specs=whole(7),
        scratch_shapes=[
            pltpu.VMEM((3, n_f * 16, 128), F32),
            pltpu.VMEM((64, n_f, 384), BF),
            pltpu.VMEM((64, 48, 384), F32),
            pltpu.VMEM((16 * 128, n_f), F32),
            pltpu.VMEM((128, 16 * n_f), BF),
            pltpu.VMEM((64, 384), F32),
            pltpu.VMEM((128, 128), F32),
        ],
        compiler_params=pltpu.CompilerParams(vmem_limit_bytes=VMEM_LIMIT),
        name="dense",
    )(x, wt, win, wout, head, hpair, label)


def table_weights(t):
    zeros = jnp.zeros(t.shape[:2] + (64,), t.dtype)
    w1 = jnp.concatenate([t, zeros], 2)
    w2 = jnp.concatenate([t[:, :, :128], zeros, t[:, :, 128:]], 2)
    return w1, w2


def order_ids(feature_ids, bag_lengths, n_zh, n_plane, rows):
    ids = feature_ids[:, 0].transpose(1, 2, 0)
    lens = bag_lengths[:, 0].T
    slots = jnp.arange(ids.shape[1], dtype=jnp.int32)[None, :, None]
    ids = jnp.where(lens[:, None, :] > slots, ids, rows)
    ids = ids.reshape(-1, n_zh, n_plane, 2, 64).transpose(1, 0, 3, 2, 4)
    return ids.reshape(n_zh, -1, n_plane * 128)


def pair_head(w_head, n_out):
    lin = w_head[n_out:].astype(F32).reshape(-1, 192)
    return jnp.concatenate([lin, lin[:, 128:], lin[:, :128]], 1)


def per_device(
    feature_ids, bag_lengths, click_labels, tables, projection, compress, w_in, w_out, w_head
):
    n_zh = lax.axis_size("zh")
    n_plane = lax.axis_size("x") * lax.axis_size("y")
    n_rep = lax.axis_size("zl") * lax.axis_size("c")
    f_dev, rows, width = tables.shape
    b_rep = feature_ids.shape[0]
    n_feat, n_rank = projection.shape
    n_lin = compress.shape[0]
    n_out = w_out.shape[1]
    total = b_rep * n_rep
    scale = 1.0 / math.sqrt(total)

    ids = order_ids(feature_ids, bag_lengths, n_zh, n_plane, rows)
    ids = lax.all_to_all(ids, "zh", split_axis=0, concat_axis=0, tiled=True)
    ids = ids.reshape(-1, n_plane * 128)
    all_tables = lax.all_gather(tables, "zh", axis=0, tiled=True)
    w1, w2 = table_weights(all_tables)
    y = lookup(ids, w1, w2, n_plane)
    x = lax.all_to_all(y, ("x", "y"), split_axis=0, concat_axis=0, tiled=True)
    x = x.reshape(n_feat, 192, 128)

    def mix_order(a):
        rest = a.shape[1:]
        a = a.reshape((n_zh, n_plane, f_dev) + rest)
        return jnp.swapaxes(a, 0, 1).reshape((n_feat,) + rest)

    wt = jnp.concatenate([mix_order(projection), mix_order(compress.T)], 1).T
    win = mix_order(w_in.reshape(n_feat, n_rank, -1)).transpose(1, 0, 2).reshape(w_in.shape)
    head = w_head[:n_out].astype(F32)[None, :]
    hpair = pair_head(w_head, n_out)
    label = click_labels.astype(F32)
    g, loss, gw, gwin, gwout, ghead, ghl = dense(
        scale, x, wt, win, w_out, head, hpair, label
    )
    back = lax.all_to_all(
        g.reshape(y.shape), ("x", "y"), split_axis=0, concat_axis=0, tiled=True
    )
    partial = scatter(ids, back, rows)
    partial = lax.psum(partial, ("zl", "c"))
    table_grad = lax.psum_scatter(partial, "zh", scatter_dimension=0, tiled=True)

    ghl = ghl[:, :192] + jnp.concatenate([ghl[:, 256:], ghl[:, 192:256]], 1)
    sums = lax.psum(
        (loss[0, 0], gw, gwin, gwout, ghead[0], ghl), ("zh", "x", "y", "zl", "c")
    )
    loss, gw, gwin, gwout, ghead, ghl = sums

    def natural(a):
        rest = a.shape[1:]
        a = a.reshape((n_plane, n_zh, f_dev) + rest)
        return jnp.swapaxes(a, 0, 1).reshape((n_feat,) + rest)

    gw = natural(gw.T)
    gwin = natural(gwin.reshape(n_rank, n_feat, -1).transpose(1, 0, 2)).reshape(w_in.shape)
    ghead = jnp.concatenate([ghead, ghl.reshape(-1)])
    return (loss / total, gw[:, :n_rank], gw[:, n_rank:].T, gwin, gwout, ghead, table_grad)


def solution(mesh):
    fine = Mesh(mesh.devices.reshape(4, 4, 4, 2, 2), ("zh", "x", "y", "zl", "c"))
    emb = ("zh", "x", "y")
    rep = ("zl", "c")
    placed = (
        P(None, rep, emb, None),
        P(None, rep, emb),
        P(emb, rep),
        P(emb, None, None),
        P(),
        P(),
        P(),
        P(),
        P(),
    )
    return jax.shard_map(
        per_device,
        mesh=fine,
        in_specs=placed,
        out_specs=(P(), P(), P(), P(), P(), P(), P(emb, None, None)),
        check_vma=False,
    )
```

time: 1200 us -> 744 us (0.62)
  local copies, waits for them, and re-layouts: 354 us -> 24.7 us
  other arithmetic: 219 us -> 4.85 us
  blocking collectives: 87 us -> 160 us
  Pallas kernels: 0 us -> 72.8 us
  matrix products: 35 us -> 0 us
  starting transfers between devices: 29 us -> 15.9 us
    gather x6 -> x0, local copies, waits for them, and re-layouts: 199 us -> none  [per_device(): picked = jnp.take(flat_tables, ids_now[:, :, slot] + offsets, axis=0)]
    scatter-add x2 -> x0, other arithmetic: 178 us -> none  [per_device(): jax.ops.segment_sum(grad_rows, index, num_segments=f_dev * rows)]
    all_to_all x2, waiting for transfers between devices: 227 us -> 101 us  [the longest x1 94.1 us: per_device(): x = lax.all_to_all(y, ('x', 'y'), split_axis=0, concat_axis=0, tiled=True)]
    reduce_scatter x0 -> x1, waiting for transfers between devices: none -> 89.6 us  [per_device(): lax.psum_scatter(partial, 'zh', scatter_dimension=0, tiled=True)]
    all_to_all x0 -> x1, blocking collectives: none -> 83 us  [per_device(): lax.all_to_all(g.reshape(y.shape), ('x', 'y'), split_axis=0, concat_axis=...]
    pallas_call x0 -> x3, Pallas kernels: none -> 72.8 us  [the longest x1 45.5 us: dense(): pl.pallas_call(functools.partial(dense_kernel, scale), out_shape=[jax.Sha...]
    convert_element_type x4 -> x2, local copies, waits for them, and re-layouts: 46.9 us -> 0.83 us  [the longest x1 0.75 us: per_device(): label = click_labels.astype(F32)]
    dot_general x11 -> x0, matrix products: 35 us -> none  [the longest x5 28.2 us: einmix(): return jnp.einsum(form, left, right, preferred_element_type=jnp.float32)]
  transfers between devices with their start and end apart: 4 -> 6, of which waited for: 3 -> 5; matrix products, arithmetic and copies ran while one was open for 4% -> 2% of each run, Pallas kernels for 0% -> 0%
where the time goes in v1:
time: 744 us; the launch traced here: 743 us
  waiting for transfers between devices  449 us (60%)
  blocking collectives  160 us (22%)
  Pallas kernels  72.8 us (10%)
  local copies, waits for them, and re-layouts  24.7 us (3%)
  starting transfers between devices  15.9 us (2%)
  between operations  15.7 us (2%)
    psum x1, waiting for transfers between devices, per_device(): lax.psum((loss[0, 0], gw, gwin, gwout, ghead[0], ghl), ('zh', 'x', 'y', '...  227 us
    all_to_all x1, waiting for transfers between devices, per_device(): x = lax.all_to_all(y, ('x', 'y'), split_axis=0, concat_axis=0, tiled=True)  94.1 us
    reduce_scatter x1, waiting for transfers between devices, per_device(): lax.psum_scatter(partial, 'zh', scatter_dimension=0, tiled=True)  89.6 us
    all_to_all x1, blocking collectives, per_device(): lax.all_to_all(g.reshape(y.shape), ('x', 'y'), split_axis=0, concat_axis=...  83 us
    psum x1, blocking collectives, per_device(): lax.psum((loss[0, 0], gw, gwin, gwout, ghead[0], ghl), ('zh', 'x', 'y', '...  77.3 us
    pallas_call x1, Pallas kernels, dense(): pl.pallas_call(functools.partial(dense_kernel, scale), out_shape=[jax.Sha...  45.5 us
    all_gather x1, waiting for transfers between devices, per_device(): all_tables = lax.all_gather(tables, 'zh', axis=0, tiled=True)  29.8 us
  transfers between devices with their start and end apart: 6, of which 5 were waited for; matrix products, arithmetic and copies ran while one was open for 2% of the time, Pallas kernels for 0%

profile of v1, /device:TPU:1, one launch (start us, length us, event | category | flops | bytes accessed | tf_op | source)
XLA Modules:
  0.0 742.9 jit_solution(1510279220157527585)
XLA Ops:
  7.2 0.7 all-gather.2.cloned.1.call-update
  7.9 1.0 compare_select_fusion
  8.9 0.3 reshape.74
  9.2 0.8 reshape.75
  10.0 9.0 %all-to-all-start = ((s32[4,4,2048]{2,1,0:T(4,128)}), s32[4,4,2048]{2,1,0:T(4,128)S(1)}, u32[]{:S(2)}, u32[]{:S(2)}) async-start(s32[4,4,2048]{2,1,0:T(4,128)} %reshape.75), calls=%async_computation | async-start | bytes 262144 | tf_op jit(solution)/shard_map/all_to_all | solution.py:338
  19.0 7.2 all-to-all-done
  26.2 0.7 reshape.76.ids_ref
  26.9 29.8 %all-gather.2.cloned.1.call-done = bf16[8,512,192]{1,2,0:T(8,128)(2,1)} async-done(((bf16[2,512,192]{1,2,0:T(8,128)(2,1)}), bf16[8,512,192]{1,2,0:T(8,128)(2,1)}) %all-gather.2.cloned.1.call-update) | async-done | bytes 1572880 | tf_op jit(solution)/shard_map/all_gather | solution.py:340
  56.7 2.7 copy.60
  59.5 0.2 slice.57
  59.7 0.2 slice.56
  59.8 1.7 concatenate.18.w1_ref
  61.5 1.9 pad_maximum_fusion.w2_ref
  63.5 14.1 %lookup.1 = bf16[16,8,192,128]{3,2,1,0:T(8,128)(2,1)} custom-call(s32[16,2048]{1,0:T(8,128)} %reshape.76.ids_ref, bf16[8,512,256]{2,1,0:T(8,128)(2,1)} %concatenate.18.w1_ref, bf16[8,512,256]{2,1,0:T(8,128)(2,1)} %pad_maximum_fusion.w2_ref), custom_call_target="tpu_custom_call" | custom-call | tf_op jit(solution)/shard_map/lookup/pallas_call | solution.py:249
  77.6 6.7 all-to-all-start.1
  84.3 0.0 reduce-scatter.2.cloned.1.call-start
  84.4 0.1 reshape.91
  84.5 0.6 reshape.90.head_ref
  85.1 0.1 copy.63
  85.2 0.1 copy.67
  85.3 0.1 copy.65
  85.5 0.1 copy.68
  85.5 0.8 copy.70.label_ref
  86.3 1.0 copy.69
  87.3 1.3 reshape.82
  88.6 0.6 maximum_bitcast_fusion.wt_ref
  89.2 0.7 pad_maximum_fusion.1.hpair_ref
  89.9 94.1 %all-to-all-done.1 = bf16[16,8,192,128]{3,2,1,0:T(8,128)(2,1)} async-done(((bf16[16,8,192,128]{3,2,1,0:T(8,128)(2,1)}), bf16[16,8,192,128]{3,2,1,0:T(8,128)(2,1)}, u32[]{:S(2)}, u32[]{:S(2)}) %all-to-all-start.1) | async-done | bytes 6291488 | tf_op jit(solution)/shard_map/all_to_all | solution.py:343
  183.9 45.5 %dense.1 = (bf16[128,192,128]{2,1,0:T(8,128)(2,1)}, f32[1,128]{1,0:T(1,128)}, f32[48,128]{1,0:T(8,128)}, f32[2048,256]{1,0:T(8,128)}, f32[256,768]{1,0:T(8,128)}, /*index=5*/f32[1,768]{1,0:T(1,128)}, f32[32,384]{1,0:T(8,128)}) custom-call(bf16[128,192,128]{2,1,0:T(8,128)(2,1)} %bitcast.5.x_ref, bf16[48,128]{1,0:T(8,128)(2,1)} %maximum_bitcast_fusion.wt_ref, ...), custom_call_target="tpu_custom_call" | custom-call | tf_op jit(solution)/shard_map/dense/pallas_call | solution.py:283
  229.4 83.0 %all_to_all.15.g_ref = bf16[16,8,192,128]{3,2,1,0:T(8,128)(2,1)} all-to-all(bf16[16,8,192,128]{3,2,1,0:T(8,128)(2,1)} %bitcast.51), channel_id=1, replica_groups=mesh['zh'=4,'x'=4,'y'=4,'zl'=2,'c'=2] {'x','y'}, dimensions={0} | all-to-all | bytes 12582912 | tf_op jit(solution)/shard_map/all_to_all | solution.py:359
  312.5 13.2 %table_grad.1 = f32[8,512,192]{2,1,0:T(8,128)} custom-call(s32[16,2048]{1,0:T(8,128)} %reshape.76.ids_ref, bf16[16,8,192,128]{3,2,1,0:T(8,128)(2,1)} %all_to_all.15.g_ref), custom_call_target="tpu_custom_call" | custom-call | tf_op jit(solution)/shard_map/table_grad/pallas_call | solution.py:262
  325.7 0.0 all-reduce.6.cloned.1.call-start
  325.7 89.6 %reduce-scatter.2.cloned.1.call-done = f32[2,512,192]{2,1,0:T(8,128)} async-done(((f32[8,512,192]{2,1,0:T(8,128)}), f32[2,512,192]{2,1,0:T(8,128)}) %reduce-scatter.2.cloned.1.call-update) | async-done | bytes 786448 | tf_op jit(solution)/shard_map/reduce_scatter | solution.py:364
  415.4 2.5 reshape.87
  417.9 2.5 copy.73
  420.5 0.8 copy-done.2
  421.2 0.1 slice.55
  421.3 0.1 reshape.88
  421.4 0.1 copy.71
  421.6 77.3 %all-reduce.1 = (f32[]{:T(128)}, f32[128,48]{1,0:T(8,128)S(1)}, f32[6144]{0:T(1024)S(1)}, f32[768]{0:T(1024)S(1)}) all-reduce(f32[]{:T(128)S(1)} %bitcast.65, f32[128,48]{1,0:T(8,128)S(1)} %bitcast.56, f32[6144]{0:T(1024)S(1)} %reshape.88, f32[768]{0:T(1024)S(1)} %reduce), channel_id=1, replica_groups=mesh['zh'=4,'x'=4,'y'=4,'zl'=2,'c'=2] {'zh','x','y','zl','c'}, use_global_device_ids=true, to_apply=%region_0.1 | all-reduce | flops 13057 | bytes 104456 | tf_op jit(solution)/shard_map/psum | solution.py:367
  498.9 0.7 copy.74
  499.5 0.1 slice_bitcast_fusion
  499.6 0.7 copy.75
  501.0 0.6 pad_maximum_fusion.2
  501.6 2.4 copy.76
  504.0 227.2 %all-reduce.8.cloned.1.call-done = (f32[2048,256]{1,0:T(8,128)}, f32[256,768]{1,0:T(8,128)}) async-done(((f32[2048,256]{1,0:T(8,128)}, f32[256,768]{1,0:T(8,128)}), (f32[2048,256]{1,0:T(8,128)}, f32[256,768]{1,0:T(8,128)})) %all-reduce.8.cloned.1.call-update) | async-done | bytes 2883600 | tf_op jit(solution)/shard_map/psum | solution.py:367
  731.2 3.1 copy.80
  734.4 0.9 copy.81
  (39 shorter events, 0.3 us)
Async XLA Ops:
  7.2 49.6 %all-gather.2.cloned.1.call-start = ((), (), s32[]{:S(2)}) async-start(), calls=%async_computation.4 | async-start | bytes 1966080 | tf_op jit(solution)/shard_map/all_gather | solution.py:340
  10.0 16.2 %all-to-all-start = ((s32[4,4,2048]{2,1,0:T(4,128)}), s32[4,4,2048]{2,1,0:T(4,128)S(1)}, u32[]{:S(2)}, u32[]{:S(2)}) async-start(s32[4,4,2048]{2,1,0:T(4,128)} %reshape.75), calls=%async_computation | async-start | bytes 262144 | tf_op jit(solution)/shard_map/all_to_all | solution.py:338
  77.6 6.8 copy-start.4
  77.6 6.9 copy-start.9
  77.6 7.5 %copy-start.6 = (bf16[128,16]{0,1:T(8,128)(2,1)S(1)}, bf16[128,16]{0,1:T(8,128)(2,1)}, u32[]{:S(2)}) copy-start(bf16[128,16]{0,1:T(8,128)(2,1)} %param.13) | copy-start | bytes 12292
  77.6 7.7 %copy-start.5 = (bf16[32,128]{1,0:T(8,128)(2,1)S(1)}, bf16[32,128]{1,0:T(8,128)(2,1)}, u32[]{:S(2)}) copy-start(bf16[32,128]{1,0:T(8,128)(2,1)} %param.14) | copy-start | bytes 24580
  77.6 8.7 %copy-start = (bf16[2048,256]{1,0:T(8,128)(2,1)S(1)}, bf16[2048,256]{1,0:T(8,128)(2,1)}, u32[]{:S(2)}) copy-start(bf16[2048,256]{1,0:T(8,128)(2,1)} %param.15) | copy-start | bytes 3145732
  77.6 106.4 %all-to-all-start.1 = ((bf16[16,8,192,128]{3,2,1,0:T(8,128)(2,1)}), bf16[16,8,192,128]{3,2,1,0:T(8,128)(2,1)}, u32[]{:S(2)}, u32[]{:S(2)}) async-start(bf16[16,8,192,128]{3,2,1,0:T(8,128)(2,1)} %lookup.1), calls=%async_computation.1 | async-start | bytes 12582912 | tf_op jit(solution)/shard_map/all_to_all | solution.py:343
  84.3 331.0 %reduce-scatter.2.cloned.1.call-start = ((), (), s32[]{:S(2)}) async-start(), calls=%async_computation.5 | async-start | bytes 5242880 | tf_op jit(solution)/shard_map/reduce_scatter | solution.py:364
  325.7 175.9 %all-reduce.6.cloned.1.call-start = ((), (), s32[]{:S(2)}) async-start(), calls=%async_computation.6 | async-start | bytes 2097152 | tf_op jit(solution)/shard_map/psum | solution.py:363
  415.3 315.9 %all-reduce.8.cloned.1.call-start = ((), (), s32[]{:S(2)}) async-start(), calls=%async_computation.7 | async-start | bytes 5767168 | tf_op jit(solution)/shard_map/psum | solution.py:367
  420.4 0.8 copy-start.2
  420.4 1.0 copy-start.3
  420.4 1.1 copy-start.7
  420.4 1.1 copy-start.8
  731.2 3.1 copy-start.1
Sparse Core Ops, SparseCore 0:
  9.8 46.8 all-gather.1
  325.8 89.4 reduce-scatter.1
  418.2 44.8 all-reduce.5
  469.0 262.1 all-reduce.7

commit v2 on v1

--- a/solution.py
+++ b/solution.py
@@ -14,6 +14,12 @@
 NT = (((1,), (1,)), ((), ()))
 TN = (((0,), (0,)), ((), ()))
 VMEM_LIMIT = 60 * 1024 * 1024
+MESH = pl.DeviceIdType.MESH
+AT_WOUT = 4096
+AT_GW = AT_WOUT + 1536
+AT_LIN = AT_GW + 48
+AT_HEAD = AT_LIN + 64
+DEN_ROWS = 6144
 
 
 def mm(a, b, dims=None):
@@ -55,7 +61,7 @@
 def scatter_kernel(ids_ref, g_ref, out_ref):
     n_src, n_f = g_ref.shape[:2]
     half = n_src * 64
-    rows = out_ref.shape[1]
+    rows = out_ref.shape[1] * 2 // 3
     group = 4
     for f in range(n_f):
         sums = [jnp.zeros((rows, 256), F32), jnp.zeros((rows, 256), F32)]
@@ -72,9 +78,11 @@
                 )
                 sums[h] = sums[h] + mm(hot.astype(BF), jnp.concatenate([main, rest], 1))
         s1, s2 = sums
-        out_ref[f, :, :128] = s1[:, :128] + s2[:, :128]
+        out_ref[f, :rows, :] = s1[:, :128] + s2[:, :128]
         tail = s1[:, 128:] + pltpu.roll(s2[:, 128:], 64, 1)
-        out_ref[f, :, 128:192] = tail[:, :64]
+        low, high = tail[: rows // 2], pltpu.roll(tail[rows // 2 :], 64, 1)
+        lane = lax.broadcasted_iota(jnp.int32, low.shape, 1)
+        out_ref[f, rows:, :] = jnp.where(lane < 64, low, high)
 
 
 def dense_kernel(
@@ -88,10 +96,8 @@
     label_ref,
     g_ref,
     loss_ref,
+    den_ref,
     gw_ref,
-    gwin_ref,
-    gwout_ref,
-    ghead_ref,
     ghl_ref,
     split_ref,
     xp_ref,
@@ -163,19 +169,29 @@
     logit = jnp.sum(factor * head, 1, keepdims=True) + jnp.concatenate([lin1, lin2], 0)
     target = label_ref[...]
     terms = jnp.maximum(logit, 0.0) + jnp.log1p(jnp.exp(-jnp.abs(logit))) - target * logit
-    loss_ref[...] = jnp.sum(jnp.broadcast_to(terms, (n_b, 128)), 0, keepdims=True)
+    loss_ref[...] = jnp.broadcast_to(
+        jnp.sum(jnp.broadcast_to(terms, (n_b, 128)), 0, keepdims=True), loss_ref.shape
+    )
     slope = scale * (1.0 / (1.0 + jnp.exp(-logit)) - target)
     slope_ref[...] = jnp.broadcast_to(slope, (n_b, 128))
-    ghead_ref[...] = jnp.sum(slope * factor, 0, keepdims=True)
+    den_ref[AT_HEAD:, :] = jnp.zeros((den_ref.shape[0] - AT_HEAD, 128), F32)
+    ghead = jnp.sum(slope * factor, 0, keepdims=True)
+    for i in range(ghead.shape[1] // 128):
+        den_ref[AT_HEAD + i : AT_HEAD + i + 1, :] = ghead[:, i * 128 : (i + 1) * 128]
     gfactor = (slope * head).astype(BF)
-    gwout_ref[...] = mm(hidden, gfactor, TN)
+    for i in range(gfactor.shape[1] // 128):
+        den_ref[AT_WOUT + i * 256 : AT_WOUT + (i + 1) * 256, :] = mm(
+            hidden, gfactor[:, i * 128 : (i + 1) * 128], TN
+        )
     ghidden = mm(gfactor, wout_ref[...], NT)
     gpre = (ghidden * sigma * (1.0 + pre_act * (1.0 - sigma))).astype(BF)
     first = jnp.zeros((n_b, n_f), F32)
     second = jnp.zeros((n_b, n_f), F32)
     for k in range(n_k):
         rows = slice(k * n_f, (k + 1) * n_f)
-        gwin_ref[rows, :] = mm(nb_ref[:, rows], gpre, TN)
+        gwin = mm(nb_ref[:, rows], gpre, TN)
+        den_ref[rows, :] = gwin[:, :128]
+        den_ref[width + k * n_f : width + (k + 1) * n_f, :] = gwin[:, 128:]
         gnormed = mm(gpre, win_ref[rows, :], NT)
         first = first + gnormed
         second = second + gnormed * inter_ref[k * n_b : (k + 1) * n_b, :]
@@ -238,6 +254,14 @@
         return carry
 
     lax.fori_loop(0, 64 // tile, back_group, 0)
+    den_ref[AT_GW : AT_GW + 48, :] = gw_ref[...]
+    ghl = ghl_ref[...]
+    second = ghl[:, 128:256]
+    lane = lax.broadcasted_iota(jnp.int32, second.shape, 1)
+    den_ref[AT_LIN : AT_LIN + 32, :] = ghl[:, :128] + ghl[:, 256:]
+    den_ref[AT_LIN + 32 : AT_LIN + 64, :] = jnp.where(
+        lane < 64, second + pltpu.roll(second, 64, 1), 0.0
+    )
 
 
 def whole(n):
@@ -261,7 +285,7 @@
     n_f = g.shape[1]
     return pl.pallas_call(
         scatter_kernel,
-        out_shape=jax.ShapeDtypeStruct((n_f, rows, 192), F32),
+        out_shape=jax.ShapeDtypeStruct((n_f, rows * 3 // 2, 128), F32),
         in_specs=whole(2),
         out_specs=whole(1)[0],
         compiler_params=pltpu.CompilerParams(vmem_limit_bytes=VMEM_LIMIT),
@@ -273,19 +297,17 @@
     n_f = x.shape[0]
     shapes = [
         (x.shape, BF),
-        ((1, 128), F32),
-        ((48, n_f), F32),
-        (win.shape, F32),
-        (wout.shape, F32),
-        (head.shape, F32),
-        ((32, 384), F32),
+        ((8, 128), F32),
+        ((DEN_ROWS, 128), F32),
     ]
     return pl.pallas_call(
         functools.partial(dense_kernel, scale),
         out_shape=[jax.ShapeDtypeStruct(*s) for s in shapes],
         in_specs=whole(7),
-        out_specs=whole(7),
+        out_specs=whole(3),
         scratch_shapes=[
+            pltpu.VMEM((48, n_f), F32),
+            pltpu.VMEM((32, 384), F32),
             pltpu.VMEM((3, n_f * 16, 128), F32),
             pltpu.VMEM((64, n_f, 384), BF),
             pltpu.VMEM((64, 48, 384), F32),
@@ -297,6 +319,237 @@
         compiler_params=pltpu.CompilerParams(vmem_limit_bytes=VMEM_LIMIT),
         name="dense",
     )(x, wt, win, wout, head, hpair, label)
+
+
+def reduce_kernel(
+    tab_ref,
+    den_ref,
+    loss_ref,
+    out_tab_ref,
+    out_den_ref,
+    out_loss_ref,
+    ta_ref,
+    tb_ref,
+    tc_ref,
+    td_ref,
+    te_ref,
+    da_ref,
+    db_ref,
+    dc_ref,
+    dd_ref,
+    de_ref,
+    df_ref,
+    la_ref,
+    lb_ref,
+    lc_ref,
+    ls_ref,
+    send_ref,
+    core_sem,
+    tz_sem,
+    tr_sem,
+    dp_sem,
+    dz_sem,
+    dg_sem,
+    dh_sem,
+    lc_sem,
+    lp_sem,
+    lz_sem,
+):
+    zh, x, y, zl, c = [lax.axis_index(name) for name in ("zh", "x", "y", "zl", "c")]
+    n_y, n_z, n_p = 4, 8, 16
+    z = zh * 2 + zl
+    p = x * n_y + y
+    other = 1 - c
+
+    def at_plane(q):
+        return (zh, q // n_y, q % n_y, zl, c)
+
+    def at_z(v):
+        return (v // 2, x, y, v % 2, c)
+
+    sibling = (zh, x, y, zl, other)
+    replicas = [sibling, (zh, x, y, 1 - zl, c), (zh, x, y, 1 - zl, other)]
+    barrier = pltpu.get_barrier_semaphore()
+    for d in range(1, n_p):
+        pl.semaphore_signal(barrier, inc=1, device_id=at_plane((p + d) % n_p), device_id_type=MESH)
+    for d in range(1, n_z):
+        pl.semaphore_signal(barrier, inc=1, device_id=at_z((z + d) % n_z), device_id_type=MESH)
+    for device in (replicas[0], replicas[2]):
+        pl.semaphore_signal(barrier, inc=1, device_id=device, device_id_type=MESH)
+    pl.semaphore_wait(barrier, n_p - 1 + n_z - 1 + 2)
+
+    sends = []
+
+    def send(src, dst, sem, device):
+        k = len(sends)
+        copy = pltpu.make_async_remote_copy(
+            src_ref=src,
+            dst_ref=dst,
+            send_sem=send_ref.at[k],
+            recv_sem=sem,
+            device_id=device,
+            device_id_type=MESH,
+        )
+        copy.start()
+        sends.append(copy)
+
+    def arrived(dst, sem):
+        pltpu.make_async_copy(dst, dst, sem).wait()
+
+    half = DEN_ROWS // 2
+    for v in range(4):
+        ta_ref[v] = tab_ref[2 * v + other].astype(BF)
+    send(ta_ref, tb_ref, core_sem.at[0], sibling)
+    da_ref[...] = den_ref[pl.ds(pl.multiple_of(other * half, half), half), :].astype(BF)
+    send(da_ref, db_ref, core_sem.at[1], sibling)
+    send(loss_ref, lc_ref, lc_sem, sibling)
+
+    arrived(tb_ref, core_sem.at[0])
+    for v in range(4):
+        mine = tab_ref[2 * v + c] + tb_ref[v].astype(F32)
+        tc_ref[2 * v] = mine[:384].astype(BF)
+        tc_ref[2 * v + 1] = mine[384:].astype(BF)
+    for d in range(1, n_z):
+        to = (z + d) % n_z
+        send(tc_ref.at[to], td_ref.at[z], tz_sem.at[z], at_z(to))
+
+    chunk = half // n_p
+    arrived(db_ref, core_sem.at[1])
+    for i in range(n_p):
+        rows = pl.ds(pl.multiple_of(c * half + i * chunk, chunk), chunk)
+        dc_ref[i] = (
+            den_ref[rows, :] + db_ref[i * chunk : (i + 1) * chunk, :].astype(F32)
+        ).astype(BF)
+    for d in range(1, n_p):
+        to = (p + d) % n_p
+        send(dc_ref.at[to], dd_ref.at[p], dp_sem.at[p], at_plane(to))
+    arrived(lc_ref, lc_sem)
+    loss = loss_ref[...] + lc_ref[...]
+    ls_ref[0] = loss
+    for d in range(1, n_p):
+        to = (p + d) % n_p
+        send(ls_ref.at[0], la_ref.at[p], lp_sem.at[p], at_plane(to))
+    la_ref[p] = loss
+
+    own = dc_ref[p].astype(F32)
+    for d in range(1, n_p):
+        q = (p + d) % n_p
+        arrived(dd_ref.at[q], dp_sem.at[q])
+        own = own + dd_ref[q].astype(F32)
+    de_ref[z] = own.astype(BF)
+    for d in range(1, n_z):
+        send(de_ref.at[z], de_ref.at[z], dz_sem.at[z], at_z((z + d) % n_z))
+    for d in range(1, n_p):
+        q = (p + d) % n_p
+        arrived(la_ref.at[q], lp_sem.at[q])
+    loss = la_ref[0]
+    for q in range(1, n_p):
+        loss = loss + la_ref[q]
+    ls_ref[1] = loss
+    for d in range(1, n_z):
+        send(ls_ref.at[1], lb_ref.at[z], lz_sem.at[z], at_z((z + d) % n_z))
+    lb_ref[z] = loss
+
+    own = tc_ref[z].astype(F32)
+    for d in range(1, n_z):
+        v = (z + d) % n_z
+        arrived(td_ref.at[v], tz_sem.at[v])
+        own = own + td_ref[v].astype(F32)
+    te_ref[2 * c + zl] = own.astype(BF)
+    for device in replicas:
+        send(te_ref.at[2 * c + zl], te_ref.at[2 * c + zl], tr_sem.at[2 * c + zl], device)
+
+    for d in range(1, n_z):
+        v = (z + d) % n_z
+        arrived(de_ref.at[v], dz_sem.at[v])
+    own = de_ref[0].astype(F32)
+    for v in range(1, n_z):
+        own = own + de_ref[v].astype(F32)
+    mine = c * n_p + p
+    df_ref[mine] = own.astype(BF)
+    for d in range(1, n_p):
+        send(df_ref.at[mine], df_ref.at[mine], dg_sem.at[p], at_plane((p + d) % n_p))
+    send(df_ref.at[mine], df_ref.at[mine], dh_sem.at[p], sibling)
+
+    for d in range(1, 4):
+        k = (2 * c + zl + d) % 4
+        arrived(te_ref.at[k], tr_sem.at[k])
+    n_rows = out_tab_ref.shape[1]
+    for j in range(2):
+        low, high = te_ref[2 * j].astype(F32), te_ref[2 * j + 1].astype(F32)
+        out_tab_ref[j, :384, :128] = low
+        out_tab_ref[j, 384:n_rows, :128] = high[: n_rows - 384]
+        rest = high[n_rows - 384 :]
+        out_tab_ref[j, : n_rows // 2, 128:192] = rest[:, :64]
+        out_tab_ref[j, n_rows // 2 :, 128:192] = pltpu.roll(rest, 64, 1)[:, :64]
+
+    for d in range(1, n_z):
+        v = (z + d) % n_z
+        arrived(lb_ref.at[v], lz_sem.at[v])
+    loss = lb_ref[0]
+    for v in range(1, n_z):
+        loss = loss + lb_ref[v]
+    out_loss_ref[...] = loss
+
+    for d in range(1, n_p):
+        q = (p + d) % n_p
+        arrived(df_ref.at[c * n_p + q], dg_sem.at[q])
+        send(df_ref.at[c * n_p + q], df_ref.at[c * n_p + q], dh_sem.at[q], sibling)
+    for q in range(n_p):
+        arrived(df_ref.at[other * n_p + q], dh_sem.at[q])
+    for i in range(2 * n_p):
+        out_den_ref[i * chunk : (i + 1) * chunk, :] = df_ref[i].astype(F32)
+    for copy in sends:
+        copy.wait_send()
+
+
+def reduce_all(tab, den, loss, rows):
+    n_f = tab.shape[0]
+    half = DEN_ROWS // 2
+    chunk = half // 16
+    dma = pltpu.SemaphoreType.DMA
+    return pl.pallas_call(
+        reduce_kernel,
+        out_shape=[
+            jax.ShapeDtypeStruct((2, rows, 192), F32),
+            jax.ShapeDtypeStruct(den.shape, F32),
+            jax.ShapeDtypeStruct(loss.shape, F32),
+        ],
+        in_specs=whole(3),
+        out_specs=whole(3),
+        scratch_shapes=[
+            pltpu.VMEM((4, 768, 128), BF),
+            pltpu.VMEM((4, 768, 128), BF),
+            pltpu.VMEM((8, 384, 128), BF),
+            pltpu.VMEM((8, 384, 128), BF),
+            pltpu.VMEM((4, 384, 128), BF),
+            pltpu.VMEM((half, 128), BF),
+            pltpu.VMEM((half, 128), BF),
+            pltpu.VMEM((16, chunk, 128), BF),
+            pltpu.VMEM((16, chunk, 128), BF),
+            pltpu.VMEM((8, chunk, 128), BF),
+            pltpu.VMEM((32, chunk, 128), BF),
+            pltpu.VMEM((16, 8, 128), F32),
+            pltpu.VMEM((8, 8, 128), F32),
+            pltpu.VMEM((8, 128), F32),
+            pltpu.VMEM((2, 8, 128), F32),
+            dma((96,)),
+            dma((2,)),
+            dma((8,)),
+            dma((4,)),
+            dma((16,)),
+            dma((8,)),
+            dma((16,)),
+            dma((16,)),
+            dma,
+            dma((16,)),
+            dma((8,)),
+        ],
+        compiler_params=pltpu.CompilerParams(
+            vmem_limit_bytes=VMEM_LIMIT, collective_id=0, has_side_effects=True
+        ),
+        name="reduce",
+    )(tab, den, loss)
 
 
 def table_weights(t):
@@ -353,21 +606,19 @@
     head = w_head[:n_out].astype(F32)[None, :]
     hpair = pair_head(w_head, n_out)
     label = click_labels.astype(F32)
-    g, loss, gw, gwin, gwout, ghead, ghl = dense(
-        scale, x, wt, win, w_out, head, hpair, label
-    )
+    g, loss, den = dense(scale, x, wt, win, w_out, head, hpair, label)
     back = lax.all_to_all(
         g.reshape(y.shape), ("x", "y"), split_axis=0, concat_axis=0, tiled=True
     )
     partial = scatter(ids, back, rows)
-    partial = lax.psum(partial, ("zl", "c"))
-    table_grad = lax.psum_scatter(partial, "zh", scatter_dimension=0, tiled=True)
-
-    ghl = ghl[:, :192] + jnp.concatenate([ghl[:, 256:], ghl[:, 192:256]], 1)
-    sums = lax.psum(
-        (loss[0, 0], gw, gwin, gwout, ghead[0], ghl), ("zh", "x", "y", "zl", "c")
-    )
-    loss, gw, gwin, gwout, ghead, ghl = sums
+    table_grad, den, loss = reduce_all(partial, den, loss, rows)
+    loss = loss[0, 0]
+    gwin = jnp.concatenate([den[:2048], den[2048:4096]], 1)
+    gwout = den[AT_WOUT:AT_GW].reshape(-1, 256, 128).transpose(1, 0, 2).reshape(w_out.shape)
+    gw = den[AT_GW:AT_LIN]
+    lin = den[AT_LIN:AT_HEAD].reshape(2, n_lin, 128)
+    lin = jnp.concatenate([lin[0], lin[1, :, :64]], 1)
+    ghead = jnp.concatenate([den[AT_HEAD : AT_HEAD + n_out // 128].reshape(-1), lin.reshape(-1)])
 
     def natural(a):
         rest = a.shape[1:]
@@ -376,7 +627,6 @@
 
     gw = natural(gw.T)
     gwin = natural(gwin.reshape(n_rank, n_feat, -1).transpose(1, 0, 2)).reshape(w_in.shape)
-    ghead = jnp.concatenate([ghead, ghl.reshape(-1)])
     return (loss / total, gw[:, :n_rank], gw[:, n_rank:].T, gwin, gwout, ghead, table_grad)
 
 

time: 744 us -> 417 us (0.56)
  waiting for transfers between devices: 449 us -> 132 us
  blocking collectives: 160 us -> 83 us
  Pallas kernels: 72.8 us -> 133 us
    psum x2 -> x0, waiting for transfers between devices: 227 us -> none  [the longest x1 227 us: per_device(): lax.psum((loss[0, 0], gw, gwin, gwout, ghead[0], ghl), ('zh', 'x', 'y', '...]
    reduce_scatter x1 -> x0, waiting for transfers between devices: 89.6 us -> none  [per_device(): lax.psum_scatter(partial, 'zh', scatter_dimension=0, tiled=True)]
    psum x1 -> x0, blocking collectives: 77.3 us -> none  [per_device(): lax.psum((loss[0, 0], gw, gwin, gwout, ghead[0], ghl), ('zh', 'x', 'y', '...]
    pallas_call x1 -> x2, Pallas kernels: 13.2 us -> 72.9 us  [the longest x1 59.9 us: reduce_all(): pl.pallas_call(reduce_kernel, out_shape=[jax.ShapeDtypeStruct((2, rows, 1...]
  transfers between devices with their start and end apart: 6 -> 3, of which waited for: 5 -> 3; matrix products, arithmetic and copies ran while one was open for 2% -> 2% of each run, Pallas kernels for 0% -> 0%
where the time goes in v2:
time: 417 us; the launch traced here: 416 us
  Pallas kernels  133 us (32%)
  waiting for transfers between devices  132 us (32%)
  blocking collectives  83 us (20%)
  local copies, waits for them, and re-layouts  30.5 us (7%)
  between operations  16 us (4%)
  starting transfers between devices  15.8 us (4%)
  other arithmetic  6.19 us (1%)
    all_to_all x1, waiting for transfers between devices, per_device(): x = lax.all_to_all(y, ('x', 'y'), split_axis=0, concat_axis=0, tiled=True)  94.2 us
    all_to_all x1, blocking collectives, per_device(): lax.all_to_all(g.reshape(y.shape), ('x', 'y'), split_axis=0, concat_axis=...  83 us
    pallas_call x1, Pallas kernels, reduce_all(): pl.pallas_call(reduce_kernel, out_shape=[jax.ShapeDtypeStruct((2, rows, 1...  59.9 us
    pallas_call x1, Pallas kernels, dense(): pl.pallas_call(functools.partial(dense_kernel, scale), out_shape=[jax.Sha...  45.8 us
    all_gather x1, waiting for transfers between devices, per_device(): all_tables = lax.all_gather(tables, 'zh', axis=0, tiled=True)  29.8 us
    pallas_call x1, Pallas kernels, lookup(): pl.pallas_call(lookup_kernel, out_shape=jax.ShapeDtypeStruct((n_dest, n_f...  14.1 us
    pallas_call x1, Pallas kernels, scatter(): pl.pallas_call(scatter_kernel, out_shape=jax.ShapeDtypeStruct((n_f, rows...  13 us
    all_to_all x1, starting transfers between devices, per_device(): ids = lax.all_to_all(ids, 'zh', split_axis=0, concat_axis=0, tiled=True)  9.01 us
  transfers between devices with their start and end apart: 3, of which 3 were waited for; matrix products, arithmetic and copies ran while one was open for 2% of the time, Pallas kernels for 0%

profile of v2, /device:TPU:1, one launch (start us, length us, event | category | flops | bytes accessed | tf_op | source)
XLA Modules:
  0.0 416.2 jit_solution(6731803078680617287)
XLA Ops:
  7.2 0.7 all-gather.2.cloned.1.call-update
  7.9 1.0 compare_select_fusion
  8.9 0.3 reshape.90
  9.2 0.8 reshape.91
  10.0 9.0 %all-to-all-start = ((s32[4,4,2048]{2,1,0:T(4,128)}), s32[4,4,2048]{2,1,0:T(4,128)S(1)}, u32[]{:S(2)}, u32[]{:S(2)}) async-start(s32[4,4,2048]{2,1,0:T(4,128)} %reshape.91), calls=%async_computation | async-start | bytes 262144 | tf_op jit(solution)/shard_map/all_to_all | solution.py:591
  19.0 7.2 %all-to-all-done = s32[4,4,2048]{2,1,0:T(4,128)S(1)} async-done(((s32[4,4,2048]{2,1,0:T(4,128)}), s32[4,4,2048]{2,1,0:T(4,128)S(1)}, u32[]{:S(2)}, u32[]{:S(2)}) %all-to-all-start) | async-done | bytes 131104 | tf_op jit(solution)/shard_map/all_to_all | solution.py:591
  26.2 0.7 reshape.92.ids_ref
  26.9 29.8 %all-gather.2.cloned.1.call-done = bf16[8,512,192]{1,2,0:T(8,128)(2,1)} async-done(((bf16[2,512,192]{1,2,0:T(8,128)(2,1)}), bf16[8,512,192]{1,2,0:T(8,128)(2,1)}) %all-gather.2.cloned.1.call-update) | async-done | bytes 1572880 | tf_op jit(solution)/shard_map/all_gather | solution.py:593
  56.7 2.7 copy.65
  59.5 0.2 slice.79
  59.7 0.2 slice.78
  59.8 1.7 concatenate.21.w1_ref
  61.5 1.9 pad_maximum_fusion.w2_ref
  63.5 14.1 %lookup.1 = bf16[16,8,192,128]{3,2,1,0:T(8,128)(2,1)} custom-call(s32[16,2048]{1,0:T(8,128)} %reshape.92.ids_ref, bf16[8,512,256]{2,1,0:T(8,128)(2,1)} %concatenate.21.w1_ref, bf16[8,512,256]{2,1,0:T(8,128)(2,1)} %pad_maximum_fusion.w2_ref), custom_call_target="tpu_custom_call" | custom-call | tf_op jit(solution)/shard_map/lookup/pallas_call | solution.py:273
  77.6 6.7 %all-to-all-start.1 = ((bf16[16,8,192,128]{3,2,1,0:T(8,128)(2,1)}), bf16[16,8,192,128]{3,2,1,0:T(8,128)(2,1)}, u32[]{:S(2)}, u32[]{:S(2)}) async-start(bf16[16,8,192,128]{3,2,1,0:T(8,128)(2,1)} %lookup.1), calls=%async_computation.1 | async-start | bytes 12582912 | tf_op jit(solution)/shard_map/all_to_all | solution.py:596
  84.3 0.1 reshape.111
  84.4 0.6 reshape.110.head_ref
  85.0 0.1 copy.68
  85.2 0.1 copy.70
  85.5 0.8 copy.75.label_ref
  86.2 1.0 copy.74
  87.3 1.2 reshape.98
  88.5 0.6 maximum_bitcast_fusion.wt_ref
  89.1 0.7 pad_maximum_fusion.2.hpair_ref
  89.8 94.2 %all-to-all-done.1 = bf16[16,8,192,128]{3,2,1,0:T(8,128)(2,1)} async-done(((bf16[16,8,192,128]{3,2,1,0:T(8,128)(2,1)}), bf16[16,8,192,128]{3,2,1,0:T(8,128)(2,1)}, u32[]{:S(2)}, u32[]{:S(2)}) %all-to-all-start.1) | async-done | bytes 6291488 | tf_op jit(solution)/shard_map/all_to_all | solution.py:596
  183.9 45.8 %dense.1 = (bf16[128,192,128]{2,1,0:T(8,128)(2,1)}, f32[8,128]{1,0:T(8,128)}, f32[6144,128]{1,0:T(8,128)}) custom-call(bf16[128,192,128]{2,1,0:T(8,128)(2,1)} %bitcast.5.x_ref, bf16[48,128]{1,0:T(8,128)(2,1)} %maximum_bitcast_fusion.wt_ref, bf16[2048,256]{1,0:T(8,128)(2,1)} %bitcast.61, bf16[256,768]{1,0:T(8,128)(2,1)} %wout_ref.1, ...), custom_call_target="tpu_custom_call" | custom-call | tf_op jit(solution)/shard_map/dense/pallas_call | solution.py:303
  229.8 83.0 %all_to_all.15.g_ref = bf16[16,8,192,128]{3,2,1,0:T(8,128)(2,1)} all-to-all(bf16[16,8,192,128]{3,2,1,0:T(8,128)(2,1)} %bitcast.60), channel_id=1, replica_groups=mesh['zh'=4,'x'=4,'y'=4,'zl'=2,'c'=2] {'x','y'}, dimensions={0} | all-to-all | bytes 12582912 | tf_op jit(solution)/shard_map/all_to_all | solution.py:610
  312.8 13.0 %table_grad.1.tab_ref = f32[8,768,128]{2,1,0:T(8,128)} custom-call(s32[16,2048]{1,0:T(8,128)} %reshape.92.ids_ref, bf16[16,8,192,128]{3,2,1,0:T(8,128)(2,1)} %all_to_all.15.g_ref), custom_call_target="tpu_custom_call" | custom-call | tf_op jit(solution)/shard_map/table_grad/pallas_call | solution.py:286
  325.8 59.9 %reduce.1 = (f32[2,512,192]{2,1,0:T(8,128)}, f32[6144,128]{1,0:T(8,128)}, f32[8,128]{1,0:T(8,128)}) custom-call(f32[8,768,128]{2,1,0:T(8,128)} %table_grad.1.tab_ref, f32[6144,128]{1,0:T(8,128)} %get-tuple-element.14.den_ref, f32[8,128]{1,0:T(8,128)} %get-tuple-element.15.loss_ref), custom_call_target="tpu_custom_call" | custom-call | tf_op jit(solution)/shard_map/reduce/pallas_call | solution.py:511
  385.7 0.7 slice_bitcast_fusion.3
  386.4 0.7 slice.75
  387.1 0.7 slice_bitcast_fusion.1
  387.9 0.8 slice.76
  388.6 2.2 slice.73
  390.8 2.6 fusion
  393.4 1.2 slice.67
  394.6 0.1 reshape.109
  394.7 0.1 copy.76
  394.8 0.1 slice_bitcast_fusion
  394.9 0.7 copy.80
  395.6 0.7 copy.81
  396.3 1.4 copy.83
  397.7 1.4 pad_maximum_fusion.1
  399.0 2.3 reshape.104
  401.3 4.2 %copy.78 = f32[16,4,2,16,256]{4,3,2,0,1:T(8,128)} copy(f32[16,4,2,16,256]{4,2,1,0,3:T(2,128)} %reshape.104) | data formatting | bytes 4194304 | tf_op jit(solution)/shard_map/reshape | solution.py:625
  405.5 0.3 copy.79
  405.8 1.1 copy.82
  407.6 0.6 pad_maximum_fusion.4
  (30 shorter events, 0.3 us)
Async XLA Ops:
  7.2 49.6 %all-gather.2.cloned.1.call-start = ((), (), s32[]{:S(2)}) async-start(), calls=%async_computation.3 | async-start | bytes 1966080 | tf_op jit(solution)/shard_map/all_gather | solution.py:593
  10.0 16.2 %all-to-all-start = ((s32[4,4,2048]{2,1,0:T(4,128)}), s32[4,4,2048]{2,1,0:T(4,128)S(1)}, u32[]{:S(2)}, u32[]{:S(2)}) async-start(s32[4,4,2048]{2,1,0:T(4,128)} %reshape.91), calls=%async_computation | async-start | bytes 262144 | tf_op jit(solution)/shard_map/all_to_all | solution.py:591
  77.5 6.8 %copy-start.3 = (bf16[6912]{0:T(1024)(128)(2,1)S(1)}, bf16[6912]{0:T(1024)(128)(2,1)}, u32[]{:S(2)}) copy-start(bf16[6912]{0:T(1024)(128)(2,1)} %param.17) | copy-start | bytes 41476
  77.5 6.9 %copy-start.6 = (s32[128,1]{0,1:T(1,128)S(1)}, s32[128,1]{0,1:T(1,128)}, u32[]{:S(2)}) copy-start(s32[128,1]{0,1:T(1,128)} %param.11) | copy-start | bytes 1540
  77.5 7.5 %copy-start.5 = (bf16[128,16]{0,1:T(8,128)(2,1)S(1)}, bf16[128,16]{0,1:T(8,128)(2,1)}, u32[]{:S(2)}) copy-start(bf16[128,16]{0,1:T(8,128)(2,1)} %param.13) | copy-start | bytes 12292
  77.5 7.7 %copy-start.4 = (bf16[32,128]{1,0:T(8,128)(2,1)S(1)}, bf16[32,128]{1,0:T(8,128)(2,1)}, u32[]{:S(2)}) copy-start(bf16[32,128]{1,0:T(8,128)(2,1)} %param.14) | copy-start | bytes 24580
  77.6 8.7 %copy-start.2 = (bf16[2048,256]{1,0:T(8,128)(2,1)S(1)}, bf16[2048,256]{1,0:T(8,128)(2,1)}, u32[]{:S(2)}) copy-start(bf16[2048,256]{1,0:T(8,128)(2,1)} %param.15) | copy-start | bytes 3145732
  77.6 106.4 %all-to-all-start.1 = ((bf16[16,8,192,128]{3,2,1,0:T(8,128)(2,1)}), bf16[16,8,192,128]{3,2,1,0:T(8,128)(2,1)}, u32[]{:S(2)}, u32[]{:S(2)}) async-start(bf16[16,8,192,128]{3,2,1,0:T(8,128)(2,1)} %lookup.1), calls=%async_computation.1 | async-start | bytes 12582912 | tf_op jit(solution)/shard_map/all_to_all | solution.py:596
  388.6 7.6 %copy-start.1 = (f32[2,512,192]{2,1,0:T(8,128)S(1)}, f32[2,512,192]{2,1,0:T(8,128)}, u32[]{:S(2)}) copy-start(f32[2,512,192]{2,1,0:T(8,128)} %get-tuple-element.46) | copy-start | bytes 2359300
  401.3 4.2 %copy-start = (f32[1536,128]{1,0:T(8,128)S(1)}, f32[1536,128]{1,0:T(8,128)}, u32[]{:S(2)}) copy-start(f32[1536,128]{1,0:T(8,128)} %slice.73) | copy-start | bytes 2359300
Sparse Core Ops, SparseCore 0:
  9.8 46.8 all-gather.1

commit v3 on v2

--- a/solution.py
+++ b/solution.py
@@ -28,75 +28,47 @@
     return lax.dot_general(a, b, dims, preferred_element_type=F32)
 
 
-def lookup_kernel(ids_ref, w1_ref, w2_ref, y_ref, col_ref):
-    n_dest, n_f = y_ref.shape[:2]
-    half = n_dest * 64
-    rows = w1_ref.shape[1]
-    for i in range(2 * half // 128):
-        col_ref[pl.ds(i * 128, 128), :] = ids_ref[:, i * 128 : (i + 1) * 128].T
-    group = 4
-
-    def chunk(c, carry):
-        base = pl.multiple_of(c * group * 64, group * 64)
-        for f in range(n_f):
-            parts = []
-            for h, w_ref in ((0, w1_ref), (1, w2_ref)):
-                both = col_ref[pl.ds(h * half + base, group * 64), 2 * f : 2 * f + 2]
-                lane = lax.broadcasted_iota(jnp.int32, (group * 64, rows), 1)
-                hot = jnp.where(lane == both[:, 0:1], 1.0, 0.0) + jnp.where(
-                    lane == both[:, 1:2], 1.0, 0.0
-                )
-                parts.append(mm(hot.astype(BF), w_ref[f]))
-            p1, p2 = parts
-            rest = p1[:, 128:] + p2[:, 128:]
-            for k, block in enumerate((p1[:, :128], p2[:, :128], rest)):
-                y_ref[pl.ds(c * group, group), f, k * 64 : (k + 1) * 64, :] = block.astype(
-                    BF
-                ).reshape(group, 64, 128)
-        return carry
-
-    lax.fori_loop(0, n_dest // group, chunk, 0)
-
-
-def scatter_kernel(ids_ref, g_ref, out_ref):
-    n_src, n_f = g_ref.shape[:2]
-    half = n_src * 64
-    rows = out_ref.shape[1] * 2 // 3
-    group = 4
-    for f in range(n_f):
-        sums = [jnp.zeros((rows, 256), F32), jnp.zeros((rows, 256), F32)]
-        for c in range(n_src // group):
-            rest = g_ref[c * group : (c + 1) * group, f, 128:192, :].reshape(group * 64, 128)
-            for h in range(2):
-                base = h * half + c * group * 64
-                row = lax.broadcasted_iota(jnp.int32, (rows, group * 64), 0)
-                id0 = ids_ref[2 * f : 2 * f + 1, base : base + group * 64]
-                id1 = ids_ref[2 * f + 1 : 2 * f + 2, base : base + group * 64]
-                hot = jnp.where(row == id0, 1.0, 0.0) + jnp.where(row == id1, 1.0, 0.0)
-                main = g_ref[c * group : (c + 1) * group, f, h * 64 : (h + 1) * 64, :].reshape(
-                    group * 64, 128
-                )
-                sums[h] = sums[h] + mm(hot.astype(BF), jnp.concatenate([main, rest], 1))
-        s1, s2 = sums
-        out_ref[f, :rows, :] = s1[:, :128] + s2[:, :128]
-        tail = s1[:, 128:] + pltpu.roll(s2[:, 128:], 64, 1)
-        low, high = tail[: rows // 2], pltpu.roll(tail[rows // 2 :], 64, 1)
-        lane = lax.broadcasted_iota(jnp.int32, low.shape, 1)
-        out_ref[f, rows:, :] = jnp.where(lane < 64, low, high)
-
-
-def dense_kernel(
+def plane_links(zh, zl, c, p):
+    def copy(src, dst, send_sems, recv_sems, q, to):
+        return pltpu.make_async_remote_copy(
+            src_ref=src.at[q, :, to],
+            dst_ref=dst.at[q, :, p],
+            send_sem=send_sems.at[q, to],
+            recv_sem=recv_sems.at[q, p],
+            device_id=(zh, to // 4, to % 4, zl, c),
+            device_id_type=MESH,
+        )
+
+    return copy
+
+
+def arrived(dst, sem):
+    pltpu.make_async_copy(dst, dst, sem).wait()
+
+
+def main_kernel(
     scale,
-    x_ref,
+    ids_ref,
+    tab_ref,
     wt_ref,
     win_ref,
     wout_ref,
     head_ref,
     hpair_ref,
     label_ref,
-    g_ref,
+    part_ref,
+    den_ref,
     loss_ref,
-    den_ref,
+    tz_ref,
+    idz_ref,
+    col_ref,
+    w1_ref,
+    w2_ref,
+    y_ref,
+    x_ref,
+    bk_ref,
+    winp_ref,
+    acc_ref,
     gw_ref,
     ghl_ref,
     split_ref,
@@ -106,20 +78,137 @@
     nb_ref,
     ld_ref,
     slope_ref,
+    zsend,
+    zsem,
+    fsem,
+    isem,
+    ysend,
+    xrecv,
+    gsend,
+    brecv,
 ):
-    n_f = x_ref.shape[0]
-    n_b = 128
-    n_k = 16
-    tile = 16
+    zh, px, py, zl, c = [lax.axis_index(name) for name in ("zh", "x", "y", "zl", "c")]
+    n_p, n_z = 16, 8
+    z = zh * 2 + zl
+    p = px * 4 + py
+    other = 1 - c
+    sibling = (zh, px, py, zl, other)
+    n_f, n_b, n_k, tile = 128, 128, 16, 16
+    rows = w1_ref.shape[1]
+    width = n_k * n_f
+
+    barrier = pltpu.get_barrier_semaphore()
+    for d in range(1, n_p):
+        q = (p + d) % n_p
+        pl.semaphore_signal(
+            barrier, inc=1, device_id=(zh, q // 4, q % 4, zl, c), device_id_type=MESH
+        )
+    for d in range(1, n_z):
+        v = (z + d) % n_z
+        pl.semaphore_signal(
+            barrier, inc=1, device_id=(v // 2, px, py, v % 2, c), device_id_type=MESH
+        )
+    pl.semaphore_signal(barrier, inc=1, device_id=sibling, device_id_type=MESH)
+    pl.semaphore_wait(barrier, n_p - 1 + n_z - 1 + 1)
+
+    sends = []
+
+    def send(src, dst, sem, device):
+        copy = pltpu.make_async_remote_copy(
+            src_ref=src,
+            dst_ref=dst,
+            send_sem=zsend.at[len(sends)],
+            recv_sem=sem,
+            device_id=device,
+            device_id_type=MESH,
+        )
+        copy.start()
+        sends.append(copy)
+
+    for d in range(1, 4):
+        to = (zh + d) % 4
+        send(ids_ref.at[to], idz_ref.at[zh], isem.at[zh], (to, px, py, zl, c))
+    near = (zh + 3 + 2 * zl) % 4
+    for to, lo in ((near, 0), (near, 1), ((zh + 2) % 4, 1 - zl)):
+        send(tab_ref.at[c], tz_ref.at[2 * zh + c], zsem.at[zh], (to, px, py, lo, c))
+    idz_ref[zh] = ids_ref[zh]
+    tz_ref[2 * zh] = tab_ref[0]
+    tz_ref[2 * zh + 1] = tab_ref[1]
+    for d in (1, 3, 2):
+        v = (zh + d) % 4
+        arrived(tz_ref.at[2 * v + c], zsem.at[v])
+        send(tz_ref.at[2 * v + c], tz_ref.at[2 * v + c], fsem.at[v], sibling)
+    for d in range(1, 4):
+        v = (zh + d) % 4
+        arrived(idz_ref.at[v], isem.at[v])
+    for i in range(n_p):
+        block = idz_ref[:, :, i * 128 : (i + 1) * 128].reshape(32, 128)
+        col_ref[i * 128 : (i + 1) * 128, :] = block.T
+    for d in range(1, 4):
+        v = (zh + d) % 4
+        arrived(tz_ref.at[2 * v + other], fsem.at[v])
+
+    def weights(f, carry):
+        main = tz_ref[f, :rows, :]
+        rest = tz_ref[f, rows:, :].astype(F32)
+        turned = pltpu.roll(rest, 64, 1)
+        low = lax.broadcasted_iota(jnp.int32, rest.shape, 1) < 64
+        w1_ref[f, :, :128] = main
+        w2_ref[f, :, :128] = main
+        w1_ref[f, : rows // 2, 128:] = jnp.where(low, rest, 0.0).astype(BF)
+        w1_ref[f, rows // 2 :, 128:] = jnp.where(low, turned, 0.0).astype(BF)
+        w2_ref[f, : rows // 2, 128:] = jnp.where(low, 0.0, turned).astype(BF)
+        w2_ref[f, rows // 2 :, 128:] = jnp.where(low, 0.0, rest).astype(BF)
+        return carry
+
+    lax.fori_loop(0, 8, weights, 0)
+
+    link = plane_links(zh, zl, c, p)
+
+    def lookup(q, carry):
+        for f in range(8):
+            at = 8 * (f // 2) + 2 * (f % 2)
+            parts = []
+            for h, w_ref in ((0, w1_ref), (1, w2_ref)):
+                first = pl.multiple_of((q * 2 + h) * 256, 256)
+                both = col_ref[pl.ds(first, 256), at : at + 2]
+                lane = lax.broadcasted_iota(jnp.int32, (256, rows), 1)
+                hot = jnp.where(lane == both[:, 0:1], 1.0, 0.0) + jnp.where(
+                    lane == both[:, 1:2], 1.0, 0.0
+                )
+                parts.append(mm(hot.astype(BF), w_ref[f]))
+            p1, p2 = parts
+            rest = p1[:, 128:] + p2[:, 128:]
+            for k, block in enumerate((p1[:, :128], p2[:, :128], rest)):
+                y_ref[q, f // 2, :, f % 2, k * tile : (k + 1) * tile, :] = block.astype(
+                    BF
+                ).reshape(n_p, tile, 128)
+        for d in range(1, n_p):
+            link(y_ref, x_ref, ysend, xrecv, q, (p + d) % n_p).start()
+        x_ref[q, :, p] = y_ref[q, :, p]
+        return carry
+
+    lax.fori_loop(0, 4, lookup, 0)
+
+    for side in range(2):
+        cols = slice(side * 128, (side + 1) * 128)
+        split_ref[side] = win_ref[:, cols].astype(F32)
+        for k in range(n_k):
+            winp_ref[k * n_f : (k + 1) * n_f, cols] = split_ref[
+                side, pl.ds(k, n_f, stride=n_k), :
+            ].astype(BF)
+
     lane1 = lax.broadcasted_iota(jnp.int32, (n_k, 384), 1) < 192
     row_lane1 = lax.broadcasted_iota(jnp.int32, (1, 384), 1) < 192
     wt = wt_ref[...]
 
     def load_group(q, carry):
+        for d in range(1, n_p):
+            src = (p + n_p - d) % n_p
+            arrived(x_ref.at[q, :, src], xrecv.at[q, src])
         for part in range(3):
-            block = x_ref[:, pl.ds(pl.multiple_of(part * 64 + q * tile, tile), tile), :]
+            block = x_ref[q, :, :, :, part * tile : (part + 1) * tile, :]
             split_ref[part] = block.astype(F32).reshape(n_f * tile, 128)
-
         def pair(j, inner):
             p = q * tile + j
             pieces = [
@@ -147,7 +236,6 @@
     total = jnp.zeros((n_b, n_f), F32)
     for k in range(n_k):
         total = total + inter_ref[k * n_b : (k + 1) * n_b, :]
-    width = n_k * n_f
     center = jnp.sum(total, 1, keepdims=True) / width
     total = jnp.zeros((n_b, n_f), F32)
     for k in range(n_k):
@@ -158,7 +246,7 @@
         normed = (inter_ref[k * n_b : (k + 1) * n_b, :] - center) * rstd
         inter_ref[k * n_b : (k + 1) * n_b, :] = normed
         nb_ref[:, k * n_f : (k + 1) * n_f] = normed.astype(BF)
-    pre_act = mm(nb_ref[...], win_ref[...])
+    pre_act = mm(nb_ref[...], winp_ref[...])
     sigma = 1.0 / (1.0 + jnp.exp(-pre_act))
     hidden = (pre_act * sigma).astype(BF)
     factor = mm(hidden, wout_ref[...])
@@ -188,21 +276,24 @@
     first = jnp.zeros((n_b, n_f), F32)
     second = jnp.zeros((n_b, n_f), F32)
     for k in range(n_k):
-        rows = slice(k * n_f, (k + 1) * n_f)
-        gwin = mm(nb_ref[:, rows], gpre, TN)
-        den_ref[rows, :] = gwin[:, :128]
+        feats = slice(k * n_f, (k + 1) * n_f)
+        gwin = mm(nb_ref[:, feats], gpre, TN)
+        den_ref[feats, :] = gwin[:, :128]
         den_ref[width + k * n_f : width + (k + 1) * n_f, :] = gwin[:, 128:]
-        gnormed = mm(gpre, win_ref[rows, :], NT)
+        gnormed = mm(gpre, winp_ref[feats, :], NT)
         first = first + gnormed
         second = second + gnormed * inter_ref[k * n_b : (k + 1) * n_b, :]
     mean1 = jnp.sum(first, 1, keepdims=True) / width
     mean2 = jnp.sum(second, 1, keepdims=True) / width
     for k in range(n_k):
-        rows = slice(k * n_f, (k + 1) * n_f)
+        feats = slice(k * n_f, (k + 1) * n_f)
         span = slice(k * n_b, (k + 1) * n_b)
-        gnormed = mm(gpre, win_ref[rows, :], NT)
+        gnormed = mm(gpre, winp_ref[feats, :], NT)
         inter_ref[span, :] = rstd * (gnormed - mean1 - inter_ref[span, :] * mean2)
 
+    for q in range(4):
+        for d in range(1, n_p):
+            link(y_ref, x_ref, ysend, xrecv, q, (p + d) % n_p).wait_send()
     gw_ref[...] = jnp.zeros_like(gw_ref)
     ghl_ref[...] = jnp.zeros_like(ghl_ref)
 
@@ -248,9 +339,12 @@
 
         lax.fori_loop(0, tile, pair, 0, unroll=2)
         for part in range(3):
-            g_ref[:, pl.ds(pl.multiple_of(part * 64 + q * tile, tile), tile), :] = (
-                split_ref[part].reshape(n_f, tile, 128).astype(BF)
+            y_ref[q, :, :, :, part * tile : (part + 1) * tile, :] = (
+                split_ref[part].reshape(4, n_p, 2, tile, 128).astype(BF)
             )
+        for d in range(1, n_p):
+            link(y_ref, bk_ref, gsend, brecv, q, (p + d) % n_p).start()
+        bk_ref[q, :, p] = y_ref[q, :, p]
         return carry
 
     lax.fori_loop(0, 64 // tile, back_group, 0)
@@ -263,62 +357,98 @@
         lane < 64, second + pltpu.roll(second, 64, 1), 0.0
     )
 
+    acc_ref[...] = jnp.zeros_like(acc_ref)
+
+    def scatter(q, carry):
+        for d in range(1, n_p):
+            src = (p + n_p - d) % n_p
+            arrived(bk_ref.at[q, :, src], brecv.at[q, src])
+        for f in range(8):
+            hots, mains = [], []
+            rest = bk_ref[q, f // 2, :, f % 2, 2 * tile :, :].reshape(256, 128)
+            turned = pltpu.roll(rest.astype(F32), 64, 1).astype(BF)
+            for h, tail in ((0, rest), (1, turned)):
+                first = pl.multiple_of((q * 2 + h) * 256, 256)
+                row = lax.broadcasted_iota(jnp.int32, (rows, 256), 0)
+                at = 2 * (f % 2)
+                id0 = idz_ref[f // 2, at : at + 1, pl.ds(first, 256)]
+                id1 = idz_ref[f // 2, at + 1 : at + 2, pl.ds(first, 256)]
+                hot = jnp.where(row == id0, 1.0, 0.0) + jnp.where(row == id1, 1.0, 0.0)
+                hots.append(hot.astype(BF))
+                main = bk_ref[q, f // 2, :, f % 2, h * tile : (h + 1) * tile, :]
+                mains.append(jnp.concatenate([main.reshape(256, 128), tail], 1))
+            acc_ref[f] += mm(jnp.concatenate(hots, 1), jnp.concatenate(mains, 0))
+        return carry
+
+    lax.fori_loop(0, 4, scatter, 0)
+
+    def pack(f, carry):
+        part_ref[f, :rows, :] = acc_ref[f, :, :128]
+        low = acc_ref[f, : rows // 2, 128:]
+        high = pltpu.roll(acc_ref[f, rows // 2 :, 128:], 64, 1)
+        lane = lax.broadcasted_iota(jnp.int32, low.shape, 1)
+        part_ref[f, rows:, :] = jnp.where(lane < 64, low, high)
+        return carry
+
+    lax.fori_loop(0, 8, pack, 0)
+    for copy in sends:
+        copy.wait_send()
+    for q in range(4):
+        for d in range(1, n_p):
+            link(y_ref, bk_ref, gsend, brecv, q, (p + d) % n_p).wait_send()
+
 
 def whole(n):
     return [pl.BlockSpec(memory_space=pltpu.VMEM)] * n
 
 
-def lookup(ids, w1, w2, n_dest):
-    n_f = w1.shape[0]
+def run_main(scale, ids, tab, wt, win, wout, head, hpair, label):
+    rows = tab.shape[1] * 2 // 3
+    blocks = (4, 4, 16, 2, 48, 128)
+    dma = pltpu.SemaphoreType.DMA
     return pl.pallas_call(
-        lookup_kernel,
-        out_shape=jax.ShapeDtypeStruct((n_dest, n_f, 192, 128), BF),
-        in_specs=whole(3),
-        out_specs=whole(1)[0],
-        scratch_shapes=[pltpu.VMEM((ids.shape[1], ids.shape[0]), jnp.int32)],
-        compiler_params=pltpu.CompilerParams(vmem_limit_bytes=VMEM_LIMIT),
-        name="lookup",
-    )(ids, w1, w2)
-
-
-def scatter(ids, g, rows):
-    n_f = g.shape[1]
-    return pl.pallas_call(
-        scatter_kernel,
-        out_shape=jax.ShapeDtypeStruct((n_f, rows * 3 // 2, 128), F32),
-        in_specs=whole(2),
-        out_specs=whole(1)[0],
-        compiler_params=pltpu.CompilerParams(vmem_limit_bytes=VMEM_LIMIT),
-        name="table_grad",
-    )(ids, g)
-
-
-def dense(scale, x, wt, win, wout, head, hpair, label):
-    n_f = x.shape[0]
-    shapes = [
-        (x.shape, BF),
-        ((8, 128), F32),
-        ((DEN_ROWS, 128), F32),
-    ]
-    return pl.pallas_call(
-        functools.partial(dense_kernel, scale),
-        out_shape=[jax.ShapeDtypeStruct(*s) for s in shapes],
-        in_specs=whole(7),
+        functools.partial(main_kernel, scale),
+        out_shape=[
+            jax.ShapeDtypeStruct((8, rows * 3 // 2, 128), F32),
+            jax.ShapeDtypeStruct((DEN_ROWS, 128), F32),
+            jax.ShapeDtypeStruct((8, 128), F32),
+        ],
+        in_specs=whole(8),
         out_specs=whole(3),
         scratch_shapes=[
-            pltpu.VMEM((48, n_f), F32),
+            pltpu.VMEM((8, rows * 3 // 2, 128), BF),
+            pltpu.VMEM(ids.shape, jnp.int32),
+            pltpu.VMEM((2048, 32), jnp.int32),
+            pltpu.VMEM((8, rows, 256), BF),
+            pltpu.VMEM((8, rows, 256), BF),
+            pltpu.VMEM(blocks, BF),
+            pltpu.VMEM(blocks, BF),
+            pltpu.VMEM(blocks, BF),
+            pltpu.VMEM(win.shape, BF),
+            pltpu.VMEM((8, rows, 256), F32),
+            pltpu.VMEM((48, 128), F32),
             pltpu.VMEM((32, 384), F32),
-            pltpu.VMEM((3, n_f * 16, 128), F32),
-            pltpu.VMEM((64, n_f, 384), BF),
+            pltpu.VMEM((3, 128 * 16, 128), F32),
+            pltpu.VMEM((64, 128, 384), BF),
             pltpu.VMEM((64, 48, 384), F32),
-            pltpu.VMEM((16 * 128, n_f), F32),
-            pltpu.VMEM((128, 16 * n_f), BF),
+            pltpu.VMEM((16 * 128, 128), F32),
+            pltpu.VMEM((128, 16 * 128), BF),
             pltpu.VMEM((64, 384), F32),
             pltpu.VMEM((128, 128), F32),
+            dma((9,)),
+            dma((4,)),
+            dma((4,)),
+            dma((4,)),
+            dma((4, 16)),
+            dma((4, 16)),
+            dma((4, 16)),
+            dma((4, 16)),
         ],
-        compiler_params=pltpu.CompilerParams(vmem_limit_bytes=VMEM_LIMIT),
-        name="dense",
-    )(x, wt, win, wout, head, hpair, label)
+        compiler_params=pltpu.CompilerParams(
+            vmem_limit_bytes=VMEM_LIMIT, collective_id=1, has_side_effects=True
+        ),
+        name="main",
+    )(ids, tab, wt, win, wout, head, hpair, label)
 
 
 def reduce_kernel(
@@ -326,7 +456,12 @@
     den_ref,
     loss_ref,
     out_tab_ref,
-    out_den_ref,
+    gwin_ref,
+    gwout_ref,
+    gproj_ref,
+    gcomp_ref,
+    ghead_ref,
+    glin_ref,
     out_loss_ref,
     ta_ref,
     tb_ref,
@@ -393,9 +528,6 @@
         copy.start()
         sends.append(copy)
 
-    def arrived(dst, sem):
-        pltpu.make_async_copy(dst, dst, sem).wait()
-
     half = DEN_ROWS // 2
     for v in range(4):
         ta_ref[v] = tab_ref[2 * v + other].astype(BF)
@@ -497,14 +629,32 @@
         send(df_ref.at[c * n_p + q], df_ref.at[c * n_p + q], dh_sem.at[q], sibling)
     for q in range(n_p):
         arrived(df_ref.at[other * n_p + q], dh_sem.at[q])
-    for i in range(2 * n_p):
-        out_den_ref[i * chunk : (i + 1) * chunk, :] = df_ref[i].astype(F32)
+
+    def final(first, count):
+        pieces = []
+        at = first
+        while at < first + count:
+            i, r = at // chunk, at % chunk
+            n = min(chunk - r, first + count - at)
+            pieces.append(df_ref[i, r : r + n, :].astype(F32))
+            at += n
+        return pieces[0] if len(pieces) == 1 else jnp.concatenate(pieces, 0)
+
+    for side in range(2):
+        for k in range(16):
+            gwin_ref[side, pl.ds(k, 128, stride=16), :] = final(side * 2048 + k * 128, 128)
+    for i in range(6):
+        gwout_ref[:, i * 128 : (i + 1) * 128] = final(AT_WOUT + i * 256, 256)
+    gproj_ref[...] = final(AT_GW, 16).T
+    gcomp_ref[...] = final(AT_GW + 16, 32)
+    glin_ref[:, :128] = final(AT_LIN, 32)
+    glin_ref[:, 128:192] = final(AT_LIN + 32, 32)[:, :64]
+    ghead_ref[...] = final(AT_HEAD, 16)
     for copy in sends:
         copy.wait_send()
 
 
 def reduce_all(tab, den, loss, rows):
-    n_f = tab.shape[0]
     half = DEN_ROWS // 2
     chunk = half // 16
     dma = pltpu.SemaphoreType.DMA
@@ -512,11 +662,16 @@
         reduce_kernel,
         out_shape=[
             jax.ShapeDtypeStruct((2, rows, 192), F32),
-            jax.ShapeDtypeStruct(den.shape, F32),
+            jax.ShapeDtypeStruct((2, 2048, 128), F32),
+            jax.ShapeDtypeStruct((256, 768), F32),
+            jax.ShapeDtypeStruct((128, 16), F32),
+            jax.ShapeDtypeStruct((32, 128), F32),
+            jax.ShapeDtypeStruct((16, 128), F32),
+            jax.ShapeDtypeStruct((32, 192), F32),
             jax.ShapeDtypeStruct(loss.shape, F32),
         ],
         in_specs=whole(3),
-        out_specs=whole(3),
+        out_specs=whole(8),
         scratch_shapes=[
             pltpu.VMEM((4, 768, 128), BF),
             pltpu.VMEM((4, 768, 128), BF),
@@ -552,20 +707,19 @@
     )(tab, den, loss)
 
 
-def table_weights(t):
-    zeros = jnp.zeros(t.shape[:2] + (64,), t.dtype)
-    w1 = jnp.concatenate([t, zeros], 2)
-    w2 = jnp.concatenate([t[:, :, :128], zeros, t[:, :, 128:]], 2)
-    return w1, w2
-
-
-def order_ids(feature_ids, bag_lengths, n_zh, n_plane, rows):
+def pack_tables(t):
+    half = t.shape[1] // 2
+    rest = jnp.concatenate([t[:, :half, 128:], t[:, half:, 128:]], 2)
+    return jnp.concatenate([t[:, :, :128], rest], 1)
+
+
+def order_ids(feature_ids, bag_lengths, rows):
     ids = feature_ids[:, 0].transpose(1, 2, 0)
     lens = bag_lengths[:, 0].T
     slots = jnp.arange(ids.shape[1], dtype=jnp.int32)[None, :, None]
     ids = jnp.where(lens[:, None, :] > slots, ids, rows)
-    ids = ids.reshape(-1, n_zh, n_plane, 2, 64).transpose(1, 0, 3, 2, 4)
-    return ids.reshape(n_zh, -1, n_plane * 128)
+    ids = ids.reshape(4, 4, 16, 2, 4, 16).transpose(1, 0, 4, 3, 2, 5).reshape(4, 4, 2048)
+    return jnp.pad(ids, ((0, 0), (0, 4), (0, 0)))
 
 
 def pair_head(w_head, n_out):
@@ -576,58 +730,24 @@
 def per_device(
     feature_ids, bag_lengths, click_labels, tables, projection, compress, w_in, w_out, w_head
 ):
-    n_zh = lax.axis_size("zh")
-    n_plane = lax.axis_size("x") * lax.axis_size("y")
-    n_rep = lax.axis_size("zl") * lax.axis_size("c")
-    f_dev, rows, width = tables.shape
-    b_rep = feature_ids.shape[0]
-    n_feat, n_rank = projection.shape
-    n_lin = compress.shape[0]
+    rows = tables.shape[1]
     n_out = w_out.shape[1]
-    total = b_rep * n_rep
+    total = feature_ids.shape[0] * lax.axis_size("zl") * lax.axis_size("c")
     scale = 1.0 / math.sqrt(total)
-
-    ids = order_ids(feature_ids, bag_lengths, n_zh, n_plane, rows)
-    ids = lax.all_to_all(ids, "zh", split_axis=0, concat_axis=0, tiled=True)
-    ids = ids.reshape(-1, n_plane * 128)
-    all_tables = lax.all_gather(tables, "zh", axis=0, tiled=True)
-    w1, w2 = table_weights(all_tables)
-    y = lookup(ids, w1, w2, n_plane)
-    x = lax.all_to_all(y, ("x", "y"), split_axis=0, concat_axis=0, tiled=True)
-    x = x.reshape(n_feat, 192, 128)
-
-    def mix_order(a):
-        rest = a.shape[1:]
-        a = a.reshape((n_zh, n_plane, f_dev) + rest)
-        return jnp.swapaxes(a, 0, 1).reshape((n_feat,) + rest)
-
-    wt = jnp.concatenate([mix_order(projection), mix_order(compress.T)], 1).T
-    win = mix_order(w_in.reshape(n_feat, n_rank, -1)).transpose(1, 0, 2).reshape(w_in.shape)
+    ids = order_ids(feature_ids, bag_lengths, rows)
+    wt = jnp.concatenate([projection.T, compress], 0)
     head = w_head[:n_out].astype(F32)[None, :]
     hpair = pair_head(w_head, n_out)
     label = click_labels.astype(F32)
-    g, loss, den = dense(scale, x, wt, win, w_out, head, hpair, label)
-    back = lax.all_to_all(
-        g.reshape(y.shape), ("x", "y"), split_axis=0, concat_axis=0, tiled=True
+    partial, den, loss = run_main(
+        scale, ids, pack_tables(tables), wt, w_in, w_out, head, hpair, label
     )
-    partial = scatter(ids, back, rows)
-    table_grad, den, loss = reduce_all(partial, den, loss, rows)
-    loss = loss[0, 0]
-    gwin = jnp.concatenate([den[:2048], den[2048:4096]], 1)
-    gwout = den[AT_WOUT:AT_GW].reshape(-1, 256, 128).transpose(1, 0, 2).reshape(w_out.shape)
-    gw = den[AT_GW:AT_LIN]
-    lin = den[AT_LIN:AT_HEAD].reshape(2, n_lin, 128)
-    lin = jnp.concatenate([lin[0], lin[1, :, :64]], 1)
-    ghead = jnp.concatenate([den[AT_HEAD : AT_HEAD + n_out // 128].reshape(-1), lin.reshape(-1)])
-
-    def natural(a):
-        rest = a.shape[1:]
-        a = a.reshape((n_plane, n_zh, f_dev) + rest)
-        return jnp.swapaxes(a, 0, 1).reshape((n_feat,) + rest)
-
-    gw = natural(gw.T)
-    gwin = natural(gwin.reshape(n_rank, n_feat, -1).transpose(1, 0, 2)).reshape(w_in.shape)
-    return (loss / total, gw[:, :n_rank], gw[:, n_rank:].T, gwin, gwout, ghead, table_grad)
+    table_grad, gwin, gwout, gproj, gcomp, ghead, glin, loss = reduce_all(
+        partial, den, loss, rows
+    )
+    gwin = jnp.concatenate([gwin[0], gwin[1]], 1)
+    ghead = jnp.concatenate([ghead[: n_out // 128].reshape(-1), glin.reshape(-1)])
+    return (loss[0, 0] / total, gproj, gcomp, gwin, gwout, ghead, table_grad)
 
 
 def solution(mesh):

time: 417 us -> 319 us (0.76)
  Pallas kernels: 133 us -> 292 us
  waiting for transfers between devices: 132 us -> 0 us
  blocking collectives: 83 us -> 0 us
  starting transfers between devices: 15.8 us -> 0 us
  local copies, waits for them, and re-layouts: 30.5 us -> 15.7 us
  between operations: 16 us -> 2.5 us
    pallas_call x3 -> x1, Pallas kernels: 72.9 us -> 229 us  [run_main(): pl.pallas_call(functools.partial(main_kernel, scale), out_shape=[jax.Shap...]
    all_to_all x2 -> x0, waiting for transfers between devices: 101 us -> none  [the longest x1 94.2 us: per_device(): x = lax.all_to_all(y, ('x', 'y'), split_axis=0, concat_axis=0, tiled=True)]
    all_to_all x1 -> x0, blocking collectives: 83 us -> none  [per_device(): lax.all_to_all(g.reshape(y.shape), ('x', 'y'), split_axis=0, concat_axis=...]
    all_gather x1 -> x0, waiting for transfers between devices: 29.8 us -> none  [per_device(): all_tables = lax.all_gather(tables, 'zh', axis=0, tiled=True)]
    all_to_all x2 -> x0, starting transfers between devices: 15.7 us -> none  [the longest x1 9.01 us: per_device(): ids = lax.all_to_all(ids, 'zh', split_axis=0, concat_axis=0, tiled=True)]
    reshape x11 -> x5, local copies, waits for them, and re-layouts: 10.6 us -> 3.02 us  [the longest x3 1.5 us: order_ids(): ids.reshape(4, 4, 16, 2, 4, 16).transpose(1, 0, 4, 3, 2, 5)]
    slice x7 -> x3, local copies, waits for them, and re-layouts: 7.82 us -> 3.06 us  [the longest x1 1.19 us: per_device(): return (loss[0, 0] / total, gproj, gcomp, gwin, gwout, ghead, table_grad)]
  transfers between devices with their start and end apart: 3 -> 0, of which waited for: 3 -> 0; matrix products, arithmetic and copies ran while one was open for 2% -> 0% of each run, Pallas kernels for 0% -> 0%
where the time goes in v3:
time: 319 us; the launch traced here: 318 us
  Pallas kernels  292 us (92%)
  local copies, waits for them, and re-layouts  15.7 us (5%)
  other arithmetic  8 us (3%)
    pallas_call x1, Pallas kernels, run_main(): pl.pallas_call(functools.partial(main_kernel, scale), out_shape=[jax.Shap...  229 us
    pallas_call x1, Pallas kernels, reduce_all(): pl.pallas_call(reduce_kernel, out_shape=[jax.ShapeDtypeStruct((2, rows, 1...  62.6 us

profile of v3, /device:TPU:1, one launch (start us, length us, event | category | flops | bytes accessed | tf_op | source)
XLA Modules:
  0.0 317.9 jit_solution(17151704877111476416)
XLA Ops:
  0.6 0.7 convert_element_type.13
  1.3 0.7 slice_convert_fusion.1
  2.0 0.6 reshape.44.head_ref
  2.6 1.3 pad_maximum_fusion.3.wt_ref
  3.9 0.7 slice_convert_fusion
  4.6 0.1 reshape.45
  4.7 0.7 pad_maximum_fusion.1.hpair_ref
  5.4 0.7 copy.27.label_ref
  6.1 1.0 compare_select_fusion
  7.1 0.9 fusion
  8.0 0.1 copy.31
  8.1 0.1 copy.32
  8.3 1.0 slice.41
  9.2 0.2 copy.30
  9.4 0.9 maximum_maximum_fusion.tab_ref
  10.3 0.8 reshape.40
  11.0 0.2 copy.34
  11.2 0.6 reshape.41
  11.8 0.7 pad.4.ids_ref
  12.5 229.1 %main.1 = (f32[8,768,128]{2,1,0:T(8,128)}, f32[6144,128]{1,0:T(8,128)}, f32[8,128]{1,0:T(8,128)}) custom-call(s32[4,8,2048]{2,1,0:T(8,128)} %pad.4.ids_ref, bf16[2,768,128]{2,1,0:T(8,128)(2,1)} %maximum_maximum_fusion.tab_ref, bf16[48,128]{1,0:T(8,128)(2,1)} %pad_maximum_fusion.3.wt_ref, bf16[2048,256]{1,0:T(8,128)(2,1)} %win_ref.1, ...), custom_call_target="tpu_custom_call" | custom-call | tf_op jit(solution)/shard_map/main/pallas_call | solution.py:409
  241.6 62.6 %reduce.1 = (f32[2,512,192]{2,1,0:T(8,128)}, f32[2,2048,128]{2,1,0:T(8,128)}, f32[256,768]{1,0:T(8,128)}, f32[128,16]{1,0:T(8,128)}, f32[32,128]{1,0:T(8,128)}, ...) custom-call(f32[8,768,128]{2,1,0:T(8,128)} %get-tuple-element.18.tab_ref, ...), custom_call_target="tpu_custom_call" | custom-call | tf_op jit(solution)/shard_map/reduce/pallas_call | solution.py:661
  304.3 1.2 slice.48
  306.1 0.7 slice_bitcast_fusion.2
  306.8 1.5 copy.28
  308.3 0.8 reshape.43
  309.1 0.6 pad_maximum_fusion.2
  309.7 2.4 copy.29
  312.2 1.7 slice_bitcast_fusion.1
  313.8 0.0 copy-start.1
  313.9 0.0 copy-start
  313.9 1.5 pad_maximum_fusion
  315.3 0.0 copy-done.1
  315.3 0.6 copy.37
  315.9 0.0 copy-done
  315.9 0.9 copy.38
  (2 shorter events, 0.0 us)
Async XLA Ops:
  313.8 1.5 copy-start.1
  313.9 2.1 copy-start

commit v4 on v1

v4 whole, which is shorter than its diff:
```python
import functools
import math

import jax
import jax.numpy as jnp
import numpy as np
from jax import lax
from jax.experimental import pallas as pl
from jax.experimental.pallas import tpu as pltpu
from jax.sharding import Mesh, PartitionSpec as P

EPS = 1e-05
BF = jnp.bfloat16
F32 = jnp.float32
NT = (((1,), (1,)), ((), ()))
TN = (((0,), (0,)), ((), ()))
VMEM_LIMIT = 60 * 1024 * 1024
MESH = pl.DeviceIdType.MESH
AT_WOUT = 4096
AT_GW = AT_WOUT + 1536
AT_LIN = AT_GW + 48
AT_HEAD = AT_LIN + 64
DEN_ROWS = 6144


def mm(a, b, dims=None):
    if dims is None:
        return jnp.dot(a, b, preferred_element_type=F32)
    return lax.dot_general(a, b, dims, preferred_element_type=F32)


def arrived(dst, sem):
    pltpu.make_async_copy(dst, dst, sem).wait()


def step_kernel(
    scale,
    ids_ref,
    tab_ref,
    perm_ref,
    wtn_ref,
    win_ref,
    wout_ref,
    head_ref,
    hpair_ref,
    label_ref,
    out_tab_ref,
    gwin_ref,
    gwout_ref,
    gproj_ref,
    gcomp_ref,
    ghead_ref,
    glin_ref,
    out_loss_ref,
    tz_ref,
    idt_ref,
    col_ref,
    y_ref,
    x_ref,
    winp_ref,
    den_ref,
    gw_ref,
    split_ref,
    xp_ref,
    mix_ref,
    inter_ref,
    nb_ref,
    ld_ref,
    slope_ref,
    da_ref,
    db_ref,
    dc_ref,
    dd_ref,
    de_ref,
    df_ref,
    te_ref,
    tf_ref,
    tr_ref,
    sa_ref,
    sb_ref,
    sp_ref,
    sz_ref,
    asend,
    arecv,
    irecv,
    ysend,
    xrecv,
    gsend,
    grecv,
    free_sem,
    core_sem,
    dsend,
    dp_sem,
    dz_sem,
    dg_sem,
    dh_sem,
    t1send,
    t1recv,
    t2send,
    t2recv,
    t3send,
    t3recv,
    t4send,
    t4recv,
    ssend,
    sc_sem,
    sp_sem,
    sz_sem,
):
    zh, px, py, zl, c = [lax.axis_index(name) for name in ("zh", "x", "y", "zl", "c")]
    n_p, n_z = 16, 8
    z = zh * 2 + zl
    p = px * 4 + py
    other = 1 - c
    sibling = (zh, px, py, zl, other)
    n_f, n_b, n_k, tile = 128, 128, 16, 16
    rows = 512
    low, high, rest_rows = slice(0, 256), slice(256, 512), slice(512, 768)
    width = n_k * n_f
    half = DEN_ROWS // 2
    chunk = half // n_p
    o = py * other + px * c
    o_other = px * other + py * c

    def at_plane(q):
        return (zh, q // 4, q % 4, zl, c)

    def at_z(v):
        return (v // 2, px, py, v % 2, c)

    def along(d):
        return (zh, (px + d * c) % 4, (py + d * other) % 4, zl, c)

    def in_row(s, d):
        if s == 0:
            return (px + d) % 4, (zh, (px + d) % 4, py, zl, c)
        return (py + d) % 4, (zh, px, (py + d) % 4, zl, c)

    def remote(src, dst, send_sem, recv_sem, device):
        return pltpu.make_async_remote_copy(
            src_ref=src,
            dst_ref=dst,
            send_sem=send_sem,
            recv_sem=recv_sem,
            device_id=device,
            device_id_type=MESH,
        )

    barrier = pltpu.get_barrier_semaphore()
    partners = [sibling, (zh, px, py, 1 - zl, other)]
    partners += [at_plane((p + d) % n_p) for d in range(1, n_p)]
    partners += [at_z((z + d) % n_z) for d in range(1, n_z)]
    for dz in range(1, 4):
        for d in range(1, 4):
            partners.append(((zh + dz) % 4, px, (py + d) % 4, zl, c))
            partners.append(((zh + dz) % 4, (px + d) % 4, py, zl, c))
    for device in partners:
        pl.semaphore_signal(barrier, inc=1, device_id=device, device_id_type=MESH)
    pl.semaphore_wait(barrier, len(partners))

    sends = []

    def send(src, dst, sem, device):
        copy = remote(src, dst, asend.at[len(sends)], sem, device)
        copy.start()
        sends.append(copy)

    def send_table(at, device):
        send(tz_ref.at[at], tz_ref.at[at], arecv.at[at], device)

    mine = c * 16 + zh * 4 + o
    tz_ref[mine] = tab_ref[c]
    tz_ref[other * 16 + zh * 4 + o_other] = tab_ref[other]
    near = (zh + 3 + 2 * zl) % 4
    for to, lo in ((near, 0), (near, 1), ((zh + 2) % 4, 1 - zl)):
        send_table(mine, (to, px, py, lo, c))
    for d in range(1, 4):
        send_table(mine, along(d))
    for dz in range(4):
        for d in range(4):
            if dz == 0 and d == 0:
                continue
            to = (zh + dz) % 4
            ty, tx = (py + d) % 4, (px + d) % 4
            send(
                ids_ref.at[0, to * 4 + ty],
                idt_ref.at[0, zh * 4 + py],
                irecv.at[0, zh * 4 + py],
                (to, px, ty, zl, c),
            )
            send(
                ids_ref.at[1, to * 4 + tx],
                idt_ref.at[1, zh * 4 + px],
                irecv.at[1, zh * 4 + px],
                (to, tx, py, zl, c),
            )
    idt_ref[0, zh * 4 + py] = ids_ref[0, zh * 4 + py]
    idt_ref[1, zh * 4 + px] = ids_ref[1, zh * 4 + px]
    for dz in (1, 3, 2):
        at = c * 16 + (zh + dz) % 4 * 4 + o
        arrived(tz_ref.at[at], arecv.at[at])
        for d in range(1, 4):
            send_table(at, along(d))
        send_table(at, sibling)

    perm = perm_ref[...]
    wt = mm(wtn_ref[...], perm).astype(BF)
    for side in range(2):
        cols = slice(side * 128, (side + 1) * 128)
        split_ref[side] = win_ref[:, cols].astype(F32)
        for k in range(n_k):
            block = split_ref[side, pl.ds(k, n_f, stride=n_k), :].astype(BF)
            winp_ref[k * n_f : (k + 1) * n_f, cols] = mm(perm, block, TN).astype(BF)

    for dz in (0, 1, 3, 2):
        for d in (1, 3, 2):
            at = c * 16 + (zh + dz) % 4 * 4 + (o + d) % 4
            arrived(tz_ref.at[at], arecv.at[at])
            send_table(at, sibling)
    for dz in range(4):
        for d in range(4):
            if dz == 0 and d == 0:
                continue
            v = (zh + dz) % 4 * 4
            for s, own in ((0, py), (1, px)):
                at = v + (own + d) % 4
                arrived(idt_ref.at[s, at], irecv.at[s, at])
    for s in range(2):
        col_ref[s] = idt_ref[s].reshape(128, 128).T
    for dz in (0, 1, 3, 2):
        for d in range(4):
            if dz == 0 and d == 0:
                continue
            at = other * 16 + (zh + dz) % 4 * 4 + (o_other + d) % 4
            arrived(tz_ref.at[at], arecv.at[at])

    def row_copy(q, s, d, send_sems, recv_sems):
        to, device = in_row(s, d)
        here = py if s else px
        return remote(
            y_ref.at[q, s, to],
            x_ref.at[q, s, here],
            send_sems.at[q, s, to],
            recv_sems.at[q, s, here],
            device,
        )

    def keep_own(q):
        x_ref[q, 0, px] = y_ref[q, 0, px]
        x_ref[q, 1, py] = y_ref[q, 1, py]

    def row_arrived(q, recv_sems):
        for s in range(2):
            for d in (1, 3, 2):
                src = in_row(s, d)[0]
                arrived(x_ref.at[q, s, src], recv_sems.at[q, s, src])

    def lookup(q, carry):
        def one_set(s, inner):
            cols = col_ref[s, pl.ds(pl.multiple_of(q * 32, 32), 32), :]
            lane = lax.broadcasted_iota(jnp.int32, (128, rows), 1)
            first = lax.broadcasted_iota(jnp.int32, (4, tile, 128), 2) < 64
            for i in range(16):
                hot = jnp.zeros((128, rows), F32)
                for slot in range(2):
                    at = i * 8 + slot * 4
                    ids = jnp.concatenate([cols[:, at + k : at + k + 1] for k in range(4)], 0)
                    hot = hot + jnp.where(lane == ids, 1.0, 0.0)
                hot = hot.astype(BF)
                f = s * 16 + i
                rest = tz_ref[f, rest_rows, :]
                one = mm(hot[:, low], jnp.concatenate([tz_ref[f, low, :], rest], 1))
                two = mm(hot[:, high], jnp.concatenate([tz_ref[f, high, :], rest], 1))
                main = one[:, :128] + two[:, :128]
                y_ref[q, s, :, i, : 2 * tile, :] = main.astype(BF).reshape(4, 2 * tile, 128)
                one, two = [v[:, 128:].reshape(4, 2, tile, 128) for v in (one, two)]

                def turn(v):
                    return pltpu.roll(v.reshape(64, 128), 64, 1).reshape(4, tile, 128)

                tail = jnp.where(
                    first, one[:, 0] + turn(two[:, 0]), turn(one[:, 1]) + two[:, 1]
                )
                y_ref[q, s, :, i, 2 * tile :, :] = tail.astype(BF)
            return inner

        lax.fori_loop(0, 2, one_set, 0)
        for d in (1, 3, 2):
            for s in range(2):
                row_copy(q, s, d, ysend, xrecv).start()
        keep_own(q)
        return carry

    lax.fori_loop(0, 4, lookup, 0)
    for copy in sends:
        copy.wait_send()

    lane1 = lax.broadcasted_iota(jnp.int32, (n_k, 384), 1) < 192
    row_lane1 = lax.broadcasted_iota(jnp.int32, (1, 384), 1) < 192

    def load_group(q, carry):
        row_arrived(q, xrecv)
        for part in range(3):
            block = x_ref[q, :, :, :, part * tile : (part + 1) * tile, :]
            split_ref[part] = block.astype(F32).reshape(n_f * tile, 128)

        def pair(j, inner):
            p = q * tile + j
            pieces = [
                split_ref[part, pl.ds(j, n_f, stride=tile), :].astype(BF) for part in (0, 2, 1)
            ]
            x3 = jnp.concatenate(pieces, 1)
            for part in range(3):
                first = pl.multiple_of(p % 2 * 384 + part * 128, 128)
                xp_ref[p // 2, pl.ds(first, 128), :] = pieces[part]
            mixed = mm(wt, x3)
            mix_ref[p] = mixed
            compact = mixed[:n_k]
            stacked = jnp.concatenate(
                [jnp.where(lane1, compact, 0.0), jnp.where(lane1, 0.0, compact)], 0
            ).astype(BF)
            inter = mm(stacked, x3, NT)
            inter_ref[pl.ds(p, n_k, stride=n_b), :] = inter[:n_k]
            inter_ref[pl.ds(64 + p, n_k, stride=n_b), :] = inter[n_k:]
            ld_ref[pl.ds(p, 1), :] = jnp.sum(mixed[n_k:] * hpair_ref[...], 0, keepdims=True)
            return inner

        lax.fori_loop(0, tile, pair, 0, unroll=2)
        return carry

    lax.fori_loop(0, 64 // tile, load_group, 0)

    for s in range(2):
        for d in range(1, 4):
            pl.semaphore_signal(
                free_sem, inc=1, device_id=in_row(s, d)[1], device_id_type=MESH
            )

    total = jnp.zeros((n_b, n_f), F32)
    for k in range(n_k):
        total = total + inter_ref[k * n_b : (k + 1) * n_b, :]
    center = jnp.sum(total, 1, keepdims=True) / width
    total = jnp.zeros((n_b, n_f), F32)
    for k in range(n_k):
        shifted = inter_ref[k * n_b : (k + 1) * n_b, :] - center
        total = total + shifted * shifted
    rstd = lax.rsqrt(jnp.sum(total, 1, keepdims=True) / width + EPS)
    for k in range(n_k):
        normed = (inter_ref[k * n_b : (k + 1) * n_b, :] - center) * rstd
        inter_ref[k * n_b : (k + 1) * n_b, :] = normed
        nb_ref[:, k * n_f : (k + 1) * n_f] = normed.astype(BF)
    pre_act = mm(nb_ref[...], winp_ref[...])
    sigma = 1.0 / (1.0 + jnp.exp(-pre_act))
    hidden = (pre_act * sigma).astype(BF)
    factor = mm(hidden, wout_ref[...])
    head = head_ref[...]
    lin = ld_ref[...]
    lin1 = jnp.sum(jnp.where(row_lane1, lin, 0.0), 1, keepdims=True)
    lin2 = jnp.sum(jnp.where(row_lane1, 0.0, lin), 1, keepdims=True)
    logit = jnp.sum(factor * head, 1, keepdims=True) + jnp.concatenate([lin1, lin2], 0)
    target = label_ref[...]
    terms = jnp.maximum(logit, 0.0) + jnp.log1p(jnp.exp(-jnp.abs(logit))) - target * logit
    sa_ref[48:, :] = jnp.broadcast_to(
        jnp.sum(jnp.broadcast_to(terms, (n_b, 128)), 0, keepdims=True), (8, 128)
    )
    slope = scale * (1.0 / (1.0 + jnp.exp(-logit)) - target)
    slope_ref[...] = jnp.broadcast_to(slope, (n_b, 128))
    den_ref[AT_HEAD:, :] = jnp.zeros((den_ref.shape[0] - AT_HEAD, 128), F32)
    ghead = jnp.sum(slope * factor, 0, keepdims=True)
    for i in range(ghead.shape[1] // 128):
        den_ref[AT_HEAD + i : AT_HEAD + i + 1, :] = ghead[:, i * 128 : (i + 1) * 128]
    gfactor = (slope * head).astype(BF)
    for i in range(gfactor.shape[1] // 128):
        den_ref[AT_WOUT + i * 256 : AT_WOUT + (i + 1) * 256, :] = mm(
            hidden, gfactor[:, i * 128 : (i + 1) * 128], TN
        )
    ghidden = mm(gfactor, wout_ref[...], NT)
    gpre = (ghidden * sigma * (1.0 + pre_act * (1.0 - sigma))).astype(BF)
    first = jnp.zeros((n_b, n_f), F32)
    second = jnp.zeros((n_b, n_f), F32)
    for k in range(n_k):
        feats = slice(k * n_f, (k + 1) * n_f)
        gwin = mm(nb_ref[:, feats], gpre, TN)
        den_ref[feats, :] = gwin[:, :128]
        den_ref[width + k * n_f : width + (k + 1) * n_f, :] = gwin[:, 128:]
        gnormed = mm(gpre, winp_ref[feats, :], NT)
        first = first + gnormed
        second = second + gnormed * inter_ref[k * n_b : (k + 1) * n_b, :]
    mean1 = jnp.sum(first, 1, keepdims=True) / width
    mean2 = jnp.sum(second, 1, keepdims=True) / width
    for k in range(n_k):
        feats = slice(k * n_f, (k + 1) * n_f)
        span = slice(k * n_b, (k + 1) * n_b)
        gnormed = mm(gpre, winp_ref[feats, :], NT)
        inter_ref[span, :] = rstd * (gnormed - mean1 - inter_ref[span, :] * mean2)

    def slope_row(p):
        s1 = slope_ref[pl.ds(p, 1), :]
        s2 = slope_ref[pl.ds(64 + p, 1), :]
        return jnp.where(
            row_lane1,
            jnp.concatenate([s1, s1, s1], 1),
            jnp.concatenate([s2, s2, s2], 1),
        )

    ghl = lax.fori_loop(
        0,
        64,
        lambda p, sum: sum + slope_row(p) * mix_ref[p, n_k:, :],
        jnp.zeros((32, 384), F32),
        unroll=4,
    )
    second = ghl[:, 128:256]
    lane = lax.broadcasted_iota(jnp.int32, second.shape, 1)
    den_ref[AT_LIN : AT_LIN + 32, :] = ghl[:, :128] + ghl[:, 256:]
    den_ref[AT_LIN + 32 : AT_LIN + 64, :] = jnp.where(
        lane < 64, second + pltpu.roll(second, 64, 1), 0.0
    )
    den_ref[AT_GW:AT_LIN, :] = jnp.zeros((AT_LIN - AT_GW, 128), F32)
    gw_ref[...] = jnp.zeros_like(gw_ref)

    def dense_core():
        return remote(da_ref, db_ref, dsend.at[0], core_sem, sibling)

    def dense_plane(d):
        to = (p + d) % n_p
        return remote(
            dc_ref.at[to], dd_ref.at[p], dsend.at[d], dp_sem.at[p], at_plane(to)
        )

    def dense_z(d):
        return remote(
            de_ref.at[z], de_ref.at[z], dsend.at[15 + d], dz_sem.at[z], at_z((z + d) % n_z)
        )

    def dense_gather(d):
        at = c * n_p + p
        return remote(
            df_ref.at[at],
            df_ref.at[at],
            dsend.at[22 + d],
            dg_sem.at[p],
            at_plane((p + d) % n_p),
        )

    def dense_last(d):
        q = (p + d) % n_p
        at = c * n_p + q
        return remote(df_ref.at[at], df_ref.at[at], dsend.at[38 + d], dh_sem.at[q], sibling)

    def dense_step1():
        arrived(db_ref, core_sem)

        def add(i, carry):
            at = pl.multiple_of(i * chunk, chunk)
            mine = den_ref[pl.ds(pl.multiple_of(c * half + i * chunk, chunk), chunk), :]
            dc_ref[i] = (mine + db_ref[pl.ds(at, chunk), :].astype(F32)).astype(BF)
            return carry

        lax.fori_loop(0, n_p, add, 0)
        for d in range(1, n_p):
            dense_plane(d).start()

    def dense_step2():
        own = dc_ref[p].astype(F32)
        for d in range(1, n_p):
            q = (p + d) % n_p
            arrived(dd_ref.at[q], dp_sem.at[q])
            own = own + dd_ref[q].astype(F32)
        de_ref[z] = own.astype(BF)
        for d in range(1, n_z):
            dense_z(d).start()

    def dense_step3():
        for d in range(1, n_z):
            v = (z + d) % n_z
            arrived(de_ref.at[v], dz_sem.at[v])
        own = de_ref[0].astype(F32)
        for v in range(1, n_z):
            own = own + de_ref[v].astype(F32)
        df_ref[c * n_p + p] = own.astype(BF)
        for d in range(1, n_p):
            dense_gather(d).start()
        dense_last(0).start()

    da_ref[...] = den_ref[pl.ds(pl.multiple_of(other * half, half), half), :].astype(BF)
    dense_core().start()
    for q in range(4):
        for s in range(2):
            for d in range(1, 4):
                row_copy(q, s, d, ysend, xrecv).wait_send()
    pl.semaphore_wait(free_sem, 6)

    def back_group(q, carry):
        pl.when(q == 1)(dense_step1)
        pl.when(q == 2)(dense_step2)
        pl.when(q == 3)(dense_step3)

        def pair(j, inner):
            p = q * tile + j
            x3 = jnp.concatenate(
                [
                    xp_ref[p // 2, pl.ds(pl.multiple_of(p % 2 * 384 + part * 128, 128), 128), :]
                    for part in range(3)
                ],
                1,
            )
            gi = jnp.concatenate(
                [
                    inter_ref[pl.ds(p, n_k, stride=n_b), :],
                    inter_ref[pl.ds(64 + p, n_k, stride=n_b), :],
                ],
                0,
            ).astype(BF)
            gc = mm(gi, x3)
            gc = jnp.where(lane1, gc[:n_k], gc[n_k:]).astype(BF)
            srow = slope_row(p)
            gl = (srow * hpair_ref[...]).astype(BF)
            compact = mix_ref[p, :n_k, :]
            tail = jnp.concatenate([gc, gl], 0)
            right = jnp.concatenate(
                [
                    jnp.where(lane1, compact, 0.0).astype(BF),
                    jnp.where(lane1, 0.0, compact).astype(BF),
                    tail,
                ],
                0,
            )
            left = jnp.concatenate([gi, wt], 0)
            gp = mm(left, right, TN)
            gw_ref[...] += mm(tail, x3, NT)
            for part, at in ((0, 0), (2, 128), (1, 256)):
                split_ref[part, pl.ds(j, n_f, stride=tile), :] = gp[:, at : at + 128]
            return inner

        lax.fori_loop(0, tile, pair, 0, unroll=2)
        for part in range(3):
            y_ref[q, :, :, :, part * tile : (part + 1) * tile, :] = (
                split_ref[part].reshape(2, 4, 16, tile, 128).astype(BF)
            )
        for d in (1, 3, 2):
            for s in range(2):
                row_copy(q, s, d, gsend, grecv).start()
        keep_own(q)
        return carry

    lax.fori_loop(0, 64 // tile, back_group, 0)

    def small_core():
        return remote(sa_ref, sb_ref, ssend.at[0], sc_sem, sibling)

    def small_plane(d):
        return remote(
            sp_ref.at[p], sp_ref.at[p], ssend.at[d], sp_sem.at[p], at_plane((p + d) % n_p)
        )

    def small_z(d):
        return remote(
            sz_ref.at[z], sz_ref.at[z], ssend.at[15 + d], sz_sem.at[z], at_z((z + d) % n_z)
        )

    sa_ref[:48, :] = gw_ref[...]
    small_core().start()

    def table_grad(s, i):
        hots, mains, rests = [], [], []
        row = lax.broadcasted_iota(jnp.int32, (rows, 128), 0)
        for src in range(4):
            hot = jnp.zeros((rows, 128), F32)
            for slot in range(2):
                ids = idt_ref[s, i, slot * 4 + src : slot * 4 + src + 1, :]
                hot = hot + jnp.where(row == ids, 1.0, 0.0)
            hots.append(hot.astype(BF))
            for q in range(4):
                mains.append(x_ref[q, s, src, i, : 2 * tile, :])
                rests.append(x_ref[q, s, src, i, 2 * tile :, :])
        turned = pltpu.roll(jnp.concatenate(rests, 0).astype(F32), 64, 1).astype(BF)
        tails = []
        for k, rest in enumerate(rests):
            tails += [rest, turned[k * tile : (k + 1) * tile]]
        right = jnp.concatenate([jnp.concatenate(mains, 0), jnp.concatenate(tails, 0)], 1)
        sums = mm(jnp.concatenate(hots, 1), right)
        lane = lax.broadcasted_iota(jnp.int32, (256, 128), 1)
        tail = jnp.where(lane < 64, sums[low, 128:], pltpu.roll(sums[high, 128:], 64, 1))
        return sums[:, :128], tail

    def table_core(i):
        return remote(
            tz_ref.at[16 + i], tz_ref.at[i], t1send.at[i], t1recv.at[i], sibling
        )

    def table_along(d, v):
        return remote(
            xp_ref.at[v * 4 + (o + d) % 4],
            xp_ref.at[16 + o * 4 + v],
            t2send.at[d * 4 + v],
            t2recv.at[o * 4 + v],
            along(d),
        )

    def table_z(d):
        to = (z + d) % n_z
        return remote(te_ref.at[to], tf_ref.at[z], t3send.at[d], t3recv.at[z], at_z(to))

    own_slot = 2 * c + zl

    def table_replica(k):
        device = (sibling, (zh, px, py, 1 - zl, c), (zh, px, py, 1 - zl, other))[k]
        return remote(
            tr_ref.at[own_slot], tr_ref.at[own_slot], t4send.at[k], t4recv.at[own_slot], device
        )

    for q in range(4):
        row_arrived(q, grecv)

    def for_sibling(n, carry):
        i = (n % 4) * 4 + (o_other + 1 + n // 4) % 4
        main, tail = table_grad(other, i)
        tz_ref[16 + i, :rows, :] = main.astype(BF)
        tz_ref[16 + i, rest_rows, :] = tail.astype(BF)
        table_core(i).start()
        return carry

    lax.fori_loop(0, 16, for_sibling, 0)

    arrived(sb_ref, sc_sem)
    sp_ref[p] = sa_ref[...] + sb_ref[...]
    for d in range(1, n_p):
        small_plane(d).start()

    def for_chip(n, carry):
        d, v = n // 4 + 1, n % 4
        i = v * 4 + (o + d) % 4
        main, tail = table_grad(c, i)
        arrived(tz_ref.at[i], t1recv.at[i])
        xp_ref[i, :rows, :] = (main + tz_ref[i, :rows, :].astype(F32)).astype(BF)
        xp_ref[i, rest_rows, :] = (tail + tz_ref[i, rest_rows, :].astype(F32)).astype(BF)

        @pl.when(d < 4)
        def _():
            table_along(d, v).start()

        return carry

    lax.fori_loop(0, 16, for_chip, 0)

    for d in range(1, n_p):
        q = (p + d) % n_p
        arrived(df_ref.at[c * n_p + q], dg_sem.at[q])
        dense_last(d).start()
    for d in range(1, n_p):
        q = (p + d) % n_p
        arrived(sp_ref.at[q], sp_sem.at[q])
    small = sp_ref[0]
    for q in range(1, n_p):
        small = small + sp_ref[q]
    sz_ref[z] = small
    for d in range(1, n_z):
        small_z(d).start()

    for d in range(1, 4):
        for v in range(4):
            at = (o + d) % 4 * 4 + v
            arrived(xp_ref.at[16 + at], t2recv.at[at])
    own = None
    for d in (1, 7, 2, 6, 3, 5, 4, 0):
        to = (z + d) % n_z
        span = pl.ds(pl.multiple_of(to % 2 * 384, 384), 384)
        own = xp_ref[to // 2 * 4 + o, span, :].astype(F32)
        for k in range(1, 4):
            own = own + xp_ref[16 + (o + k) % 4 * 4 + to // 2, span, :].astype(F32)
        if d > 0:
            te_ref[to] = own.astype(BF)
            table_z(d).start()

    for q in range(n_p):
        arrived(df_ref.at[other * n_p + q], dh_sem.at[q])

    def final(first, count):
        pieces = []
        at = first
        while at < first + count:
            i, r = at // chunk, at % chunk
            n = min(chunk - r, first + count - at)
            pieces.append(df_ref[i, r : r + n, :])
            at += n
        return pieces[0] if len(pieces) == 1 else jnp.concatenate(pieces, 0)

    for side in range(2):
        for k in range(n_k):
            block = final(side * 2048 + k * 128, 128)
            gwin_ref[side, pl.ds(k, n_f, stride=n_k), :] = mm(perm, block)
    for i in range(6):
        gwout_ref[:, i * 128 : (i + 1) * 128] = final(AT_WOUT + i * 256, 256).astype(F32)
    glin_ref[:, :128] = final(AT_LIN, 32).astype(F32)
    glin_ref[:, 128:192] = final(AT_LIN + 32, 32).astype(F32)[:, :64]
    ghead_ref[...] = final(AT_HEAD, 16).astype(F32)

    for d in range(1, n_z):
        v = (z + d) % n_z
        arrived(tf_ref.at[v], t3recv.at[v])
        own = own + tf_ref[v].astype(F32)
    tr_ref[own_slot] = own.astype(BF)
    for k in range(3):
        table_replica(k).start()

    for d in range(1, n_z):
        v = (z + d) % n_z
        arrived(sz_ref.at[v], sz_sem.at[v])
    small = sz_ref[0]
    for v in range(1, n_z):
        small = small + sz_ref[v]
    out_loss_ref[...] = small[48:]
    natural = lax.dot_general(
        small[:48],
        perm.astype(F32),
        NT,
        precision=lax.Precision.HIGHEST,
        preferred_element_type=F32,
    )
    gproj_ref[...] = natural[:n_k].T
    gcomp_ref[...] = natural[n_k:]

    for d in range(1, 4):
        k = (own_slot + d) % 4
        arrived(tr_ref.at[k], t4recv.at[k])
    for j in range(2):
        first, second = tr_ref[2 * j].astype(F32), tr_ref[2 * j + 1].astype(F32)
        out_tab_ref[j, :384, :128] = first
        out_tab_ref[j, 384:rows, :128] = second[: rows - 384]
        rest = second[rows - 384 :]
        out_tab_ref[j, : rows // 2, 128:192] = rest[:, :64]
        out_tab_ref[j, rows // 2 :, 128:192] = pltpu.roll(rest, 64, 1)[:, :64]

    for q in range(4):
        for s in range(2):
            for d in range(1, 4):
                row_copy(q, s, d, gsend, grecv).wait_send()
    dense_core().wait_send()
    small_core().wait_send()
    for d in range(1, n_p):
        dense_plane(d).wait_send()
        dense_gather(d).wait_send()
        small_plane(d).wait_send()
    for d in range(n_p):
        dense_last(d).wait_send()
        table_core(d).wait_send()
    for d in range(1, n_z):
        dense_z(d).wait_send()
        small_z(d).wait_send()
        table_z(d).wait_send()
    for d in range(1, 4):
        for v in range(4):
            table_along(d, v).wait_send()
    for k in range(3):
        table_replica(k).wait_send()


def whole(n):
    return [pl.BlockSpec(memory_space=pltpu.VMEM)] * n


def run_step(scale, *args):
    half = DEN_ROWS // 2
    chunk = half // 16
    blocks = (4, 2, 4, 16, 48, 128)
    dma = pltpu.SemaphoreType.DMA
    vmem = pltpu.VMEM
    return pl.pallas_call(
        functools.partial(step_kernel, scale),
        out_shape=[
            jax.ShapeDtypeStruct((2, 512, 192), F32),
            jax.ShapeDtypeStruct((2, 2048, 128), F32),
            jax.ShapeDtypeStruct((256, 768), F32),
            jax.ShapeDtypeStruct((128, 16), F32),
            jax.ShapeDtypeStruct((32, 128), F32),
            jax.ShapeDtypeStruct((16, 128), F32),
            jax.ShapeDtypeStruct((32, 192), F32),
            jax.ShapeDtypeStruct((8, 128), F32),
        ],
        in_specs=whole(9),
        out_specs=whole(8),
        scratch_shapes=[
            vmem((32, 768, 128), BF),
            vmem((2, 16, 8, 128), jnp.int32),
            vmem((2, 128, 128), jnp.int32),
            vmem(blocks, BF),
            vmem(blocks, BF),
            vmem((2048, 256), BF),
            vmem((DEN_ROWS, 128), F32),
            vmem((48, 128), F32),
            vmem((3, 2048, 128), F32),
            vmem((32, 768, 128), BF),
            vmem((64, 48, 384), F32),
            vmem((2048, 128), F32),
            vmem((128, 2048), BF),
            vmem((64, 384), F32),
            vmem((128, 128), F32),
            vmem((half, 128), BF),
            vmem((half, 128), BF),
            vmem((16, chunk, 128), BF),
            vmem((16, chunk, 128), BF),
            vmem((8, chunk, 128), BF),
            vmem((32, chunk, 128), BF),
            vmem((8, 384, 128), BF),
            vmem((8, 384, 128), BF),
            vmem((4, 384, 128), BF),
            vmem((56, 128), F32),
            vmem((56, 128), F32),
            vmem((16, 56, 128), F32),
            vmem((8, 56, 128), F32),
            dma((64,)),
            dma((32,)),
            dma((2, 16)),
            dma((4, 2, 4)),
            dma((4, 2, 4)),
            dma((4, 2, 4)),
            dma((4, 2, 4)),
            pltpu.SemaphoreType.REGULAR,
            dma,
            dma((56,)),
            dma((16,)),
            dma((8,)),
            dma((16,)),
            dma((16,)),
            dma((16,)),
            dma((16,)),
            dma((20,)),
            dma((16,)),
            dma((8,)),
            dma((8,)),
            dma((3,)),
            dma((4,)),
            dma((24,)),
            dma,
            dma((16,)),
            dma((8,)),
        ],
        compiler_params=pltpu.CompilerParams(
            vmem_limit_bytes=VMEM_LIMIT, collective_id=0, has_side_effects=True
        ),
        name="step",
    )(*args)


def pack_tables(t):
    half = t.shape[1] // 2
    rest = jnp.concatenate([t[:, :half, 128:], t[:, half:, 128:]], 2)
    return jnp.concatenate([t[:, :, :128], rest], 1)


def order_ids(feature_ids, bag_lengths, rows):
    ids = feature_ids[:, 0].transpose(1, 2, 0)
    lens = bag_lengths[:, 0].T
    slots = jnp.arange(ids.shape[1], dtype=jnp.int32)[None, :, None]
    ids = jnp.where(lens[:, None, :] > slots, ids, rows)
    ids = ids.reshape(2, 2, 4, 4, 4, 2, 4, 16).swapaxes(5, 6).reshape(2, 2, 4, 4, 4, 128)
    even = ids[0].transpose(1, 3, 0, 2, 4)
    odd = ids[1].transpose(1, 2, 0, 3, 4)
    return jnp.stack([even, odd]).reshape(2, 16, 8, 128)


def feature_order():
    at = np.arange(128)
    j, a, zh, b = at // 64, at // 16 % 4, at // 4 % 4, at % 4
    x, y = np.where(j == 0, a, b), np.where(j == 0, b, a)
    perm = np.zeros((128, 128), np.float32)
    perm[zh * 32 + x * 8 + y * 2 + j, at] = 1.0
    return perm


def pair_head(w_head, n_out):
    lin = w_head[n_out:].astype(F32).reshape(-1, 192)
    return jnp.concatenate([lin, lin[:, 128:], lin[:, :128]], 1)


def per_device(
    feature_ids, bag_lengths, click_labels, tables, projection, compress, w_in, w_out, w_head
):
    n_out = w_out.shape[1]
    total = feature_ids.shape[0] * lax.axis_size("zl") * lax.axis_size("c")
    scale = 1.0 / math.sqrt(total)
    table_grad, gwin, gwout, gproj, gcomp, ghead, glin, loss = run_step(
        scale,
        order_ids(feature_ids, bag_lengths, tables.shape[1]),
        pack_tables(tables),
        jnp.asarray(feature_order(), BF),
        jnp.concatenate([projection.T, compress], 0),
        w_in,
        w_out,
        w_head[:n_out].astype(F32)[None, :],
        pair_head(w_head, n_out),
        click_labels.astype(F32),
    )
    gwin = jnp.concatenate([gwin[0], gwin[1]], 1)
    ghead = jnp.concatenate([ghead[: n_out // 128].reshape(-1), glin.reshape(-1)])
    return (loss[0, 0] / total, gproj, gcomp, gwin, gwout, ghead, table_grad)


def solution(mesh):
    fine = Mesh(mesh.devices.reshape(4, 4, 4, 2, 2), ("zh", "x", "y", "zl", "c"))
    emb = ("zh", "x", "y")
    rep = ("zl", "c")
    placed = (
        P(None, rep, emb, None),
        P(None, rep, emb),
        P(emb, rep),
        P(emb, None, None),
        P(),
        P(),
        P(),
        P(),
        P(),
    )
    return jax.shard_map(
        per_device,
        mesh=fine,
        in_specs=placed,
        out_specs=(P(), P(), P(), P(), P(), P(), P(emb, None, None)),
        check_vma=False,
    )
```

time: 744 us -> 245 us (0.33)
  waiting for transfers between devices: 449 us -> 0 us
  blocking collectives: 160 us -> 0 us
  Pallas kernels: 72.8 us -> 214 us
  starting transfers between devices: 15.9 us -> 0 us
  between operations: 15.7 us -> 2.51 us
  local copies, waits for them, and re-layouts: 24.7 us -> 16.4 us
    psum x2 -> x0, waiting for transfers between devices: 227 us -> none  [the longest x1 227 us: per_device(): lax.psum((loss[0, 0], gw, gwin, gwout, ghead[0], ghl), ('zh', 'x', 'y', '...]
    pallas_call x3 -> x1, Pallas kernels: 72.8 us -> 214 us  [run_step(): pl.pallas_call(functools.partial(step_kernel, scale), out_shape=[jax.Shap...]
    all_to_all x2 -> x0, waiting for transfers between devices: 101 us -> none  [the longest x1 94.1 us: per_device(): x = lax.all_to_all(y, ('x', 'y'), split_axis=0, concat_axis=0, tiled=True)]
    reduce_scatter x1 -> x0, waiting for transfers between devices: 89.6 us -> none  [per_device(): lax.psum_scatter(partial, 'zh', scatter_dimension=0, tiled=True)]
    all_to_all x1 -> x0, blocking collectives: 83 us -> none  [per_device(): lax.all_to_all(g.reshape(y.shape), ('x', 'y'), split_axis=0, concat_axis=...]
    psum x1 -> x0, blocking collectives: 77.3 us -> none  [per_device(): lax.psum((loss[0, 0], gw, gwin, gwout, ghead[0], ghl), ('zh', 'x', 'y', '...]
    all_gather x1 -> x0, waiting for transfers between devices: 29.8 us -> none  [per_device(): all_tables = lax.all_gather(tables, 'zh', axis=0, tiled=True)]
    all_to_all x2 -> x0, starting transfers between devices: 15.7 us -> none  [the longest x1 9.01 us: per_device(): ids = lax.all_to_all(ids, 'zh', split_axis=0, concat_axis=0, tiled=True)]
  transfers between devices with their start and end apart: 6 -> 0, of which waited for: 5 -> 0; matrix products, arithmetic and copies ran while one was open for 2% -> 0% of each run, Pallas kernels for 0% -> 0%
where the time goes in v4:
time: 245 us; the launch traced here: 242 us
  Pallas kernels  214 us (87%)
  local copies, waits for them, and re-layouts  16.4 us (7%)
  other arithmetic  8.66 us (4%)
  between operations  2.51 us (1%)
    pallas_call x1, Pallas kernels, run_step(): pl.pallas_call(functools.partial(step_kernel, scale), out_shape=[jax.Shap...  214 us
    unnamed x11, local copies, waits for them, and re-layouts  5.83 us

profile of v4, /device:TPU:1, one launch (start us, length us, event | category | flops | bytes accessed | tf_op | source)
XLA Modules:
  0.0 242.0 jit_solution(11923134129934849346)
XLA Ops:
  0.6 0.7 convert_element_type.13
  1.3 0.7 slice_convert_fusion.1
  2.0 0.6 reshape.50.head_ref
  2.6 1.3 pad_maximum_fusion.3.wtn_ref
  3.9 0.7 slice_convert_fusion
  4.6 0.1 reshape.51
  4.7 0.7 pad_maximum_fusion.1.hpair_ref
  5.4 0.7 copy.30.label_ref
  6.1 1.0 compare_select_fusion
  7.1 0.9 fusion.1
  8.0 0.1 copy.34
  8.1 0.1 copy.35
  8.3 1.0 slice.51
  9.2 0.2 copy.33
  9.4 0.9 maximum_maximum_fusion.tab_ref
  10.3 0.8 reshape.47
  11.0 0.2 fusion
  11.3 0.3 copy.25
  11.6 0.7 squeeze.21
  12.2 0.3 copy.26
  12.6 0.7 squeeze.22
  13.2 0.7 pad_add_fusion.ids_ref
  13.9 214.4 %step.1 = (f32[2,512,192]{2,1,0:T(8,128)}, f32[2,2048,128]{2,1,0:T(8,128)}, f32[256,768]{1,0:T(8,128)}, f32[128,16]{1,0:T(8,128)}, f32[32,128]{1,0:T(8,128)}, /*...) custom-call(s32[2,16,8,128]{3,2,1,0:T(8,128)} %pad_add_fusion.ids_ref, ...), custom_call_target="tpu_custom_call" | custom-call | tf_op jit(solution)/shard_map/step/pallas_call | solution.py:769
  228.3 1.2 slice.58
  230.1 0.7 slice_bitcast_fusion.2
  230.8 1.5 copy.31
  232.3 0.8 reshape.49
  233.2 0.6 pad_maximum_fusion.2
  233.8 2.4 %copy.32 = f32[2,512,192]{1,2,0:T(8,128)} copy(f32[2,512,192]{2,1,0:T(8,128)} %get-tuple-element.36) | data formatting | bytes 1572864
  236.2 1.7 slice_bitcast_fusion.1
  237.9 0.0 copy-start.1
  237.9 0.0 copy-start
  237.9 1.5 pad_maximum_fusion
  239.4 0.0 copy-done.1
  239.4 0.6 copy.38
  240.0 0.0 copy-done
  240.0 0.9 copy.39
  (2 shorter events, 0.0 us)
Async XLA Ops:
  237.9 1.5 copy-start.1
  237.9 2.1 copy-start

commit v5 on v4

--- a/solution.py
+++ b/solution.py
@@ -35,23 +35,31 @@
 
 def step_kernel(
     scale,
-    ids_ref,
-    tab_ref,
+    raw_ref,
+    lens_ref,
+    tabt_ref,
     perm_ref,
-    wtn_ref,
-    win_ref,
-    wout_ref,
-    head_ref,
-    hpair_ref,
+    proj_ref,
+    comp_ref,
+    win_hbm,
+    wout_hbm,
+    whead_ref,
     label_ref,
     out_tab_ref,
-    gwin_ref,
-    gwout_ref,
+    gwin_hbm,
+    gwout_hbm,
     gproj_ref,
     gcomp_ref,
     ghead_ref,
-    glin_ref,
     out_loss_ref,
+    win_ref,
+    wout_ref,
+    win_sem,
+    wout_sem,
+    gwin_sem,
+    gwout_sem,
+    ids_ref,
+    hp_ref,
     tz_ref,
     idt_ref,
     col_ref,
@@ -146,6 +154,10 @@
             device_id_type=MESH,
         )
 
+    load_win = pltpu.make_async_copy(win_hbm, win_ref, win_sem)
+    load_wout = pltpu.make_async_copy(wout_hbm, wout_ref, wout_sem)
+    load_win.start()
+    load_wout.start()
     barrier = pltpu.get_barrier_semaphore()
     partners = [sibling, (zh, px, py, 1 - zl, other)]
     partners += [at_plane((p + d) % n_p) for d in range(1, n_p)]
@@ -156,6 +168,27 @@
             partners.append(((zh + dz) % 4, (px + d) % 4, py, zl, c))
     for device in partners:
         pl.semaphore_signal(barrier, inc=1, device_id=device, device_id_type=MESH)
+    eye = (
+        lax.broadcasted_iota(jnp.int32, (128, 128), 0)
+        == lax.broadcasted_iota(jnp.int32, (128, 128), 1)
+    ).astype(F32).astype(BF)
+    mine = c * 16 + zh * 4 + o
+    for j, at in ((c, mine), (other, other * 16 + zh * 4 + o_other)):
+        tz_ref[at, :rows, :] = mm(tabt_ref[j, :128, :], eye, TN).astype(BF)
+        tz_ref[at, rest_rows, :] = (
+            mm(tabt_ref[j, 128:, low], eye[:64], TN) + mm(tabt_ref[j, 128:, high], eye[64:], TN)
+        ).astype(BF)
+    for slot in range(2):
+        for j in range(2):
+            ids = jnp.where(
+                lens_ref[j : j + 1, :] > slot, raw_ref[j, slot : slot + 1, :], rows
+            )
+            for e in range(64):
+                ez, ex, ey = e // 16, e // 4 % 4, e % 4
+                to, at = (ez * 4 + ey, ex) if j == 0 else (ez * 4 + ex, ey)
+                ids_ref[j, to, slot * 4 + at : slot * 4 + at + 1, :] = ids[
+                    :, e * 128 : (e + 1) * 128
+                ]
     pl.semaphore_wait(barrier, len(partners))
 
     sends = []
@@ -168,9 +201,6 @@
     def send_table(at, device):
         send(tz_ref.at[at], tz_ref.at[at], arecv.at[at], device)
 
-    mine = c * 16 + zh * 4 + o
-    tz_ref[mine] = tab_ref[c]
-    tz_ref[other * 16 + zh * 4 + o_other] = tab_ref[other]
     near = (zh + 3 + 2 * zl) % 4
     for to, lo in ((near, 0), (near, 1), ((zh + 2) % 4, 1 - zl)):
         send_table(mine, (to, px, py, lo, c))
@@ -204,7 +234,21 @@
         send_table(at, sibling)
 
     perm = perm_ref[...]
-    wt = mm(wtn_ref[...], perm).astype(BF)
+    wt = jnp.concatenate([mm(proj_ref[...], perm), mm(comp_ref[...], perm)], 0).astype(BF)
+    n_head = wout_ref.shape[1] // 128
+    heads = whead_ref[...].astype(F32)
+    head = jnp.concatenate([heads[i : i + 1] for i in range(n_head)], 1)
+    split_ref[2, :48, :] = heads[n_head:]
+    r0, r1, r2 = [split_ref[2, pl.ds(i, 16, stride=3), :] for i in range(3)]
+    left64 = lax.broadcasted_iota(jnp.int32, (16, 128), 1) < 64
+    turn1, turn2 = pltpu.roll(r1, 64, 1), pltpu.roll(r2, 64, 1)
+    hp_ref[0, pl.ds(0, 16, stride=2), :] = r0
+    hp_ref[0, pl.ds(1, 16, stride=2), :] = jnp.where(left64, turn1, turn2)
+    hp_ref[1, pl.ds(0, 16, stride=2), :] = jnp.where(left64, r1, turn1)
+    hp_ref[1, pl.ds(1, 16, stride=2), :] = jnp.where(left64, turn2, r2)
+    hpair = jnp.concatenate([hp_ref[0], hp_ref[1], hp_ref[0]], 1)
+    load_win.wait()
+    load_wout.wait()
     for side in range(2):
         cols = slice(side * 128, (side + 1) * 128)
         split_ref[side] = win_ref[:, cols].astype(F32)
@@ -257,7 +301,13 @@
 
     def lookup(q, carry):
         def one_set(s, inner):
-            cols = col_ref[s, pl.ds(pl.multiple_of(q * 32, 32), 32), :]
+            cols = jnp.concatenate(
+                [
+                    col_ref[s, pl.ds(pl.multiple_of(h * 64 + q * tile, tile), tile), :]
+                    for h in range(2)
+                ],
+                0,
+            )
             lane = lax.broadcasted_iota(jnp.int32, (128, rows), 1)
             first = lax.broadcasted_iota(jnp.int32, (4, tile, 128), 2) < 64
             for i in range(16):
@@ -322,7 +372,7 @@
             inter = mm(stacked, x3, NT)
             inter_ref[pl.ds(p, n_k, stride=n_b), :] = inter[:n_k]
             inter_ref[pl.ds(64 + p, n_k, stride=n_b), :] = inter[n_k:]
-            ld_ref[pl.ds(p, 1), :] = jnp.sum(mixed[n_k:] * hpair_ref[...], 0, keepdims=True)
+            ld_ref[pl.ds(p, 1), :] = jnp.sum(mixed[n_k:] * hpair, 0, keepdims=True)
             return inner
 
         lax.fori_loop(0, tile, pair, 0, unroll=2)
@@ -353,12 +403,11 @@
     sigma = 1.0 / (1.0 + jnp.exp(-pre_act))
     hidden = (pre_act * sigma).astype(BF)
     factor = mm(hidden, wout_ref[...])
-    head = head_ref[...]
     lin = ld_ref[...]
     lin1 = jnp.sum(jnp.where(row_lane1, lin, 0.0), 1, keepdims=True)
     lin2 = jnp.sum(jnp.where(row_lane1, 0.0, lin), 1, keepdims=True)
     logit = jnp.sum(factor * head, 1, keepdims=True) + jnp.concatenate([lin1, lin2], 0)
-    target = label_ref[...]
+    target = jnp.broadcast_to(label_ref[...].astype(F32), (8, 128)).T[:, :1]
     terms = jnp.maximum(logit, 0.0) + jnp.log1p(jnp.exp(-jnp.abs(logit))) - target * logit
     sa_ref[48:, :] = jnp.broadcast_to(
         jnp.sum(jnp.broadcast_to(terms, (n_b, 128)), 0, keepdims=True), (8, 128)
@@ -492,9 +541,7 @@
     pl.semaphore_wait(free_sem, 6)
 
     def back_group(q, carry):
-        pl.when(q == 1)(dense_step1)
-        pl.when(q == 2)(dense_step2)
-        pl.when(q == 3)(dense_step3)
+        pl.when(q == 3)(dense_step2)
 
         def pair(j, inner):
             p = q * tile + j
@@ -515,7 +562,7 @@
             gc = mm(gi, x3)
             gc = jnp.where(lane1, gc[:n_k], gc[n_k:]).astype(BF)
             srow = slope_row(p)
-            gl = (srow * hpair_ref[...]).astype(BF)
+            gl = (srow * hpair).astype(BF)
             compact = mix_ref[p, :n_k, :]
             tail = jnp.concatenate([gc, gl], 0)
             right = jnp.concatenate(
@@ -538,6 +585,7 @@
             y_ref[q, :, :, :, part * tile : (part + 1) * tile, :] = (
                 split_ref[part].reshape(2, 4, 16, tile, 128).astype(BF)
             )
+        pl.when(q == 0)(dense_step1)
         for d in (1, 3, 2):
             for s in range(2):
                 row_copy(q, s, d, gsend, grecv).start()
@@ -571,13 +619,15 @@
                 ids = idt_ref[s, i, slot * 4 + src : slot * 4 + src + 1, :]
                 hot = hot + jnp.where(row == ids, 1.0, 0.0)
             hots.append(hot.astype(BF))
+            for k in range(8):
+                mains.append(x_ref[k % 4, s, src, i, k // 4 * tile : (k // 4 + 1) * tile, :])
             for q in range(4):
-                mains.append(x_ref[q, s, src, i, : 2 * tile, :])
                 rests.append(x_ref[q, s, src, i, 2 * tile :, :])
         turned = pltpu.roll(jnp.concatenate(rests, 0).astype(F32), 64, 1).astype(BF)
         tails = []
-        for k, rest in enumerate(rests):
-            tails += [rest, turned[k * tile : (k + 1) * tile]]
+        for src in range(4):
+            tails += rests[src * 4 : src * 4 + 4]
+            tails.append(turned[src * 64 : (src + 1) * 64])
         right = jnp.concatenate([jnp.concatenate(mains, 0), jnp.concatenate(tails, 0)], 1)
         sums = mm(jnp.concatenate(hots, 1), right)
         lane = lax.broadcasted_iota(jnp.int32, (256, 128), 1)
@@ -598,9 +648,8 @@
             along(d),
         )
 
-    def table_z(d):
-        to = (z + d) % n_z
-        return remote(te_ref.at[to], tf_ref.at[z], t3send.at[d], t3recv.at[z], at_z(to))
+    def table_z(to):
+        return remote(te_ref.at[to], tf_ref.at[z], t3send.at[to], t3recv.at[z], at_z(to))
 
     own_slot = 2 * c + zl
 
@@ -612,9 +661,10 @@
 
     for q in range(4):
         row_arrived(q, grecv)
+    dense_step3()
 
     def for_sibling(n, carry):
-        i = (n % 4) * 4 + (o_other + 1 + n // 4) % 4
+        i = (zh + 1 + n // 4) % 4 * 4 + (o_other + 1 + n % 4) % 4
         main, tail = table_grad(other, i)
         tz_ref[16 + i, :rows, :] = main.astype(BF)
         tz_ref[16 + i, rest_rows, :] = tail.astype(BF)
@@ -629,7 +679,7 @@
         small_plane(d).start()
 
     def for_chip(n, carry):
-        d, v = n // 4 + 1, n % 4
+        d, v = n % 4 + 1, (zh + 1 + n // 4) % 4
         i = v * 4 + (o + d) % 4
         main, tail = table_grad(c, i)
         arrived(tz_ref.at[i], t1recv.at[i])
@@ -643,6 +693,22 @@
         return carry
 
     lax.fori_loop(0, 16, for_chip, 0)
+
+    own = None
+    for dv in (1, 2, 3, 0):
+        v = (zh + dv) % 4
+        for k in range(1, 4):
+            at = (o + k) % 4 * 4 + v
+            arrived(xp_ref.at[16 + at], t2recv.at[at])
+        for flip in (1, 0):
+            lo = (zl + flip) % 2
+            span = pl.ds(pl.multiple_of(lo * 384, 384), 384)
+            own = xp_ref[v * 4 + o, span, :].astype(F32)
+            for k in range(1, 4):
+                own = own + xp_ref[16 + (o + k) % 4 * 4 + v, span, :].astype(F32)
+            if dv > 0 or flip > 0:
+                te_ref[v * 2 + lo] = own.astype(BF)
+                table_z(v * 2 + lo).start()
 
     for d in range(1, n_p):
         q = (p + d) % n_p
@@ -658,21 +724,6 @@
     for d in range(1, n_z):
         small_z(d).start()
 
-    for d in range(1, 4):
-        for v in range(4):
-            at = (o + d) % 4 * 4 + v
-            arrived(xp_ref.at[16 + at], t2recv.at[at])
-    own = None
-    for d in (1, 7, 2, 6, 3, 5, 4, 0):
-        to = (z + d) % n_z
-        span = pl.ds(pl.multiple_of(to % 2 * 384, 384), 384)
-        own = xp_ref[to // 2 * 4 + o, span, :].astype(F32)
-        for k in range(1, 4):
-            own = own + xp_ref[16 + (o + k) % 4 * 4 + to // 2, span, :].astype(F32)
-        if d > 0:
-            te_ref[to] = own.astype(BF)
-            table_z(d).start()
-
     for q in range(n_p):
         arrived(df_ref.at[other * n_p + q], dh_sem.at[q])
 
@@ -686,15 +737,43 @@
             at += n
         return pieces[0] if len(pieces) == 1 else jnp.concatenate(pieces, 0)
 
+    stores = []
+
+    def store(src, dst, sem):
+        copy = pltpu.make_async_copy(src, dst, sem)
+        copy.start()
+        stores.append(copy)
+
     for side in range(2):
         for k in range(n_k):
             block = final(side * 2048 + k * 128, 128)
-            gwin_ref[side, pl.ds(k, n_f, stride=n_k), :] = mm(perm, block)
-    for i in range(6):
-        gwout_ref[:, i * 128 : (i + 1) * 128] = final(AT_WOUT + i * 256, 256).astype(F32)
-    glin_ref[:, :128] = final(AT_LIN, 32).astype(F32)
-    glin_ref[:, 128:192] = final(AT_LIN + 32, 32).astype(F32)[:, :64]
-    ghead_ref[...] = final(AT_HEAD, 16).astype(F32)
+            split_ref[side, pl.ds(k, n_f, stride=n_k), :] = mm(perm, block)
+        store(
+            split_ref.at[side],
+            gwin_hbm.at[:, side * 128 : (side + 1) * 128],
+            gwin_sem.at[side],
+        )
+    for i in range(n_head):
+        span = slice(i * 256, (i + 1) * 256)
+        split_ref[2, span, :] = final(AT_WOUT + i * 256, 256).astype(F32)
+        store(
+            split_ref.at[2, span],
+            gwout_hbm.at[:, i * 128 : (i + 1) * 128],
+            gwout_sem.at[i],
+        )
+    ghead_ref[:n_head, :] = final(AT_HEAD, 16).astype(F32)[:n_head]
+    hp_ref[0] = final(AT_LIN, 32).astype(F32)
+    hp_ref[1] = final(AT_LIN + 32, 32).astype(F32)
+    even, odd = [hp_ref[0, pl.ds(i, 16, stride=2), :] for i in range(2)]
+    even_rest, odd_rest = [hp_ref[1, pl.ds(i, 16, stride=2), :] for i in range(2)]
+    turned = pltpu.roll(odd, 64, 1)
+    lin_ref = split_ref.at[2, 1536:]
+    lin_ref[pl.ds(0, 16, stride=3), :] = even
+    lin_ref[pl.ds(1, 16, stride=3), :] = jnp.where(left64, even_rest, turned)
+    lin_ref[pl.ds(2, 16, stride=3), :] = jnp.where(
+        left64, turned, pltpu.roll(odd_rest, 64, 1)
+    )
+    ghead_ref[n_head:, :] = lin_ref[:48, :]
 
     for d in range(1, n_z):
         v = (z + d) % n_z
@@ -710,7 +789,7 @@
     small = sz_ref[0]
     for v in range(1, n_z):
         small = small + sz_ref[v]
-    out_loss_ref[...] = small[48:]
+    out_loss_ref[...] = small[48:49, :1] * (scale * scale)
     natural = lax.dot_general(
         small[:48],
         perm.astype(F32),
@@ -718,19 +797,21 @@
         precision=lax.Precision.HIGHEST,
         preferred_element_type=F32,
     )
-    gproj_ref[...] = natural[:n_k].T
+    gproj_ref[...] = natural[:n_k]
     gcomp_ref[...] = natural[n_k:]
 
     for d in range(1, 4):
         k = (own_slot + d) % 4
         arrived(tr_ref.at[k], t4recv.at[k])
     for j in range(2):
-        first, second = tr_ref[2 * j].astype(F32), tr_ref[2 * j + 1].astype(F32)
-        out_tab_ref[j, :384, :128] = first
-        out_tab_ref[j, 384:rows, :128] = second[: rows - 384]
+        first, second = tr_ref[2 * j], tr_ref[2 * j + 1]
+        main = jnp.concatenate([first, second[: rows - 384]], 0)
         rest = second[rows - 384 :]
-        out_tab_ref[j, : rows // 2, 128:192] = rest[:, :64]
-        out_tab_ref[j, rows // 2 :, 128:192] = pltpu.roll(rest, 64, 1)[:, :64]
+        out_tab_ref[j, :128, :] = mm(eye, main, NT)
+        out_tab_ref[j, 128:, low] = mm(eye[:64], rest, NT)
+        out_tab_ref[j, 128:, high] = mm(eye[64:], rest, NT)
+    for copy in stores:
+        copy.wait()
 
     for q in range(4):
         for s in range(2):
@@ -748,7 +829,7 @@
     for d in range(1, n_z):
         dense_z(d).wait_send()
         small_z(d).wait_send()
-        table_z(d).wait_send()
+        table_z((z + d) % n_z).wait_send()
     for d in range(1, 4):
         for v in range(4):
             table_along(d, v).wait_send()
@@ -766,21 +847,29 @@
     blocks = (4, 2, 4, 16, 48, 128)
     dma = pltpu.SemaphoreType.DMA
     vmem = pltpu.VMEM
+    anywhere = [pl.BlockSpec(memory_space=pl.ANY)]
     return pl.pallas_call(
         functools.partial(step_kernel, scale),
         out_shape=[
-            jax.ShapeDtypeStruct((2, 512, 192), F32),
-            jax.ShapeDtypeStruct((2, 2048, 128), F32),
+            jax.ShapeDtypeStruct((2, 192, 512), F32),
+            jax.ShapeDtypeStruct((2048, 256), F32),
             jax.ShapeDtypeStruct((256, 768), F32),
-            jax.ShapeDtypeStruct((128, 16), F32),
+            jax.ShapeDtypeStruct((16, 128), F32),
             jax.ShapeDtypeStruct((32, 128), F32),
-            jax.ShapeDtypeStruct((16, 128), F32),
-            jax.ShapeDtypeStruct((32, 192), F32),
-            jax.ShapeDtypeStruct((8, 128), F32),
+            jax.ShapeDtypeStruct((54, 128), F32),
+            jax.ShapeDtypeStruct((1, 1), F32),
         ],
-        in_specs=whole(9),
-        out_specs=whole(8),
+        in_specs=whole(6) + anywhere * 2 + whole(2),
+        out_specs=whole(1) + anywhere * 2 + whole(4),
         scratch_shapes=[
+            vmem((2048, 256), BF),
+            vmem((256, 768), BF),
+            dma,
+            dma,
+            dma((2,)),
+            dma((6,)),
+            vmem((2, 16, 8, 128), jnp.int32),
+            vmem((2, 32, 128), F32),
             vmem((32, 768, 128), BF),
             vmem((2, 16, 8, 128), jnp.int32),
             vmem((2, 128, 128), jnp.int32),
@@ -843,23 +932,6 @@
     )(*args)
 
 
-def pack_tables(t):
-    half = t.shape[1] // 2
-    rest = jnp.concatenate([t[:, :half, 128:], t[:, half:, 128:]], 2)
-    return jnp.concatenate([t[:, :, :128], rest], 1)
-
-
-def order_ids(feature_ids, bag_lengths, rows):
-    ids = feature_ids[:, 0].transpose(1, 2, 0)
-    lens = bag_lengths[:, 0].T
-    slots = jnp.arange(ids.shape[1], dtype=jnp.int32)[None, :, None]
-    ids = jnp.where(lens[:, None, :] > slots, ids, rows)
-    ids = ids.reshape(2, 2, 4, 4, 4, 2, 4, 16).swapaxes(5, 6).reshape(2, 2, 4, 4, 4, 128)
-    even = ids[0].transpose(1, 3, 0, 2, 4)
-    odd = ids[1].transpose(1, 2, 0, 3, 4)
-    return jnp.stack([even, odd]).reshape(2, 16, 8, 128)
-
-
 def feature_order():
     at = np.arange(128)
     j, a, zh, b = at // 64, at // 16 % 4, at // 4 % 4, at % 4
@@ -869,32 +941,32 @@
     return perm
 
 
-def pair_head(w_head, n_out):
-    lin = w_head[n_out:].astype(F32).reshape(-1, 192)
-    return jnp.concatenate([lin, lin[:, 128:], lin[:, :128]], 1)
-
-
 def per_device(
     feature_ids, bag_lengths, click_labels, tables, projection, compress, w_in, w_out, w_head
 ):
-    n_out = w_out.shape[1]
     total = feature_ids.shape[0] * lax.axis_size("zl") * lax.axis_size("c")
-    scale = 1.0 / math.sqrt(total)
-    table_grad, gwin, gwout, gproj, gcomp, ghead, glin, loss = run_step(
-        scale,
-        order_ids(feature_ids, bag_lengths, tables.shape[1]),
-        pack_tables(tables),
+    table_grad, gwin, gwout, gproj, gcomp, ghead, loss = run_step(
+        1.0 / math.sqrt(total),
+        feature_ids[:, 0].transpose(1, 2, 0),
+        bag_lengths[:, 0].T,
+        tables.transpose(0, 2, 1),
         jnp.asarray(feature_order(), BF),
-        jnp.concatenate([projection.T, compress], 0),
+        projection.T,
+        compress,
         w_in,
         w_out,
-        w_head[:n_out].astype(F32)[None, :],
-        pair_head(w_head, n_out),
-        click_labels.astype(F32),
+        w_head.reshape(-1, 128),
+        click_labels.T,
     )
-    gwin = jnp.concatenate([gwin[0], gwin[1]], 1)
-    ghead = jnp.concatenate([ghead[: n_out // 128].reshape(-1), glin.reshape(-1)])
-    return (loss[0, 0] / total, gproj, gcomp, gwin, gwout, ghead, table_grad)
+    return (
+        loss[0, 0],
+        gproj.T,
+        gcomp,
+        gwin,
+        gwout,
+        ghead.reshape(-1),
+        table_grad.transpose(0, 2, 1),
+    )
 
 
 def solution(mesh):

time: 245 us -> 212 us (0.87)
  Pallas kernels: 214 us -> 201 us
  other arithmetic: 8.66 us -> 0 us
  local copies, waits for them, and re-layouts: 16.4 us -> 8.16 us
    pallas_call x1, Pallas kernels: 214 us -> 201 us  [run_step(): pl.pallas_call(functools.partial(step_kernel, scale), out_shape=[jax.Shap...]
    concatenate x5 -> x0, other arithmetic: 4.94 us -> none  [the longest x1 1.46 us: per_device(): gwin = jnp.concatenate([gwin[0], gwin[1]], 1)]
    slice x8 -> x0, local copies, waits for them, and re-layouts: 3.9 us -> none  [the longest x1 1.19 us: per_device(): return (loss[0, 0] / total, gproj, gcomp, gwin, gwout, ghead, table_grad)]
    squeeze x3 -> x0, local copies, waits for them, and re-layouts: 3.02 us -> none  [the longest x1 1.68 us: per_device(): gwin = jnp.concatenate([gwin[0], gwin[1]], 1)]
    unnamed x11 -> x12, local copies, waits for them, and re-layouts: 5.83 us -> 8.16 us
where the time goes in v5:
time: 212 us; the launch traced here: 211 us
  Pallas kernels  201 us (95%)
  local copies, waits for them, and re-layouts  8.16 us (4%)
  between operations  2.4 us (1%)
    pallas_call x1, Pallas kernels, run_step(): pl.pallas_call(functools.partial(step_kernel, scale), out_shape=[jax.Shap...  201 us
    unnamed x12, local copies, waits for them, and re-layouts  8.16 us

profile of v5, /device:TPU:1, one launch (start us, length us, event | category | flops | bytes accessed | tf_op | source)
XLA Modules:
  0.0 211.4 jit_solution(8582218805985365478)
XLA Ops:
  0.6 200.8 %step.1 = (f32[2,192,512]{2,1,0:T(8,128)}, f32[2048,256]{1,0:T(8,128)}, f32[256,768]{1,0:T(8,128)}, f32[16,128]{1,0:T(8,128)}, f32[32,128]{1,0:T(8,128)}, /*index=5*/f32[54,128]{1,0:T(8,128)}, f32[1,1]{1,0:T(1,128)}) custom-call(s32[2,2,8192]{2,1,0:T(2,128)} %bitcast.16, s32[2,8192]{1,0:T(2,128)} %bitcast.17, bf16[2,192,512]{2,1,0:T(8,128)(2,1)} %bitcast.15, ...), custom_call_target="tpu_custom_call" | custom-call | tf_op jit(solution)/shard_map/step/pallas_call | solution.py:851
  202.1 1.3 copy.25
  203.4 1.3 copy.26
  204.7 0.0 copy-start.1
  204.7 0.0 copy-start.2
  204.7 0.0 copy-start
  204.7 3.2 %copy.27 = f32[2048,256]{1,0:T(8,128)} copy(f32[2048,256]{1,0:T(8,128)} %get-tuple-element.31) | data formatting | bytes 4194304
  207.9 0.0 copy-done.1
  207.9 0.9 copy.28
  208.7 0.0 copy-done.2
  208.8 0.6 copy.29
  209.4 0.0 copy-done
  209.4 0.9 copy.30
Async XLA Ops:
  204.7 3.2 %copy-start.1 = (f32[256,768]{1,0:T(8,128)S(1)}, f32[256,768]{1,0:T(8,128)}, u32[]{:S(2)}) copy-start(f32[256,768]{1,0:T(8,128)} %get-tuple-element.32) | copy-start | bytes 2359300
  204.7 4.1 %copy-start.2 = (f32[54,128]{1,0:T(8,128)S(1)}, f32[54,128]{1,0:T(8,128)}, u32[]{:S(2)}) copy-start(f32[54,128]{1,0:T(8,128)} %get-tuple-element.19) | copy-start | bytes 82948
  204.7 4.7 %copy-start = (f32[2,192,512]{2,1,0:T(8,128)S(1)}, f32[2,192,512]{2,1,0:T(8,128)}, u32[]{:S(2)}) copy-start(f32[2,192,512]{2,1,0:T(8,128)} %get-tuple-element.20) | copy-start | bytes 2359300

commit v6 on v5

--- a/solution.py
+++ b/solution.py
@@ -101,6 +101,7 @@
     dp_sem,
     dz_sem,
     dg_sem,
+    dx_sem,
     dh_sem,
     t1send,
     t1recv,
@@ -132,6 +133,15 @@
 
     def at_plane(q):
         return (zh, q // 4, q % 4, zl, c)
+
+    m = o_other * 4 + o
+
+    def at_m(k):
+        a, b = k // 4, k % 4
+        return (zh, a * other + b * c, b * other + a * c, zl, c)
+
+    def cross(d):
+        return (zh, (px + d * other) % 4, (py + d * c) % 4, zl, c)
 
     def at_z(v):
         return (v // 2, px, py, v % 2, c)
@@ -435,6 +445,109 @@
         gnormed = mm(gpre, winp_ref[feats, :], NT)
         first = first + gnormed
         second = second + gnormed * inter_ref[k * n_b : (k + 1) * n_b, :]
+    def slope_row(p):
+        s1 = slope_ref[pl.ds(p, 1), :]
+        s2 = slope_ref[pl.ds(64 + p, 1), :]
+        return jnp.where(
+            row_lane1,
+            jnp.concatenate([s1, s1, s1], 1),
+            jnp.concatenate([s2, s2, s2], 1),
+        )
+
+    ghl = lax.fori_loop(
+        0,
+        64,
+        lambda p, sum: sum + slope_row(p) * mix_ref[p, n_k:, :],
+        jnp.zeros((32, 384), F32),
+        unroll=4,
+    )
+    middle = ghl[:, 128:256]
+    lane = lax.broadcasted_iota(jnp.int32, middle.shape, 1)
+    den_ref[AT_LIN : AT_LIN + 32, :] = ghl[:, :128] + ghl[:, 256:]
+    den_ref[AT_LIN + 32 : AT_LIN + 64, :] = jnp.where(
+        lane < 64, middle + pltpu.roll(middle, 64, 1), 0.0
+    )
+    den_ref[AT_GW:AT_LIN, :] = jnp.zeros((AT_LIN - AT_GW, 128), F32)
+
+    def dense_core():
+        return remote(da_ref, db_ref, dsend.at[0], core_sem, sibling)
+
+    def dense_plane(d):
+        to = (m + d) % n_p
+        return remote(
+            dc_ref.at[to], dd_ref.at[m], dsend.at[d], dp_sem.at[m], at_m(to)
+        )
+
+    def dense_z(d):
+        return remote(
+            de_ref.at[z], de_ref.at[z], dsend.at[15 + d], dz_sem.at[z], at_z((z + d) % n_z)
+        )
+
+    def dense_gather(d):
+        at = c * n_p + m
+        return remote(df_ref.at[at], df_ref.at[at], dsend.at[22 + d], dg_sem.at[o], along(d))
+
+    def four(core, a):
+        return df_ref.at[pl.ds(core * n_p + a * 4, 4)]
+
+    def dense_spread(d):
+        part = four(c, o_other)
+        return remote(part, part, dsend.at[25 + d], dx_sem.at[o_other], cross(d))
+
+    def dense_last(d):
+        a = (o_other + d) % 4
+        return remote(four(c, a), four(c, a), dsend.at[29 + d], dh_sem.at[a], sibling)
+
+    def dense_step1():
+        arrived(db_ref, core_sem)
+
+        def add(i, carry):
+            at = pl.multiple_of(i * chunk, chunk)
+            mine = den_ref[pl.ds(pl.multiple_of(c * half + i * chunk, chunk), chunk), :]
+            dc_ref[i] = (mine + db_ref[pl.ds(at, chunk), :].astype(F32)).astype(BF)
+            return carry
+
+        lax.fori_loop(0, n_p, add, 0)
+        for d in range(1, n_p):
+            dense_plane(d).start()
+
+    def dense_step2():
+        own = dc_ref[m].astype(F32)
+        for d in range(1, n_p):
+            q = (m + d) % n_p
+            arrived(dd_ref.at[q], dp_sem.at[q])
+            own = own + dd_ref[q].astype(F32)
+        de_ref[z] = own.astype(BF)
+        for d in range(1, n_z):
+            dense_z(d).start()
+
+    def dense_step3():
+        for d in range(1, n_z):
+            v = (z + d) % n_z
+            arrived(de_ref.at[v], dz_sem.at[v])
+        own = de_ref[0].astype(F32)
+        for v in range(1, n_z):
+            own = own + de_ref[v].astype(F32)
+        df_ref[c * n_p + m] = own.astype(BF)
+        for d in range(1, 4):
+            dense_gather(d).start()
+
+    def dense_step4():
+        for d in range(1, 4):
+            k = (o + d) % 4
+            arrived(df_ref.at[c * n_p + o_other * 4 + k], dg_sem.at[k])
+        for d in range(1, 4):
+            dense_spread(d).start()
+        dense_last(0).start()
+
+    def dense_step5():
+        for d in range(1, 4):
+            a = (o_other + d) % 4
+            arrived(four(c, a), dx_sem.at[a])
+            dense_last(d).start()
+
+    da_ref[...] = den_ref[pl.ds(pl.multiple_of(other * half, half), half), :].astype(BF)
+    dense_core().start()
     mean1 = jnp.sum(first, 1, keepdims=True) / width
     mean2 = jnp.sum(second, 1, keepdims=True) / width
     for k in range(n_k):
@@ -443,105 +556,17 @@
         gnormed = mm(gpre, winp_ref[feats, :], NT)
         inter_ref[span, :] = rstd * (gnormed - mean1 - inter_ref[span, :] * mean2)
 
-    def slope_row(p):
-        s1 = slope_ref[pl.ds(p, 1), :]
-        s2 = slope_ref[pl.ds(64 + p, 1), :]
-        return jnp.where(
-            row_lane1,
-            jnp.concatenate([s1, s1, s1], 1),
-            jnp.concatenate([s2, s2, s2], 1),
-        )
-
-    ghl = lax.fori_loop(
-        0,
-        64,
-        lambda p, sum: sum + slope_row(p) * mix_ref[p, n_k:, :],
-        jnp.zeros((32, 384), F32),
-        unroll=4,
-    )
-    second = ghl[:, 128:256]
-    lane = lax.broadcasted_iota(jnp.int32, second.shape, 1)
-    den_ref[AT_LIN : AT_LIN + 32, :] = ghl[:, :128] + ghl[:, 256:]
-    den_ref[AT_LIN + 32 : AT_LIN + 64, :] = jnp.where(
-        lane < 64, second + pltpu.roll(second, 64, 1), 0.0
-    )
-    den_ref[AT_GW:AT_LIN, :] = jnp.zeros((AT_LIN - AT_GW, 128), F32)
-    gw_ref[...] = jnp.zeros_like(gw_ref)
-
-    def dense_core():
-        return remote(da_ref, db_ref, dsend.at[0], core_sem, sibling)
-
-    def dense_plane(d):
-        to = (p + d) % n_p
-        return remote(
-            dc_ref.at[to], dd_ref.at[p], dsend.at[d], dp_sem.at[p], at_plane(to)
-        )
-
-    def dense_z(d):
-        return remote(
-            de_ref.at[z], de_ref.at[z], dsend.at[15 + d], dz_sem.at[z], at_z((z + d) % n_z)
-        )
-
-    def dense_gather(d):
-        at = c * n_p + p
-        return remote(
-            df_ref.at[at],
-            df_ref.at[at],
-            dsend.at[22 + d],
-            dg_sem.at[p],
-            at_plane((p + d) % n_p),
-        )
-
-    def dense_last(d):
-        q = (p + d) % n_p
-        at = c * n_p + q
-        return remote(df_ref.at[at], df_ref.at[at], dsend.at[38 + d], dh_sem.at[q], sibling)
-
-    def dense_step1():
-        arrived(db_ref, core_sem)
-
-        def add(i, carry):
-            at = pl.multiple_of(i * chunk, chunk)
-            mine = den_ref[pl.ds(pl.multiple_of(c * half + i * chunk, chunk), chunk), :]
-            dc_ref[i] = (mine + db_ref[pl.ds(at, chunk), :].astype(F32)).astype(BF)
-            return carry
-
-        lax.fori_loop(0, n_p, add, 0)
-        for d in range(1, n_p):
-            dense_plane(d).start()
-
-    def dense_step2():
-        own = dc_ref[p].astype(F32)
-        for d in range(1, n_p):
-            q = (p + d) % n_p
-            arrived(dd_ref.at[q], dp_sem.at[q])
-            own = own + dd_ref[q].astype(F32)
-        de_ref[z] = own.astype(BF)
-        for d in range(1, n_z):
-            dense_z(d).start()
-
-    def dense_step3():
-        for d in range(1, n_z):
-            v = (z + d) % n_z
-            arrived(de_ref.at[v], dz_sem.at[v])
-        own = de_ref[0].astype(F32)
-        for v in range(1, n_z):
-            own = own + de_ref[v].astype(F32)
-        df_ref[c * n_p + p] = own.astype(BF)
-        for d in range(1, n_p):
-            dense_gather(d).start()
-        dense_last(0).start()
-
-    da_ref[...] = den_ref[pl.ds(pl.multiple_of(other * half, half), half), :].astype(BF)
-    dense_core().start()
     for q in range(4):
         for s in range(2):
             for d in range(1, 4):
                 row_copy(q, s, d, ysend, xrecv).wait_send()
     pl.semaphore_wait(free_sem, 6)
+    gw_ref[...] = jnp.zeros_like(gw_ref)
+    dense_step1()
 
     def back_group(q, carry):
-        pl.when(q == 3)(dense_step2)
+        pl.when(q == 2)(dense_step2)
+        pl.when(q == 3)(dense_step3)
 
         def pair(j, inner):
             p = q * tile + j
@@ -585,7 +610,6 @@
             y_ref[q, :, :, :, part * tile : (part + 1) * tile, :] = (
                 split_ref[part].reshape(2, 4, 16, tile, 128).astype(BF)
             )
-        pl.when(q == 0)(dense_step1)
         for d in (1, 3, 2):
             for s in range(2):
                 row_copy(q, s, d, gsend, grecv).start()
@@ -597,10 +621,30 @@
     def small_core():
         return remote(sa_ref, sb_ref, ssend.at[0], sc_sem, sibling)
 
-    def small_plane(d):
+    def small_row(s, d):
+        here = py if s else px
         return remote(
-            sp_ref.at[p], sp_ref.at[p], ssend.at[d], sp_sem.at[p], at_plane((p + d) % n_p)
-        )
+            sp_ref.at[s, here],
+            sp_ref.at[s, here],
+            ssend.at[s * 4 + d],
+            sp_sem.at[s, here],
+            in_row(s, d)[1],
+        )
+
+    def small_start(s):
+        if s == 0:
+            arrived(sb_ref, sc_sem)
+            sp_ref[0, px] = sa_ref[...] + sb_ref[...]
+        else:
+            sp_ref[1, py] = small_sum(0)
+        for d in range(1, 4):
+            small_row(s, d).start()
+
+    def small_sum(s):
+        for d in range(1, 4):
+            src = in_row(s, d)[0]
+            arrived(sp_ref.at[s, src], sp_sem.at[s, src])
+        return sp_ref[s, 0] + sp_ref[s, 1] + sp_ref[s, 2] + sp_ref[s, 3]
 
     def small_z(d):
         return remote(
@@ -609,6 +653,7 @@
 
     sa_ref[:48, :] = gw_ref[...]
     small_core().start()
+    dense_step4()
 
     def table_grad(s, i):
         hots, mains, rests = [], [], []
@@ -661,7 +706,6 @@
 
     for q in range(4):
         row_arrived(q, grecv)
-    dense_step3()
 
     def for_sibling(n, carry):
         i = (zh + 1 + n // 4) % 4 * 4 + (o_other + 1 + n % 4) % 4
@@ -671,13 +715,6 @@
         table_core(i).start()
         return carry
 
-    lax.fori_loop(0, 16, for_sibling, 0)
-
-    arrived(sb_ref, sc_sem)
-    sp_ref[p] = sa_ref[...] + sb_ref[...]
-    for d in range(1, n_p):
-        small_plane(d).start()
-
     def for_chip(n, carry):
         d, v = n % 4 + 1, (zh + 1 + n // 4) % 4
         i = v * 4 + (o + d) % 4
@@ -692,7 +729,25 @@
 
         return carry
 
-    lax.fori_loop(0, 16, for_chip, 0)
+    def by_owner(t, carry):
+        pl.when(t == 1)(functools.partial(small_start, 0))
+        pl.when(t == 3)(functools.partial(small_start, 1))
+
+        @pl.when(t < 4)
+        def _():
+            lax.fori_loop(t * 4, t * 4 + 4, for_sibling, 0)
+
+        @pl.when(t > 0)
+        def _():
+            lax.fori_loop(t * 4 - 4, t * 4, for_chip, 0)
+
+        return carry
+
+    lax.fori_loop(0, 5, by_owner, 0)
+    dense_step5()
+    sz_ref[z] = small_sum(1)
+    for d in range(1, n_z):
+        small_z(d).start()
 
     own = None
     for dv in (1, 2, 3, 0):
@@ -710,22 +765,8 @@
                 te_ref[v * 2 + lo] = own.astype(BF)
                 table_z(v * 2 + lo).start()
 
-    for d in range(1, n_p):
-        q = (p + d) % n_p
-        arrived(df_ref.at[c * n_p + q], dg_sem.at[q])
-        dense_last(d).start()
-    for d in range(1, n_p):
-        q = (p + d) % n_p
-        arrived(sp_ref.at[q], sp_sem.at[q])
-    small = sp_ref[0]
-    for q in range(1, n_p):
-        small = small + sp_ref[q]
-    sz_ref[z] = small
-    for d in range(1, n_z):
-        small_z(d).start()
-
-    for q in range(n_p):
-        arrived(df_ref.at[other * n_p + q], dh_sem.at[q])
+    for a in range(4):
+        arrived(four(other, a), dh_sem.at[a])
 
     def final(first, count):
         pieces = []
@@ -821,11 +862,15 @@
     small_core().wait_send()
     for d in range(1, n_p):
         dense_plane(d).wait_send()
+    for d in range(n_p):
+        table_core(d).wait_send()
+    for d in range(4):
+        dense_last(d).wait_send()
+    for d in range(1, 4):
         dense_gather(d).wait_send()
-        small_plane(d).wait_send()
-    for d in range(n_p):
-        dense_last(d).wait_send()
-        table_core(d).wait_send()
+        dense_spread(d).wait_send()
+        small_row(0, d).wait_send()
+        small_row(1, d).wait_send()
     for d in range(1, n_z):
         dense_z(d).wait_send()
         small_z(d).wait_send()
@@ -896,7 +941,7 @@
             vmem((4, 384, 128), BF),
             vmem((56, 128), F32),
             vmem((56, 128), F32),
-            vmem((16, 56, 128), F32),
+            vmem((2, 4, 56, 128), F32),
             vmem((8, 56, 128), F32),
             dma((64,)),
             dma((32,)),
@@ -907,11 +952,12 @@
             dma((4, 2, 4)),
             pltpu.SemaphoreType.REGULAR,
             dma,
-            dma((56,)),
+            dma((36,)),
             dma((16,)),
             dma((8,)),
-            dma((16,)),
-            dma((16,)),
+            dma((4,)),
+            dma((4,)),
+            dma((4,)),
             dma((16,)),
             dma((16,)),
             dma((20,)),
@@ -922,7 +968,7 @@
             dma((4,)),
             dma((24,)),
             dma,
-            dma((16,)),
+            dma((2, 4)),
             dma((8,)),
         ],
         compiler_params=pltpu.CompilerParams(
@@ -941,11 +987,28 @@
     return perm
 
 
+def finish_kernel(*refs):
+    n = len(refs) // 2
+    for src, dst in zip(refs[:n], refs[n:]):
+        dst[...] = src[...]
+
+
+def finish(*args):
+    return pl.pallas_call(
+        finish_kernel,
+        out_shape=[jax.ShapeDtypeStruct(a.shape, a.dtype) for a in args],
+        in_specs=whole(len(args)),
+        out_specs=whole(len(args)),
+        compiler_params=pltpu.CompilerParams(vmem_limit_bytes=VMEM_LIMIT),
+        name="finish",
+    )(*args)
+
+
 def per_device(
     feature_ids, bag_lengths, click_labels, tables, projection, compress, w_in, w_out, w_head
 ):
     total = feature_ids.shape[0] * lax.axis_size("zl") * lax.axis_size("c")
-    table_grad, gwin, gwout, gproj, gcomp, ghead, loss = run_step(
+    results = run_step(
         1.0 / math.sqrt(total),
         feature_ids[:, 0].transpose(1, 2, 0),
         bag_lengths[:, 0].T,
@@ -958,6 +1021,7 @@
         w_head.reshape(-1, 128),
         click_labels.T,
     )
+    table_grad, gwin, gwout, gproj, gcomp, ghead, loss = finish(*results)
     return (
         loss[0, 0],
         gproj.T,

time: 212 us -> 195 us (0.920)
  local copies, waits for them, and re-layouts: 8.16 us -> 0 us
  Pallas kernels: 201 us -> 194 us
    pallas_call x1, Pallas kernels: 201 us -> 189 us  [run_step(): pl.pallas_call(functools.partial(step_kernel, scale), out_shape=[jax.Shap...]
    unnamed x12 -> x0, local copies, waits for them, and re-layouts: 8.16 us -> none
    pallas_call x0 -> x1, Pallas kernels: none -> 4.55 us  [finish(): pl.pallas_call(finish_kernel, out_shape=[jax.ShapeDtypeStruct(a.shape, a....]
where the time goes in v6:
time: 195 us; the launch traced here: 194 us
  Pallas kernels  194 us (99%)
    pallas_call x1, Pallas kernels, run_step(): pl.pallas_call(functools.partial(step_kernel, scale), out_shape=[jax.Shap...  189 us
    pallas_call x1, Pallas kernels, finish(): pl.pallas_call(finish_kernel, out_shape=[jax.ShapeDtypeStruct(a.shape, a....  4.55 us

profile of v6, /device:TPU:1, one launch (start us, length us, event | category | flops | bytes accessed | tf_op | source)
XLA Modules:
  0.0 194.5 jit_solution(16355356646521505029)
XLA Ops:
  0.6 189.3 %step.1 = (f32[2,192,512]{2,1,0:T(8,128)}, f32[2048,256]{1,0:T(8,128)}, f32[256,768]{1,0:T(8,128)}, f32[16,128]{1,0:T(8,128)}, f32[32,128]{1,0:T(8,128)}, /*index=5*/f32[54,128]{1,0:T(8,128)}, f32[1,1]{1,0:T(1,128)}) custom-call(s32[2,2,8192]{2,1,0:T(2,128)} %bitcast.15, s32[2,8192]{1,0:T(2,128)} %bitcast.16, bf16[2,192,512]{2,1,0:T(8,128)(2,1)} %bitcast.14, ...), custom_call_target="tpu_custom_call" | custom-call | tf_op jit(solution)/shard_map/step/pallas_call | solution.py:896
  189.9 4.5 %finish.1 = (f32[2,192,512]{2,1,0:T(8,128)}, f32[2048,256]{1,0:T(8,128)}, f32[256,768]{1,0:T(8,128)}, f32[16,128]{1,0:T(8,128)}, f32[32,128]{1,0:T(8,128)}, /*index=5*/f32[54,128]{1,0:T(8,128)}, f32[1,1]{1,0:T(1,128)}) custom-call(f32[2,192,512]{2,1,0:T(8,128)} %get-tuple-element.21.refs_0_, f32[2048,256]{1,0:T(8,128)} %get-tuple-element.22.refs_1_, ...), custom_call_target="tpu_custom_call" | custom-call | tf_op jit(solution)/shard_map/finish/pallas_call | solution.py:997

commit v7 on v6

--- a/solution.py
+++ b/solution.py
@@ -59,6 +59,8 @@
     gwin_sem,
     gwout_sem,
     ids_ref,
+    mid_ref,
+    msem,
     hp_ref,
     tz_ref,
     idt_ref,
@@ -172,10 +174,6 @@
     partners = [sibling, (zh, px, py, 1 - zl, other)]
     partners += [at_plane((p + d) % n_p) for d in range(1, n_p)]
     partners += [at_z((z + d) % n_z) for d in range(1, n_z)]
-    for dz in range(1, 4):
-        for d in range(1, 4):
-            partners.append(((zh + dz) % 4, px, (py + d) % 4, zl, c))
-            partners.append(((zh + dz) % 4, (px + d) % 4, py, zl, c))
     for device in partners:
         pl.semaphore_signal(barrier, inc=1, device_id=device, device_id_type=MESH)
     eye = (
@@ -196,7 +194,7 @@
             for e in range(64):
                 ez, ex, ey = e // 16, e // 4 % 4, e % 4
                 to, at = (ez * 4 + ey, ex) if j == 0 else (ez * 4 + ex, ey)
-                ids_ref[j, to, slot * 4 + at : slot * 4 + at + 1, :] = ids[
+                ids_ref[j, to // 4, to % 4, slot * 4 + at : slot * 4 + at + 1, :] = ids[
                     :, e * 128 : (e + 1) * 128
                 ]
     pl.semaphore_wait(barrier, len(partners))
@@ -216,32 +214,30 @@
         send_table(mine, (to, px, py, lo, c))
     for d in range(1, 4):
         send_table(mine, along(d))
-    for dz in range(4):
-        for d in range(4):
-            if dz == 0 and d == 0:
-                continue
-            to = (zh + dz) % 4
-            ty, tx = (py + d) % 4, (px + d) % 4
+    for dz in range(1, 4):
+        to = (zh + dz) % 4
+        for s in range(2):
             send(
-                ids_ref.at[0, to * 4 + ty],
-                idt_ref.at[0, zh * 4 + py],
-                irecv.at[0, zh * 4 + py],
-                (to, px, ty, zl, c),
+                ids_ref.at[s, to], mid_ref.at[s, :, zh], msem.at[s, zh], (to, px, py, zl, c)
             )
-            send(
-                ids_ref.at[1, to * 4 + tx],
-                idt_ref.at[1, zh * 4 + px],
-                irecv.at[1, zh * 4 + px],
-                (to, tx, py, zl, c),
-            )
-    idt_ref[0, zh * 4 + py] = ids_ref[0, zh * 4 + py]
-    idt_ref[1, zh * 4 + px] = ids_ref[1, zh * 4 + px]
+    for s in range(2):
+        mid_ref[s, :, zh] = ids_ref[s, zh]
     for dz in (1, 3, 2):
         at = c * 16 + (zh + dz) % 4 * 4 + o
         arrived(tz_ref.at[at], arecv.at[at])
         for d in range(1, 4):
             send_table(at, along(d))
         send_table(at, sibling)
+
+    for s, own in ((0, py), (1, px)):
+        for dz in range(1, 4):
+            v = (zh + dz) % 4
+            arrived(mid_ref.at[s, :, v], msem.at[s, v])
+        for d in range(1, 4):
+            to = (own + d) % 4
+            device = (zh, px, to, zl, c) if s == 0 else (zh, to, py, zl, c)
+            send(mid_ref.at[s, to], idt_ref.at[s, :, own], irecv.at[s, own], device)
+        idt_ref[s, :, own] = mid_ref[s, own]
 
     perm = perm_ref[...]
     wt = jnp.concatenate([mm(proj_ref[...], perm), mm(comp_ref[...], perm)], 0).astype(BF)
@@ -271,14 +267,10 @@
             at = c * 16 + (zh + dz) % 4 * 4 + (o + d) % 4
             arrived(tz_ref.at[at], arecv.at[at])
             send_table(at, sibling)
-    for dz in range(4):
-        for d in range(4):
-            if dz == 0 and d == 0:
-                continue
-            v = (zh + dz) % 4 * 4
-            for s, own in ((0, py), (1, px)):
-                at = v + (own + d) % 4
-                arrived(idt_ref.at[s, at], irecv.at[s, at])
+    for s, own in ((0, py), (1, px)):
+        for d in range(1, 4):
+            src = (own + d) % 4
+            arrived(idt_ref.at[s, :, src], irecv.at[s, src])
     for s in range(2):
         col_ref[s] = idt_ref[s].reshape(128, 128).T
     for dz in (0, 1, 3, 2):
@@ -661,7 +653,7 @@
         for src in range(4):
             hot = jnp.zeros((rows, 128), F32)
             for slot in range(2):
-                ids = idt_ref[s, i, slot * 4 + src : slot * 4 + src + 1, :]
+                ids = idt_ref[s, i // 4, i % 4, slot * 4 + src : slot * 4 + src + 1, :]
                 hot = hot + jnp.where(row == ids, 1.0, 0.0)
             hots.append(hot.astype(BF))
             for k in range(8):
@@ -913,10 +905,12 @@
             dma,
             dma((2,)),
             dma((6,)),
-            vmem((2, 16, 8, 128), jnp.int32),
+            vmem((2, 4, 4, 8, 128), jnp.int32),
+            vmem((2, 4, 4, 8, 128), jnp.int32),
+            dma((2, 4)),
             vmem((2, 32, 128), F32),
             vmem((32, 768, 128), BF),
-            vmem((2, 16, 8, 128), jnp.int32),
+            vmem((2, 4, 4, 8, 128), jnp.int32),
             vmem((2, 128, 128), jnp.int32),
             vmem(blocks, BF),
             vmem(blocks, BF),
@@ -945,7 +939,7 @@
             vmem((8, 56, 128), F32),
             dma((64,)),
             dma((32,)),
-            dma((2, 16)),
+            dma((2, 4)),
             dma((4, 2, 4)),
             dma((4, 2, 4)),
             dma((4, 2, 4)),

time: 195 us -> 195 us (level)
  no operation moved by 1% of the time
where the time goes in v7:
time: 195 us; the launch traced here: 194 us
  Pallas kernels  193 us (99%)
    pallas_call x1, Pallas kernels, run_step(): pl.pallas_call(functools.partial(step_kernel, scale), out_shape=[jax.Shap...  189 us
    pallas_call x1, Pallas kernels, finish(): pl.pallas_call(finish_kernel, out_shape=[jax.ShapeDtypeStruct(a.shape, a....  4.55 us

profile of v7, /device:TPU:1, one launch (start us, length us, event | category | flops | bytes accessed | tf_op | source)
XLA Modules:
  0.0 193.9 jit_solution(6567920086962317195)
XLA Ops:
  0.6 188.7 %step.1 = (f32[2,192,512]{2,1,0:T(8,128)}, f32[2048,256]{1,0:T(8,128)}, f32[256,768]{1,0:T(8,128)}, f32[16,128]{1,0:T(8,128)}, f32[32,128]{1,0:T(8,128)}, /*index=5*/f32[54,128]{1,0:T(8,128)}, f32[1,1]{1,0:T(1,128)}) custom-call(s32[2,2,8192]{2,1,0:T(2,128)} %bitcast.15, s32[2,8192]{1,0:T(2,128)} %bitcast.16, bf16[2,192,512]{2,1,0:T(8,128)(2,1)} %bitcast.14, ...), custom_call_target="tpu_custom_call" | custom-call | tf_op jit(solution)/shard_map/step/pallas_call | solution.py:888
  189.3 4.5 %finish.1 = (f32[2,192,512]{2,1,0:T(8,128)}, f32[2048,256]{1,0:T(8,128)}, f32[256,768]{1,0:T(8,128)}, f32[16,128]{1,0:T(8,128)}, f32[32,128]{1,0:T(8,128)}, /*index=5*/f32[54,128]{1,0:T(8,128)}, f32[1,1]{1,0:T(1,128)}) custom-call(f32[2,192,512]{2,1,0:T(8,128)} %get-tuple-element.21.refs_0_, f32[2048,256]{1,0:T(8,128)} %get-tuple-element.22.refs_1_, ...), custom_call_target="tpu_custom_call" | custom-call | tf_op jit(solution)/shard_map/finish/pallas_call | solution.py:991
